TPU v7x, 32 devices: a whole 2x2x4 slice. The times are simulated.
32 devices in a mesh: rep: 2 (over x), grp: 4 (over y, core), exp: 4 (over z).
Axes of the slice: x: 2, y: 2, z: 4, core: 2. Of those that a mesh axis runs over, the one named last changes fastest.
Arguments:
- tokens: bfloat16 [512, 7168], P(('rep', 'grp')), parts along dimension 0, may hold values from -6 to 6
- group_ids: int32 [512, 2], P(('rep', 'grp')), parts along dimension 0, may hold values from 0 to 3, all different within a row; in each aligned block of 64 rows (0 to 63, 64 to 127, ...) at most 48 rows name the same one
- gates: bfloat16 [512, 4], P(('rep', 'grp')), parts along dimension 0, may hold values from 0.19921875 to 1
- w_in: bfloat16 [8, 7168, 2, 1024], P('grp', None, None, 'exp'), may hold values from -0.0625 to 0.0625
- w_down: bfloat16 [8, 1024, 7168], P('grp', 'exp'), may hold values from -0.1875 to 0.1875
Outputs:
- mixed: bfloat16 [512, 7168], P(('rep', 'grp', 'exp')), parts along dimension 0
There are 2 independent parts, one for each index of `rep`. A program takes and returns all parts, laid end to end along the dimension named above; an argument that names none is the same for every part. Nothing has to cross between parts.
Inputs may be any that keep to these rules, and one draw needn't show every extreme that they name: `group_ids`: each token names 2 different groups. Among the 64 tokens of one index of grp (aligned blocks of rows) no group is named by more than 48 tokens, a bound that some block reaches.
All inputs are finite; a program needn't handle non-finite values.
Results may differ from a plain program's by a relative error of at most 0.012.
Values may be sent and summed in bfloat16 or wider, within the bound.
No kernel may reach another device: no remote copies, remote signals or barrier semaphores. Data moves between devices by JAX's collectives and lax.ppermute only.
A program may use at most 128 MiB of HBM per device.

v0:
```python
import jax
import jax.numpy as jnp
from jax import lax
from jax.sharding import PartitionSpec as P


def build_tables(group_ids, gates, group_count, capacity):
    tok_rows = group_ids.shape[0]
    top_groups = group_ids.shape[1]
    groups = jnp.arange(group_count, dtype=jnp.int32)
    matches = group_ids[:, :, None] == groups[None, None, :]
    chosen = jnp.sum(matches.astype(jnp.int32), axis=1)
    position = jnp.cumsum(chosen, axis=0) - 1
    slots = jnp.arange(capacity, dtype=jnp.int32)
    placed = (chosen[:, :, None] == 1) & (position[:, :, None] == slots[None, None, :])
    table = placed.transpose(1, 2, 0).astype(jnp.bfloat16)
    gate_pairs = gates.astype(jnp.float32).reshape(tok_rows, top_groups, 2)
    choice_gate = jnp.einsum("tkg,tkj->tgj", matches.astype(jnp.float32), gate_pairs).astype(
        jnp.bfloat16
    )
    return (table, choice_gate, position)


def run_experts(rows, row_gates, w_in, w_down):
    feature_width = rows.shape[1]
    hidden_dev = w_in.shape[3]
    total = jnp.zeros(rows.shape, jnp.float32)
    for member in range(2):
        gate_up = jnp.dot(
            rows,
            w_in[member].reshape(feature_width, 2 * hidden_dev),
            preferred_element_type=jnp.float32,
        )
        hidden_act = (jax.nn.silu(gate_up[:, :hidden_dev]) * gate_up[:, hidden_dev:]).astype(
            jnp.bfloat16
        )
        output_rows = jnp.dot(hidden_act, w_down[member], preferred_element_type=jnp.float32)
        total = total + row_gates[:, member : member + 1].astype(jnp.float32) * output_rows
    return total


def local(tokens, group_ids, gates, w_in, w_down):
    group_count = lax.axis_size("grp")
    tok_rows = tokens.shape[0]
    feature_width = tokens.shape[1]
    top_groups = group_ids.shape[1]
    capacity = min(tok_rows, max(2, 3 * tok_rows * top_groups // (2 * group_count)))
    table, choice_gate, position = build_tables(group_ids, gates, group_count, capacity)
    packed = jnp.einsum("gct,td->gcd", table, tokens, preferred_element_type=jnp.float32).astype(
        jnp.bfloat16
    )
    packed_gates = jnp.einsum(
        "gct,tgj->gcj", table, choice_gate, preferred_element_type=jnp.float32
    ).astype(jnp.bfloat16)
    arrived, arrived_gates = (
        lax.all_to_all(packed, "grp", split_axis=0, concat_axis=0, tiled=True),
        lax.all_to_all(packed_gates, "grp", split_axis=0, concat_axis=0, tiled=True),
    )
    partial_value = run_experts(
        arrived.reshape(-1, feature_width), arrived_gates.reshape(-1, 2), w_in, w_down
    )
    parts = partial_value.astype(jnp.bfloat16).reshape(group_count, capacity, feature_width)
    coming_back = lax.all_to_all(parts, "grp", split_axis=0, concat_axis=0, tiled=True)
    local_sum = jnp.einsum("gct,gcd->td", table, coming_back, preferred_element_type=jnp.float32)
    mixed = lax.psum_scatter(local_sum.astype(jnp.bfloat16), "exp", scatter_dimension=0, tiled=True)
    return mixed


def solution(mesh):
    in_specs = (
        P(("rep", "grp"), None),
        P(("rep", "grp"), None),
        P(("rep", "grp"), None),
        P("grp", None, None, "exp"),
        P("grp", "exp", None),
    )
    out_specs = P(("rep", "grp", "exp"), None)
    return jax.shard_map(local, mesh=mesh, in_specs=in_specs, out_specs=out_specs, check_vma=False)
```

profile of v0, /device:TPU:0, one launch (start us, length us, event | category | flops | bytes accessed | tf_op | source)
XLA Modules:
  0.0 136.8 jit_solution(7142255675647409442)
XLA Ops:
  6.5 0.0 copy-start
  6.5 0.8 convert_reduce_fusion
  7.3 0.1 copy.13
  7.4 0.7 iota_compare_fusion.1
  8.1 0.1 reduce_window_sum.11
  8.2 0.1 copy.14
  8.3 0.1 copy.15
  8.4 0.8 copy.16
  9.2 0.2 convolution_convert_fusion.1
  9.4 0.1 copy.17
  9.5 0.7 convolution_convert_fusion.2
  10.3 4.2 %all-to-all-start = ((bf16[4,48,2]{1,2,0:T(2,128)(2,1)}), bf16[4,48,2]{1,2,0:T(2,128)(2,1)S(1)}, u32[]{:S(2)}, u32[]{:S(2)}) async-start(bf16[4,48,2]{1,2,0:T(2,128)(2,1)} %convolution_convert_fusion.2), calls=%async_computation | async-start | bytes 4096 | tf_op jit(solution)/shard_map/all_to_all | solution.py:57
  14.5 0.0 copy-done
  14.5 2.4 %convolution_convert_fusion = bf16[4,48,7168]{2,1,0:T(8,128)(2,1)} fusion(bf16[64,7168]{1,0:T(8,128)(2,1)S(1)} %copy-done, s32[4,64]{1,0:T(4,128)S(1)} %copy.14, pred[4,64]{1,0:T(4,128)(4,1)S(1)} %compare_bitcast_fusion), kind=kOutput, calls=%fused_computation.4 | convolution fusion | flops 177561600 | bytes 3671296 | tf_op jit(solution)/shard_map/gct,td->gcd/dot_general | solution.py:49
  16.9 1.3 all-to-all-done
  18.2 4.6 %all-to-all-start.1 = ((bf16[4,48,7168]{2,1,0:T(8,128)(2,1)}), bf16[4,48,7168]{2,1,0:T(8,128)(2,1)}, u32[]{:S(2)}, u32[]{:S(2)}) async-start(bf16[4,48,7168]{2,1,0:T(8,128)(2,1)} %convolution_convert_fusion), calls=%async_computation.1 | async-start | bytes 5505024 | tf_op jit(solution)/shard_map/all_to_all | solution.py:56
  22.8 0.0 reduce-scatter.2.cloned.1.call-start
  22.8 12.4 %fusion.26 = (bf16[1,7168,2,256]{3,2,1,0:T(2,128)(2,1)S(1)}, bf16[1,7168,2,256]{3,2,1,0:T(2,128)(2,1)}) fusion(bf16[2,7168,2,256]{3,2,1,0:T(2,128)(2,1)} %param.8), kind=kLoop, calls=%fused_computation.36 | loop fusion | bytes 29360128 | tf_op jit(solution)/shard_map/slice | solution.py:31
  35.2 7.3 %copy.19 = bf16[896,8,2,256]{3,1,2,0:T(8,128)(2,1)} copy(bf16[896,8,2,256]{3,2,1,0:T(2,128)(2,1)} %bitcast.39) | data formatting | bytes 14680064
  42.5 4.2 %copy.20 = bf16[896,8,2,256]{3,1,2,0:T(8,128)(2,1)} copy(bf16[896,8,2,256]{3,2,1,0:T(2,128)(2,1)S(1)} %bitcast.38) | data formatting | bytes 14680064
  46.8 0.1 reshape.25
  46.9 8.7 %all-to-all-done.1 = bf16[4,48,7168]{2,1,0:T(8,128)(2,1)} async-done(((bf16[4,48,7168]{2,1,0:T(8,128)(2,1)}), bf16[4,48,7168]{2,1,0:T(8,128)(2,1)}, u32[]{:S(2)}, u32[]{:S(2)}) %all-to-all-start.1) | async-done | bytes 2752544 | tf_op jit(solution)/shard_map/all_to_all | solution.py:56
  55.5 0.0 copy-start.2
  55.5 0.0 slice-start
  55.5 5.6 %fusion.27 = f32[192,512]{1,0:T(8,128)S(1)} fusion(bf16[192,7168]{1,0:T(8,128)(2,1)} %bitcast.5, bf16[7168,512]{1,0:T(8,128)(2,1)} %bitcast.41), kind=kOutput, calls=%fused_computation.37 | convolution fusion | flops 1409286144 | bytes 10485760 | tf_op jit(solution)/shard_map/dot_general | solution.py:29
  61.2 0.3 copy-done.2
  61.5 0.0 slice-start.1
  61.5 3.6 %fusion.28 = f32[192,512]{1,0:T(8,128)S(1)} fusion(bf16[192,7168]{1,0:T(8,128)(2,1)} %bitcast.5, bf16[7168,512]{1,0:T(8,128)(2,1)S(1)} %bitcast.42), kind=kOutput, calls=%fused_computation.38 | convolution fusion | flops 1409286144 | bytes 10485760 | tf_op jit(solution)/shard_map/dot_general | solution.py:29
  65.2 0.0 slice-done
  65.2 0.0 slice-done.1
  65.2 0.9 convolution_multiply_fusion.1
  66.1 0.0 copy-start.1
  66.1 1.0 fusion.1
  67.1 35.2 %all_to_all.15 = bf16[4,48,7168]{2,1,0:T(8,128)(2,1)S(1)} all-to-all(bf16[4,48,7168]{2,1,0:T(8,128)(2,1)S(1)} %bitcast.40), channel_id=1, replica_groups=mesh['rep'=2,'grp'=4,'exp'=4] {'grp'}, dimensions={0} | all-to-all | bytes 5505024 | tf_op jit(solution)/shard_map/all_to_all | solution.py:63
  102.4 1.6 %fusion.2 = bf16[64,7168]{1,0:T(8,128)(2,1)} fusion(bf16[4,48,7168]{2,1,0:T(8,128)(2,1)S(1)} %all_to_all.15, s32[4,64]{1,0:T(4,128)S(1)} %copy.14, pred[4,64]{1,0:T(4,128)(4,1)S(1)} %compare_bitcast_fusion), kind=kOutput, calls=%fused_computation.6 | convolution fusion | flops 176644096 | bytes 3671296 | tf_op jit(solution)/shard_map/gct,gcd->td/dot_general | solution.py:64
  104.0 0.0 reduce-scatter.2.cloned.1.call-update
  104.0 26.0 %reduce-scatter.2.cloned.1.call-done = bf16[16,7168]{1,0:T(8,128)(2,1)} async-done(((bf16[64,7168]{1,0:T(8,128)(2,1)}), bf16[16,7168]{1,0:T(8,128)(2,1)}) %reduce-scatter.2.cloned.1.call-update) | async-done | bytes 229392 | tf_op jit(solution)/shard_map/reduce_scatter | solution.py:65
  130.0 0.0 copy-done.1
  (5 shorter events, 0.0 us)
Async XLA Ops:
  6.5 8.0 %copy-start = (bf16[64,7168]{1,0:T(8,128)(2,1)S(1)}, bf16[64,7168]{1,0:T(8,128)(2,1)}, u32[]{:S(2)}) copy-start(bf16[64,7168]{1,0:T(8,128)(2,1)} %param.5) | copy-start | bytes 2752516
  10.3 7.9 %all-to-all-start = ((bf16[4,48,2]{1,2,0:T(2,128)(2,1)}), bf16[4,48,2]{1,2,0:T(2,128)(2,1)S(1)}, u32[]{:S(2)}, u32[]{:S(2)}) async-start(bf16[4,48,2]{1,2,0:T(2,128)(2,1)} %convolution_convert_fusion.2), calls=%async_computation | async-start | bytes 4096 | tf_op jit(solution)/shard_map/all_to_all | solution.py:57
  18.2 37.4 %all-to-all-start.1 = ((bf16[4,48,7168]{2,1,0:T(8,128)(2,1)}), bf16[4,48,7168]{2,1,0:T(8,128)(2,1)}, u32[]{:S(2)}, u32[]{:S(2)}) async-start(bf16[4,48,7168]{2,1,0:T(8,128)(2,1)} %convolution_convert_fusion), calls=%async_computation.1 | async-start | bytes 5505024 | tf_op jit(solution)/shard_map/all_to_all | solution.py:56
  22.8 107.2 %reduce-scatter.2.cloned.1.call-start = ((), (), s32[]{:S(2)}) async-start(), calls=%async_computation.4 | async-start | bytes 1146880 | tf_op jit(solution)/shard_map/reduce_scatter | solution.py:65
  55.5 6.0 %copy-start.2 = (bf16[896,8,2,256]{3,1,2,0:T(8,128)(2,1)S(1)}, bf16[896,8,2,256]{3,1,2,0:T(8,128)(2,1)}, u32[]{:S(2)}) copy-start(bf16[896,8,2,256]{3,1,2,0:T(8,128)(2,1)} %copy.20) | copy-start | bytes 22020100
  55.5 9.6 %slice-start = ((s8[7340032]{0:T(1024)(128)(4,1)}), s8[4194304]{0:T(1024)(128)(4,1)S(1)}, s32[]{:S(2)}) async-start(s8[7340032]{0:T(1024)(128)(4,1)} %bitcast.43), calls=%async_computation.5 | async-start | bytes 8388608
  61.5 3.6 %slice-start.1 = ((s8[7340032]{0:T(1024)(128)(4,1)}), s8[3145728]{0:T(1024)(128)(4,1)S(1)}, s32[]{:S(2)}) async-start(s8[7340032]{0:T(1024)(128)(4,1)} %bitcast.43), calls=%async_computation.6 | async-start | bytes 6291456
  66.1 63.8 %copy-start.1 = (bf16[64,7168]{1,0:T(8,128)(2,1)S(1)}, bf16[64,7168]{1,0:T(8,128)(2,1)}, u32[]{:S(2)}) copy-start(bf16[64,7168]{1,0:T(8,128)(2,1)} %param.5) | copy-start | bytes 2752516
Sparse Core Ops, SparseCore 0:
  104.1 25.7 reduce-scatter.1
where the time goes:
time: 137 us
  waiting for transfers between devices  35.9 us (26%)
  blocking collectives  35.2 us (26%)
  local copies, waits for them, and re-layouts  25.6 us (19%)
  matrix products  16.1 us (12%)
  between operations  13.5 us (10%)
  starting transfers between devices  8.85 us (6%)
  other arithmetic  1.57 us (1%)
    all_to_all x1, blocking collectives, local(): lax.all_to_all(parts, 'grp', split_axis=0, concat_axis=0, tiled=True)  35.2 us
    reduce_scatter x1, waiting for transfers between devices, local(): lax.psum_scatter(local_sum.astype(jnp.bfloat16), 'exp', scatter_dimension...  26 us
    slice x1, local copies, waits for them, and re-layouts, run_experts(): w_in[member].reshape(feature_width, 2 * hidden_dev)  12.4 us
    unnamed x12, local copies, waits for them, and re-layouts  11.9 us
    dot_general x2, matrix products, run_experts(): jnp.dot(rows, w_in[member].reshape(feature_width, 2 * hidden_dev), prefer...  9.26 us
    all_to_all x1, waiting for transfers between devices, local(): lax.all_to_all(packed, 'grp', split_axis=0, concat_axis=0, tiled=True)  8.67 us
    all_to_all x1, starting transfers between devices, local(): lax.all_to_all(packed, 'grp', split_axis=0, concat_axis=0, tiled=True)  4.57 us
    all_to_all x1, starting transfers between devices, local(): lax.all_to_all(packed_gates, 'grp', split_axis=0, concat_axis=0, tiled=True)  4.24 us
  transfers between devices with their start and end apart: 3, of which 3 were waited for; matrix products, arithmetic and copies ran while one was open for 19% of the time, Pallas kernels for 0%

commit v1 on v0

v1 whole, which is shorter than its diff:
```python
import functools

import jax
import jax.numpy as jnp
from jax import lax
from jax.experimental import pallas as pl
from jax.experimental.pallas import tpu as pltpu
from jax.sharding import PartitionSpec as P

F32 = jnp.float32
BF16 = jnp.bfloat16
LANES = 128
VMEM_LIMIT = 40 << 20


def bits_of(count):
    bits = count.bit_length() - 1
    assert 1 << bits == count
    return bits


def bit_reverse(value, bits):
    return sum(((value >> b) & 1) << (bits - 1 - b) for b in range(bits))


def exchange(x, axis, mask):
    return lax.ppermute(x, axis, [(i, i ^ mask) for i in range(lax.axis_size(axis))])


def add(*terms):
    return sum(t.astype(F32) for t in terms).astype(BF16)


def split(total, unit, shares):
    edges, whole = [0], total // unit
    for i in range(len(shares)):
        edges.append(round(whole * sum(shares[: i + 1]) / sum(shares)) * unit)
    return [(a, b - a) for a, b in zip(edges, edges[1:]) if b > a]


def gate_table(group_ids, gates):
    lane = lax.broadcasted_iota(jnp.int32, (group_ids.shape[0], LANES), 1)
    table = jnp.zeros(lane.shape, BF16)
    for k in range(group_ids.shape[1]):
        pair = jnp.where(lane % 2 == 0, gates[:, 2 * k, None], gates[:, 2 * k + 1, None])
        table = jnp.where(lane // 2 == group_ids[:, k, None], pair, table)
    return table


def up_kernel(first, last, blocks, hidden, parts, *refs):
    refs = list(refs)
    place = refs.pop(0) if last else None
    xs = [refs.pop(0) for _ in range(blocks)]
    w_ref = refs.pop(0)
    before = None if first else refs.pop(0)
    tables = [refs.pop(0) for _ in range(blocks)] if last else []
    out_ref = refs.pop(0)
    wide = refs.pop(0)
    acc = refs.pop(0) if last else out_ref
    step = pl.program_id(0)
    depth = xs[0].shape[1]
    rows = xs[0].shape[0]
    halves = hidden // LANES

    @pl.when(step == 0)
    def _():
        acc[...] = jnp.zeros_like(acc) if first else before[...]

    x = jnp.concatenate([ref[...] for ref in xs], axis=0)
    for member in range(2):
        wide[...] = w_ref[member].astype(F32)
        weights = jnp.concatenate(
            [
                wide[pl.ds(2 * t + s, depth, stride=2 * halves), :].astype(BF16)
                for s in range(2)
                for t in range(halves)
            ],
            axis=1,
        )
        acc[member] += jnp.dot(x, weights, preferred_element_type=F32)

    if last:

        @pl.when(step == pl.num_programs(0) - 1)
        def _():
            group, slot = place[0], place[1]
            bits = bits_of(parts)
            part = rows // parts
            lane = lax.broadcasted_iota(jnp.int32, (rows, LANES), 1)
            for position in range(blocks):
                block = bit_reverse(position, bits_of(blocks))
                table = tables[block][...].astype(F32)
                for member in range(2):
                    gate = jnp.sum(
                        jnp.where(lane == 2 * group + member, table, 0.0), axis=1, keepdims=True
                    )
                    both = acc[member, pl.ds(block * rows, rows), :]
                    a, b = both[:, :hidden], both[:, hidden:]
                    acc[member, pl.ds(block * rows, rows), :hidden] = gate * (jax.nn.silu(a) * b)
                    pieces = []
                    for p in range(parts):
                        source = jnp.bitwise_xor(bit_reverse(p, bits), slot)
                        start = pl.multiple_of(block * rows + source * part, part)
                        pieces.append(acc[member, pl.ds(start, part), :hidden])
                    out_ref[pl.ds(position * rows, rows), pl.ds(member * hidden, hidden)] = (
                        jnp.concatenate(pieces, axis=0).astype(BF16)
                    )


def up_step(xs, w_view, before, tables, place, start, width, hidden, parts):
    first, last = before is None, tables is not None
    blocks, rows = len(xs), xs[0].shape[0]
    depth = width
    ratio = w_view.shape[1] // w_view_depth(w_view, hidden)
    steps = width // depth
    offset = start // depth if start % depth == 0 else None
    if offset is None:
        raise ValueError("uneven chunk")
    operands, specs = [], []
    if last:
        operands.append(place)
        specs.append(pl.BlockSpec(memory_space=pltpu.SMEM))
    for x in xs:
        base = offset if x.shape[1] != width else 0
        operands.append(x)
        specs.append(pl.BlockSpec((rows, depth), lambda j, base=base: (0, base + j)))
    operands.append(w_view)
    specs.append(pl.BlockSpec((2, depth * ratio, LANES), lambda j: (0, offset + j, 0)))
    acc_shape = (2, blocks * rows, 2 * hidden)
    if not first:
        operands.append(before)
        specs.append(pl.BlockSpec(acc_shape, lambda j: (0, 0, 0)))
    if last:
        operands += tables
        specs += [pl.BlockSpec((rows, LANES), lambda j: (0, 0))] * blocks
    scratch = [pltpu.VMEM((depth * ratio, LANES), F32)]
    if last:
        scratch.append(pltpu.VMEM(acc_shape, F32))
        out_shape = jax.ShapeDtypeStruct((blocks * rows, 2 * hidden), BF16)
        out_spec = pl.BlockSpec(out_shape.shape, lambda j: (0, 0))
    else:
        out_shape = jax.ShapeDtypeStruct(acc_shape, F32)
        out_spec = pl.BlockSpec(acc_shape, lambda j: (0, 0, 0))
    return pl.pallas_call(
        functools.partial(up_kernel, first, last, blocks, hidden, parts),
        grid=(steps,),
        in_specs=specs,
        out_specs=out_spec,
        out_shape=out_shape,
        scratch_shapes=scratch,
        compiler_params=pltpu.CompilerParams(vmem_limit_bytes=VMEM_LIMIT),
        cost_estimate=pl.CostEstimate(
            flops=8 * blocks * rows * width * hidden,
            bytes_accessed=8 * width * hidden,
            transcendentals=0,
        ),
        name="up_last" if last else "up",
    )(*operands)


def w_view_depth(w_view, hidden):
    return w_view.shape[1] * LANES // (2 * hidden)


def down_kernel(h_ref, w_ref, keep_ref, send_ref):
    out = jnp.dot(h_ref[...], w_ref[...], preferred_element_type=F32).astype(BF16)
    half = keep_ref.shape[0]
    keep_ref[...] = out[:half]
    send_ref[...] = out[half:]


def down_step(hidden_rows, w_flat, start, width, unit):
    rows, depth = hidden_rows.shape
    offset = start // unit
    half = jax.ShapeDtypeStruct((rows // 2, width), BF16)
    spec = pl.BlockSpec((rows // 2, unit), lambda j: (0, j))
    return pl.pallas_call(
        down_kernel,
        grid=(width // unit,),
        in_specs=[
            pl.BlockSpec((rows, depth), lambda j: (0, 0)),
            pl.BlockSpec((depth, unit), lambda j: (0, offset + j)),
        ],
        out_specs=[spec, spec],
        out_shape=[half, half],
        compiler_params=pltpu.CompilerParams(vmem_limit_bytes=VMEM_LIMIT),
        cost_estimate=pl.CostEstimate(
            flops=2 * rows * width * depth, bytes_accessed=2 * width * depth, transcendentals=0
        ),
        name="down",
    )(hidden_rows, w_flat)


def local(tokens, group_ids, gates, w_in, w_down):
    groups, parts = lax.axis_size("grp"), lax.axis_size("exp")
    rows, features = tokens.shape
    hidden = w_in.shape[3]
    group_bits, part_bits = bits_of(groups), bits_of(parts)
    w_view = (
        w_in.reshape(2, features, 2, hidden // LANES, LANES)
        .transpose(0, 1, 3, 2, 4)
        .reshape(2, -1, LANES)
    )
    w_flat = w_down.reshape(2 * hidden, features)
    place = jnp.stack([lax.axis_index("grp"), lax.axis_index("exp")]).astype(jnp.int32)

    def spread(x):
        held = {0: x}
        for bit in reversed(range(group_bits)):
            for r in list(held):
                held[r | 1 << bit] = exchange(held[r], "grp", 1 << bit)
        return held

    beside = exchange(tokens, "grp", 1)
    chunks = split(features, features // 4, [1, 1, 1, 1])
    tables = spread(gate_table(group_ids, gates))
    value = None
    for at, (start, width) in enumerate(chunks):
        held = {0: lax.slice_in_dim(tokens, start, start + width, axis=1)}
        for bit in reversed(range(group_bits)):
            for r in list(held):
                if r or bit:
                    held[r | 1 << bit] = exchange(held[r], "grp", 1 << bit)
        held[0], held[1] = tokens, beside
        last = at == len(chunks) - 1
        value = up_step(
            [held[r] for r in range(groups)],
            w_view,
            value,
            [tables[r] for r in range(groups)] if last else None,
            place,
            start,
            width,
            hidden,
            parts,
        )

    unit = features // 7
    outs = []
    for start, width in split(features, unit, [1, 2, 2, 1, 1]):
        keep, send = down_step(value, w_flat, start, width, unit)
        terms, height = [keep], keep.shape[0]
        terms.append(exchange(send, "grp", 1))
        for axis, bit in [("grp", b) for b in range(1, group_bits)] + [
            ("exp", b) for b in range(part_bits)
        ]:
            height //= 2
            send = add(*[t[height : 2 * height] for t in terms])
            terms.append(exchange(send, axis, 1 << bit))
        outs.append(add(*[t[:height] for t in terms]))
    return jnp.concatenate(outs, axis=1)


def solution(mesh):
    in_specs = (
        P(("rep", "grp"), None),
        P(("rep", "grp"), None),
        P(("rep", "grp"), None),
        P("grp", None, None, "exp"),
        P("grp", "exp", None),
    )
    out_specs = P(("rep", "grp", "exp"), None)
    return jax.shard_map(local, mesh=mesh, in_specs=in_specs, out_specs=out_specs, check_vma=False)
```

time: 137 us -> 93.1 us (0.68)
  blocking collectives: 35.2 us -> 0 us
  starting transfers between devices: 8.85 us -> 32.3 us
  local copies, waits for them, and re-layouts: 25.6 us -> 4.8 us
  Pallas kernels: 0 us -> 18.3 us
  matrix products: 16.1 us -> 0 us
  between operations: 13.5 us -> 0.3 us
    ppermute x0 -> x32, waiting for transfers between devices: none -> 35.6 us  [exchange(): lax.ppermute(x, axis, [(i, i ^ mask) for i in range(lax.axis_size(axis))])]
    all_to_all x1 -> x0, blocking collectives: 35.2 us -> none  [local(): lax.all_to_all(parts, 'grp', split_axis=0, concat_axis=0, tiled=True)]
    ppermute x0 -> x32, starting transfers between devices: none -> 32.3 us  [exchange(): lax.ppermute(x, axis, [(i, i ^ mask) for i in range(lax.axis_size(axis))])]
    reduce_scatter x1 -> x0, waiting for transfers between devices: 26 us -> none  [local(): lax.psum_scatter(local_sum.astype(jnp.bfloat16), 'exp', scatter_dimension...]
    pallas_call x0 -> x9, Pallas kernels: none -> 18.3 us  [the longest x4 14.7 us: up_step(): pl.pallas_call(functools.partial(up_kernel, first, last, blocks, hidden,...]
    dot_general x8 -> x0, matrix products: 16.1 us -> none  [the longest x2 9.26 us: run_experts(): jnp.dot(rows, w_in[member].reshape(feature_width, 2 * hidden_dev), prefer...]
    slice x1, local copies, waits for them, and re-layouts: 12.4 us -> 1.34 us  [local(): held = {0: lax.slice_in_dim(tokens, start, start + width, axis=1)}]
    unnamed x12 -> x8, local copies, waits for them, and re-layouts: 11.9 us -> 1.87 us
  transfers between devices with their start and end apart: 3 -> 32, of which waited for: 3 -> 11; matrix products, arithmetic and copies ran while one was open for 19% -> 4% of each run, Pallas kernels for 0% -> 15%
where the time goes in v1:
time: 93.1 us; the launch traced here: 92.8 us
  waiting for transfers between devices  35.6 us (38%)
  starting transfers between devices  32.3 us (35%)
  Pallas kernels  18.3 us (20%)
  local copies, waits for them, and re-layouts  4.8 us (5%)
  other arithmetic  1.54 us (2%)
    ppermute x32, waiting for transfers between devices, exchange(): lax.ppermute(x, axis, [(i, i ^ mask) for i in range(lax.axis_size(axis))])  35.6 us
    ppermute x32, starting transfers between devices, exchange(): lax.ppermute(x, axis, [(i, i ^ mask) for i in range(lax.axis_size(axis))])  32.3 us
    pallas_call x4, Pallas kernels, up_step(): pl.pallas_call(functools.partial(up_kernel, first, last, blocks, hidden,...  14.7 us
    pallas_call x5, Pallas kernels, down_step(): pl.pallas_call(down_kernel, grid=(width // unit,), in_specs=[pl.BlockSpec...  3.54 us
    unnamed x8, local copies, waits for them, and re-layouts  1.87 us
  transfers between devices with their start and end apart: 32, of which 11 were waited for; matrix products, arithmetic and copies ran while one was open for 4% of the time, Pallas kernels for 15%

profile of v1, /device:TPU:0, one launch (start us, length us, event | category | flops | bytes accessed | tf_op | source)
XLA Modules:
  0.0 92.8 jit_solution(10809853589223958675)
XLA Ops:
  0.0 0.5 collective-permute-start
  0.5 1.3 %fusion.9 = (bf16[64,1792]{1,0:T(8,128)(2,1)S(1)}, bf16[64,1792]{1,0:T(8,128)(2,1)S(1)}, bf16[64,1792]{1,0:T(8,128)(2,1)S(1)}, bf16[64,1792]{1,0:T(8,128)(2,1)S(1)}) fusion(bf16[64,7168]{1,0:T(8,128)(2,1)} %refs_1_.1), kind=kLoop, calls=%fused_computation.46 | loop fusion | bytes 1835008 | tf_op jit(solution)/shard_map/slice | solution.py:219
  1.8 2.6 %collective-permute-start.3 = (bf16[64,1792]{1,0:T(8,128)(2,1)S(1)}, bf16[64,1792]{1,0:T(8,128)(2,1)S(1)}, u32[]{:S(2)}, u32[]{:S(2)}) collective-permute-start(bf16[64,1792]{1,0:T(8,128)(2,1)S(1)} %get-tuple-element.27), channel_id=1, source_target_pairs={{0,8},{4,12},{8,0},{12,4},{1,9},{5,13},{9,1},{13,5},{2,10},{6,14},... | collective-permute-start | bytes 688136 | tf_op jit(solution)/shard_map/ppermute | solution.py:27
  4.5 1.9 %collective-permute-start.7 = (bf16[64,1792]{1,0:T(8,128)(2,1)S(1)}, bf16[64,1792]{1,0:T(8,128)(2,1)S(1)}, u32[]{:S(2)}, u32[]{:S(2)}) collective-permute-start(bf16[64,1792]{1,0:T(8,128)(2,1)S(1)} %get-tuple-element.25), channel_id=1, source_target_pairs={{0,8},{4,12},{8,0},{12,4},{1,9},{5,13},{9,1},{13,5},{2,10},{6,14},... | collective-permute-start | bytes 688136 | tf_op jit(solution)/shard_map/ppermute | solution.py:27
  6.4 0.8 slice_bitcast_fusion.5
  7.2 0.8 slice_bitcast_fusion.4
  8.3 12.6 %collective-permute-done.10.refs_9_ = bf16[64,128]{1,0:T(8,128)(2,1)S(1)} collective-permute-done((bf16[64,128]{1,0:T(8,128)(2,1)S(1)}, bf16[64,128]{1,0:T(8,128)(2,1)S(1)}, u32[]{:S(2)}, u32[]{:S(2)}) %collective-permute-start.10) | collective-permute-done | bytes 16416 | tf_op jit(solution)/shard_map/ppermute | solution.py:27
  20.8 1.8 %collective-permute-start.1 = (bf16[64,1792]{1,0:T(8,128)(2,1)S(1)}, bf16[64,1792]{1,0:T(8,128)(2,1)S(1)}, u32[]{:S(2)}, u32[]{:S(2)}) collective-permute-start(bf16[64,1792]{1,0:T(8,128)(2,1)S(1)} %get-tuple-element.28), channel_id=1, source_target_pairs={{0,8},{4,12},{8,0},{12,4},{1,9},{5,13},{9,1},{13,5},{2,10},{6,14},... | collective-permute-start | bytes 688136 | tf_op jit(solution)/shard_map/ppermute | solution.py:27
  22.6 0.5 collective-permute-start.6
  23.3 5.0 %collective-permute-done.1.refs_3_ = bf16[64,1792]{1,0:T(8,128)(2,1)S(1)} collective-permute-done((bf16[64,1792]{1,0:T(8,128)(2,1)S(1)}, bf16[64,1792]{1,0:T(8,128)(2,1)S(1)}, u32[]{:S(2)}, u32[]{:S(2)}) %collective-permute-start.1) | collective-permute-done | bytes 229408 | tf_op jit(solution)/shard_map/ppermute | solution.py:27
  28.3 0.5 collective-permute-start.11
  28.9 1.2 %copy-done = bf16[64,7168]{1,0:T(8,128)(2,1)S(1)} copy-done((bf16[64,7168]{1,0:T(8,128)(2,1)S(1)}, bf16[64,7168]{1,0:T(8,128)(2,1)}, u32[]{:S(2)}) %copy-start) | copy-done | bytes 917528
  30.0 3.6 %up.3.refs_5_ = f32[2,256,512]{2,1,0:T(8,128)S(1)} custom-call(bf16[64,7168]{1,0:T(8,128)(2,1)S(1)} %copy-done, bf16[64,7168]{1,0:T(8,128)(2,1)S(1)} %collective-permute-done.refs_1_.refs_2_, bf16[64,1792]{1,0:T(8,128)(2,1)S(1)} %collective-permute-done.7.refs_2_, bf16[64,1792]{1,0:T(8,128)(2,1)S(1)} %collective-permute-done.8.refs_3_, ...), custom_call_target="tpu_custom_call" | custom-call | flops 939524096 | bytes 3670016 | tf_op jit(solution)/shard_map/up/pallas_call | solution.py:144
  33.6 3.7 %up.4.refs_5_ = f32[2,256,512]{2,1,0:T(8,128)S(1)} custom-call(bf16[64,7168]{1,0:T(8,128)(2,1)S(1)} %copy-done, bf16[64,7168]{1,0:T(8,128)(2,1)S(1)} %collective-permute-done.refs_1_.refs_2_, bf16[64,1792]{1,0:T(8,128)(2,1)S(1)} %collective-permute-done.5.refs_2_, bf16[64,1792]{1,0:T(8,128)(2,1)S(1)} %collective-permute-done.6.refs_3_, ...), custom_call_target="tpu_custom_call" | custom-call | flops 939524096 | bytes 3670016 | tf_op jit(solution)/shard_map/up/pallas_call | solution.py:144
  37.4 3.7 %up.5.refs_6_ = f32[2,256,512]{2,1,0:T(8,128)S(1)} custom-call(bf16[64,7168]{1,0:T(8,128)(2,1)S(1)} %copy-done, bf16[64,7168]{1,0:T(8,128)(2,1)S(1)} %collective-permute-done.refs_1_.refs_2_, bf16[64,1792]{1,0:T(8,128)(2,1)S(1)} %collective-permute-done.3.refs_2_, bf16[64,1792]{1,0:T(8,128)(2,1)S(1)} %collective-permute-done.4.refs_3_, ...), custom_call_target="tpu_custom_call" | custom-call | flops 939524096 | bytes 3670016 | tf_op jit(solution)/shard_map/up/pallas_call | solution.py:144
  41.2 3.7 %up_last.1.h_ref = bf16[256,512]{1,0:T(8,128)(2,1)S(1)} custom-call(s32[2]{0:T(128)S(1)} %pad_add_fusion.refs_0_, bf16[64,7168]{1,0:T(8,128)(2,1)S(1)} %copy-done, bf16[64,7168]{1,0:T(8,128)(2,1)S(1)} %collective-permute-done.refs_1_.refs_2_, bf16[64,1792]{1,0:T(8,128)(2,1)S(1)} %collective-permute-done.1.refs_3_, ...), custom_call_target="tpu_custom_call" | custom-call | flops 939524096 | bytes 3670016 | tf_op jit(solution)/shard_map/up_last/pallas_call | solution.py:144
  44.9 0.4 down.5
  45.4 0.5 collective-permute-start.12
  45.9 0.4 down.8
  46.4 1.1 %down.6 = (bf16[128,2048]{1,0:T(8,128)(2,1)S(1)}, bf16[128,2048]{1,0:T(8,128)(2,1)S(1)}) custom-call(bf16[256,512]{1,0:T(8,128)(2,1)S(1)} %up_last.1.h_ref, bf16[512,7168]{1,0:T(8,128)(2,1)S(1)} %bitcast.24), custom_call_target="tpu_custom_call" | custom-call | flops 536870912 | bytes 2097152 | tf_op jit(solution)/shard_map/down/pallas_call | solution.py:177
  47.6 1.1 %down.7 = (bf16[128,2048]{1,0:T(8,128)(2,1)S(1)}, bf16[128,2048]{1,0:T(8,128)(2,1)S(1)}) custom-call(bf16[256,512]{1,0:T(8,128)(2,1)S(1)} %up_last.1.h_ref, bf16[512,7168]{1,0:T(8,128)(2,1)S(1)} %bitcast.25), custom_call_target="tpu_custom_call" | custom-call | flops 536870912 | bytes 2097152 | tf_op jit(solution)/shard_map/down/pallas_call | solution.py:177
  48.7 0.5 collective-permute-start.16
  49.3 0.4 down.9
  49.7 0.5 collective-permute-start.28
  50.3 1.6 %collective-permute-start.13 = (bf16[64,1024]{1,0:T(8,128)(2,1)S(1)}, bf16[64,1024]{1,0:T(8,128)(2,1)S(1)}, u32[]{:S(2)}, u32[]{:S(2)}) collective-permute-start(bf16[64,1024]{1,0:T(8,128)(2,1)S(1)} %add_convert_fusion.6), channel_id=1, source_target_pairs={{0,8},{4,12},{8,0},{12,4},{1,9},{5,13},{9,1},{13,5},{2,10},{6,14},... | collective-permute-start | bytes 393224 | tf_op jit(solution)/shard_map/ppermute | solution.py:27
  52.0 0.5 collective-permute-start.25
  52.5 1.6 %collective-permute-start.29 = (bf16[64,1024]{1,0:T(8,128)(2,1)S(1)}, bf16[64,1024]{1,0:T(8,128)(2,1)S(1)}, u32[]{:S(2)}, u32[]{:S(2)}) collective-permute-start(bf16[64,1024]{1,0:T(8,128)(2,1)S(1)} %add_convert_fusion.2), channel_id=1, source_target_pairs={{0,8},{4,12},{8,0},{12,4},{1,9},{5,13},{9,1},{13,5},{2,10},{6,14},... | collective-permute-start | bytes 393224 | tf_op jit(solution)/shard_map/ppermute | solution.py:27
  54.2 2.5 %collective-permute-done.13 = bf16[64,1024]{1,0:T(8,128)(2,1)S(1)} collective-permute-done((bf16[64,1024]{1,0:T(8,128)(2,1)S(1)}, bf16[64,1024]{1,0:T(8,128)(2,1)S(1)}, u32[]{:S(2)}, u32[]{:S(2)}) %collective-permute-start.13) | collective-permute-done | bytes 131104 | tf_op jit(solution)/shard_map/ppermute | solution.py:27
  56.7 1.7 %collective-permute-start.14 = (bf16[32,1024]{1,0:T(8,128)(2,1)S(1)}, bf16[32,1024]{1,0:T(8,128)(2,1)S(1)}, u32[]{:S(2)}, u32[]{:S(2)}) collective-permute-start(bf16[32,1024]{1,0:T(8,128)(2,1)S(1)} %add_convert_fusion.13), channel_id=1, source_target_pairs={{0,1},{1,0},{2,3},{3,2},{4,5},{5,4},{6,7},{7,6},{8,9},{9,8},{10,11... | collective-permute-start | bytes 196616 | tf_op jit(solution)/shard_map/ppermute | solution.py:27
  58.4 1.1 %collective-permute-done.25 = bf16[64,1024]{1,0:T(8,128)(2,1)S(1)} collective-permute-done((bf16[64,1024]{1,0:T(8,128)(2,1)S(1)}, bf16[64,1024]{1,0:T(8,128)(2,1)S(1)}, u32[]{:S(2)}, u32[]{:S(2)}) %collective-permute-start.25) | collective-permute-done | bytes 131104 | tf_op jit(solution)/shard_map/ppermute | solution.py:27
  59.5 1.7 %collective-permute-start.26 = (bf16[32,1024]{1,0:T(8,128)(2,1)S(1)}, bf16[32,1024]{1,0:T(8,128)(2,1)S(1)}, u32[]{:S(2)}, u32[]{:S(2)}) collective-permute-start(bf16[32,1024]{1,0:T(8,128)(2,1)S(1)} %add_convert_fusion.8), channel_id=1, source_target_pairs={{0,1},{1,0},{2,3},{3,2},{4,5},{5,4},{6,7},{7,6},{8,9},{9,8},{10,11... | collective-permute-start | bytes 196616 | tf_op jit(solution)/shard_map/ppermute | solution.py:27
  61.5 1.7 %collective-permute-start.30 = (bf16[32,1024]{1,0:T(8,128)(2,1)S(1)}, bf16[32,1024]{1,0:T(8,128)(2,1)S(1)}, u32[]{:S(2)}, u32[]{:S(2)}) collective-permute-start(bf16[32,1024]{1,0:T(8,128)(2,1)S(1)} %add_convert_fusion.7), channel_id=1, source_target_pairs={{0,1},{1,0},{2,3},{3,2},{4,5},{5,4},{6,7},{7,6},{8,9},{9,8},{10,11... | collective-permute-start | bytes 196616 | tf_op jit(solution)/shard_map/ppermute | solution.py:27
  63.2 2.7 %collective-permute-start.15 = (bf16[16,1024]{1,0:T(8,128)(2,1)S(1)}, bf16[16,1024]{1,0:T(8,128)(2,1)S(1)}, u32[]{:S(2)}, u32[]{:S(2)}) collective-permute-start(bf16[16,1024]{1,0:T(8,128)(2,1)S(1)} %add_convert_fusion.19), channel_id=1, source_target_pairs={{0,2},{1,3},{2,0},{3,1},{4,6},{5,7},{6,4},{7,5},{8,10},{9,11},{10,... | collective-permute-start | bytes 98312 | tf_op jit(solution)/shard_map/ppermute | solution.py:27
  65.8 1.2 %collective-permute-start.27 = (bf16[16,1024]{1,0:T(8,128)(2,1)S(1)}, bf16[16,1024]{1,0:T(8,128)(2,1)S(1)}, u32[]{:S(2)}, u32[]{:S(2)}) collective-permute-start(bf16[16,1024]{1,0:T(8,128)(2,1)S(1)} %add_convert_fusion.17), channel_id=1, source_target_pairs={{0,2},{1,3},{2,0},{3,1},{4,6},{5,7},{6,4},{7,5},{8,10},{9,11},{10,... | collective-permute-start | bytes 98312 | tf_op jit(solution)/shard_map/ppermute | solution.py:27
  67.1 1.8 %collective-permute-start.31 = (bf16[16,1024]{1,0:T(8,128)(2,1)S(1)}, bf16[16,1024]{1,0:T(8,128)(2,1)S(1)}, u32[]{:S(2)}, u32[]{:S(2)}) collective-permute-start(bf16[16,1024]{1,0:T(8,128)(2,1)S(1)} %add_convert_fusion.15), channel_id=1, source_target_pairs={{0,2},{1,3},{2,0},{3,1},{4,6},{5,7},{6,4},{7,5},{8,10},{9,11},{10,... | collective-permute-start | bytes 98312 | tf_op jit(solution)/shard_map/ppermute | solution.py:27
  69.0 1.6 %collective-permute-start.17 = (bf16[64,2048]{1,0:T(8,128)(2,1)S(1)}, bf16[64,2048]{1,0:T(8,128)(2,1)S(1)}, u32[]{:S(2)}, u32[]{:S(2)}) collective-permute-start(bf16[64,2048]{1,0:T(8,128)(2,1)S(1)} %add_convert_fusion.1), channel_id=1, source_target_pairs={{0,8},{4,12},{8,0},{12,4},{1,9},{5,13},{9,1},{13,5},{2,10},{6,14},... | collective-permute-start | bytes 786440 | tf_op jit(solution)/shard_map/ppermute | solution.py:27
  70.7 0.6 collective-permute-start.21
  71.3 7.0 %collective-permute-done.17 = bf16[64,2048]{1,0:T(8,128)(2,1)S(1)} collective-permute-done((bf16[64,2048]{1,0:T(8,128)(2,1)S(1)}, bf16[64,2048]{1,0:T(8,128)(2,1)S(1)}, u32[]{:S(2)}, u32[]{:S(2)}) %collective-permute-start.17) | collective-permute-done | bytes 262176 | tf_op jit(solution)/shard_map/ppermute | solution.py:27
  78.3 1.5 %collective-permute-start.18 = (bf16[32,2048]{1,0:T(8,128)(2,1)S(1)}, bf16[32,2048]{1,0:T(8,128)(2,1)S(1)}, u32[]{:S(2)}, u32[]{:S(2)}) collective-permute-start(bf16[32,2048]{1,0:T(8,128)(2,1)S(1)} %add_convert_fusion.5), channel_id=1, source_target_pairs={{0,1},{1,0},{2,3},{3,2},{4,5},{5,4},{6,7},{7,6},{8,9},{9,8},{10,11... | collective-permute-start | bytes 393224 | tf_op jit(solution)/shard_map/ppermute | solution.py:27
  79.8 1.3 %collective-permute-done.21 = bf16[64,2048]{1,0:T(8,128)(2,1)S(1)} collective-permute-done((bf16[64,2048]{1,0:T(8,128)(2,1)S(1)}, bf16[64,2048]{1,0:T(8,128)(2,1)S(1)}, u32[]{:S(2)}, u32[]{:S(2)}) %collective-permute-start.21) | collective-permute-done | bytes 262176 | tf_op jit(solution)/shard_map/ppermute | solution.py:27
  81.1 1.5 %collective-permute-start.22 = (bf16[32,2048]{1,0:T(8,128)(2,1)S(1)}, bf16[32,2048]{1,0:T(8,128)(2,1)S(1)}, u32[]{:S(2)}, u32[]{:S(2)}) collective-permute-start(bf16[32,2048]{1,0:T(8,128)(2,1)S(1)} %add_convert_fusion.4), channel_id=1, source_target_pairs={{0,1},{1,0},{2,3},{3,2},{4,5},{5,4},{6,7},{7,6},{8,9},{9,8},{10,11... | collective-permute-start | bytes 393224 | tf_op jit(solution)/shard_map/ppermute | solution.py:27
  82.6 1.9 %collective-permute-done.18 = bf16[32,2048]{1,0:T(8,128)(2,1)S(1)} collective-permute-done((bf16[32,2048]{1,0:T(8,128)(2,1)S(1)}, bf16[32,2048]{1,0:T(8,128)(2,1)S(1)}, u32[]{:S(2)}, u32[]{:S(2)}) %collective-permute-start.18) | collective-permute-done | bytes 131104 | tf_op jit(solution)/shard_map/ppermute | solution.py:27
  84.5 1.3 %collective-permute-start.19 = (bf16[16,2048]{1,0:T(8,128)(2,1)S(1)}, bf16[16,2048]{1,0:T(8,128)(2,1)S(1)}, u32[]{:S(2)}, u32[]{:S(2)}) collective-permute-start(bf16[16,2048]{1,0:T(8,128)(2,1)S(1)} %add_convert_fusion.12), channel_id=1, source_target_pairs={{0,2},{1,3},{2,0},{3,1},{4,6},{5,7},{6,4},{7,5},{8,10},{9,11},{10,... | collective-permute-start | bytes 196616 | tf_op jit(solution)/shard_map/ppermute | solution.py:27
  86.2 1.5 %collective-permute-start.23 = (bf16[16,2048]{1,0:T(8,128)(2,1)S(1)}, bf16[16,2048]{1,0:T(8,128)(2,1)S(1)}, u32[]{:S(2)}, u32[]{:S(2)}) collective-permute-start(bf16[16,2048]{1,0:T(8,128)(2,1)S(1)} %add_convert_fusion.10), channel_id=1, source_target_pairs={{0,2},{1,3},{2,0},{3,1},{4,6},{5,7},{6,4},{7,5},{8,10},{9,11},{10,... | collective-permute-start | bytes 196616 | tf_op jit(solution)/shard_map/ppermute | solution.py:27
  87.7 2.0 %collective-permute-done.19 = bf16[16,2048]{1,0:T(8,128)(2,1)S(1)} collective-permute-done((bf16[16,2048]{1,0:T(8,128)(2,1)S(1)}, bf16[16,2048]{1,0:T(8,128)(2,1)S(1)}, u32[]{:S(2)}, u32[]{:S(2)}) %collective-permute-start.19) | collective-permute-done | bytes 65568 | tf_op jit(solution)/shard_map/ppermute | solution.py:27
  89.8 1.6 %collective-permute-done.23 = bf16[16,2048]{1,0:T(8,128)(2,1)S(1)} collective-permute-done((bf16[16,2048]{1,0:T(8,128)(2,1)S(1)}, bf16[16,2048]{1,0:T(8,128)(2,1)S(1)}, u32[]{:S(2)}, u32[]{:S(2)}) %collective-permute-start.23) | collective-permute-done | bytes 65568 | tf_op jit(solution)/shard_map/ppermute | solution.py:27
  91.5 0.7 copy-done.1
  92.2 0.6 fusion.4
  (62 shorter events, 2.2 us)
Async XLA Ops:
  0.0 28.8 %collective-permute-start = (bf16[64,7168]{1,0:T(8,128)(2,1)}, bf16[64,7168]{1,0:T(8,128)(2,1)S(1)}, u32[]{:S(2)}, u32[]{:S(2)}) collective-permute-start(bf16[64,7168]{1,0:T(8,128)(2,1)} %refs_1_.1), channel_id=1, source_target_pairs={{0,4},{4,0},{8,12},{12,8},{1,5},{5,1},{9,13},{13,9},{2,6},{6,2},{1... | collective-permute-start | bytes 2752520 | tf_op jit(solution)/shard_map/ppermute | solution.py:27
  1.8 21.3 %collective-permute-start.3 = (bf16[64,1792]{1,0:T(8,128)(2,1)S(1)}, bf16[64,1792]{1,0:T(8,128)(2,1)S(1)}, u32[]{:S(2)}, u32[]{:S(2)}) collective-permute-start(bf16[64,1792]{1,0:T(8,128)(2,1)S(1)} %get-tuple-element.27), channel_id=1, source_target_pairs={{0,8},{4,12},{8,0},{12,4},{1,9},{5,13},{9,1},{13,5},{2,10},{6,14},... | collective-permute-start | bytes 688136 | tf_op jit(solution)/shard_map/ppermute | solution.py:27
  4.4 18.2 %collective-permute-start.5 = (bf16[64,1792]{1,0:T(8,128)(2,1)S(1)}, bf16[64,1792]{1,0:T(8,128)(2,1)S(1)}, u32[]{:S(2)}, u32[]{:S(2)}) collective-permute-start(bf16[64,1792]{1,0:T(8,128)(2,1)S(1)} %get-tuple-element.26), channel_id=1, source_target_pairs={{0,8},{4,12},{8,0},{12,4},{1,9},{5,13},{9,1},{13,5},{2,10},{6,14},... | collective-permute-start | bytes 688136 | tf_op jit(solution)/shard_map/ppermute | solution.py:27
  4.5 18.1 %collective-permute-start.7 = (bf16[64,1792]{1,0:T(8,128)(2,1)S(1)}, bf16[64,1792]{1,0:T(8,128)(2,1)S(1)}, u32[]{:S(2)}, u32[]{:S(2)}) collective-permute-start(bf16[64,1792]{1,0:T(8,128)(2,1)S(1)} %get-tuple-element.25), channel_id=1, source_target_pairs={{0,8},{4,12},{8,0},{12,4},{1,9},{5,13},{9,1},{13,5},{2,10},{6,14},... | collective-permute-start | bytes 688136 | tf_op jit(solution)/shard_map/ppermute | solution.py:27
  8.1 12.7 %collective-permute-start.10 = (bf16[64,128]{1,0:T(8,128)(2,1)S(1)}, bf16[64,128]{1,0:T(8,128)(2,1)S(1)}, u32[]{:S(2)}, u32[]{:S(2)}) collective-permute-start(bf16[64,128]{1,0:T(8,128)(2,1)S(1)} %fusion.7.refs_7_), channel_id=1, source_target_pairs={{0,8},{4,12},{8,0},{12,4},{1,9},{5,13},{9,1},{13,5},{2,10},{6,14},... | collective-permute-start | bytes 49160 | tf_op jit(solution)/shard_map/ppermute | solution.py:27
  20.8 7.4 %collective-permute-start.1 = (bf16[64,1792]{1,0:T(8,128)(2,1)S(1)}, bf16[64,1792]{1,0:T(8,128)(2,1)S(1)}, u32[]{:S(2)}, u32[]{:S(2)}) collective-permute-start(bf16[64,1792]{1,0:T(8,128)(2,1)S(1)} %get-tuple-element.28), channel_id=1, source_target_pairs={{0,8},{4,12},{8,0},{12,4},{1,9},{5,13},{9,1},{13,5},{2,10},{6,14},... | collective-permute-start | bytes 688136 | tf_op jit(solution)/shard_map/ppermute | solution.py:27
  22.6 5.7 %collective-permute-start.8 = (bf16[64,1792]{1,0:T(8,128)(2,1)S(1)}, bf16[64,1792]{1,0:T(8,128)(2,1)S(1)}, u32[]{:S(2)}, u32[]{:S(2)}) collective-permute-start(bf16[64,1792]{1,0:T(8,128)(2,1)S(1)} %collective-permute-done.7.refs_2_), channel_id=1, source_target_pairs={{0,4},{4,0},{8,12},{12,8},{1,5},{5,1},{9,13},{13,9},{2,6},{6,2},{1... | collective-permute-start | bytes 688136 | tf_op jit(solution)/shard_map/ppermute | solution.py:27
  22.6 11.0 %collective-permute-start.6 = (bf16[64,1792]{1,0:T(8,128)(2,1)S(1)}, bf16[64,1792]{1,0:T(8,128)(2,1)S(1)}, u32[]{:S(2)}, u32[]{:S(2)}) collective-permute-start(bf16[64,1792]{1,0:T(8,128)(2,1)S(1)} %collective-permute-done.5.refs_2_), channel_id=1, source_target_pairs={{0,4},{4,0},{8,12},{12,8},{1,5},{5,1},{9,13},{13,9},{2,6},{6,2},{1... | collective-permute-start | bytes 688136 | tf_op jit(solution)/shard_map/ppermute | solution.py:27
  23.1 14.3 %collective-permute-start.4 = (bf16[64,1792]{1,0:T(8,128)(2,1)S(1)}, bf16[64,1792]{1,0:T(8,128)(2,1)S(1)}, u32[]{:S(2)}, u32[]{:S(2)}) collective-permute-start(bf16[64,1792]{1,0:T(8,128)(2,1)S(1)} %collective-permute-done.3.refs_2_), channel_id=1, source_target_pairs={{0,4},{4,0},{8,12},{12,8},{1,5},{5,1},{9,13},{13,9},{2,6},{6,2},{1... | collective-permute-start | bytes 688136 | tf_op jit(solution)/shard_map/ppermute | solution.py:27
  28.3 12.9 %collective-permute-start.9 = (bf16[64,128]{1,0:T(8,128)(2,1)S(1)}, bf16[64,128]{1,0:T(8,128)(2,1)S(1)}, u32[]{:S(2)}, u32[]{:S(2)}) collective-permute-start(bf16[64,128]{1,0:T(8,128)(2,1)S(1)} %fusion.7.refs_7_), channel_id=1, source_target_pairs={{0,4},{4,0},{8,12},{12,8},{1,5},{5,1},{9,13},{13,9},{2,6},{6,2},{1... | collective-permute-start | bytes 49160 | tf_op jit(solution)/shard_map/ppermute | solution.py:27
  28.3 12.9 %collective-permute-start.11 = (bf16[64,128]{1,0:T(8,128)(2,1)S(1)}, bf16[64,128]{1,0:T(8,128)(2,1)S(1)}, u32[]{:S(2)}, u32[]{:S(2)}) collective-permute-start(bf16[64,128]{1,0:T(8,128)(2,1)S(1)} %collective-permute-done.10.refs_9_), channel_id=1, source_target_pairs={{0,4},{4,0},{8,12},{12,8},{1,5},{5,1},{9,13},{13,9},{2,6},{6,2},{1... | collective-permute-start | bytes 49160 | tf_op jit(solution)/shard_map/ppermute | solution.py:27
  28.8 12.4 %collective-permute-start.2 = (bf16[64,1792]{1,0:T(8,128)(2,1)S(1)}, bf16[64,1792]{1,0:T(8,128)(2,1)S(1)}, u32[]{:S(2)}, u32[]{:S(2)}) collective-permute-start(bf16[64,1792]{1,0:T(8,128)(2,1)S(1)} %collective-permute-done.1.refs_3_), channel_id=1, source_target_pairs={{0,4},{4,0},{8,12},{12,8},{1,5},{5,1},{9,13},{13,9},{2,6},{6,2},{1... | collective-permute-start | bytes 688136 | tf_op jit(solution)/shard_map/ppermute | solution.py:27
  28.9 1.2 %copy-start = (bf16[64,7168]{1,0:T(8,128)(2,1)S(1)}, bf16[64,7168]{1,0:T(8,128)(2,1)}, u32[]{:S(2)}) copy-start(bf16[64,7168]{1,0:T(8,128)(2,1)} %refs_1_.1) | copy-start | bytes 2752516
  33.6 11.3 %slice-start = ((s8[7340032]{0:T(1024)(128)(4,1)}), s8[4194304]{0:T(1024)(128)(4,1)S(1)}, s32[]{:S(2)}) async-start(s8[7340032]{0:T(1024)(128)(4,1)} %bitcast.20), calls=%async_computation | async-start | bytes 8388608
  37.4 7.5 %slice-start.1 = ((s8[7340032]{0:T(1024)(128)(4,1)}), s8[3145728]{0:T(1024)(128)(4,1)S(1)}, s32[]{:S(2)}) async-start(s8[7340032]{0:T(1024)(128)(4,1)} %bitcast.20), calls=%async_computation.1 | async-start | bytes 6291456
  45.4 4.9 %collective-permute-start.12 = (bf16[128,1024]{1,0:T(8,128)(2,1)S(1)}, bf16[128,1024]{1,0:T(8,128)(2,1)S(1)}, u32[]{:S(2)}, u32[]{:S(2)}) collective-permute-start(bf16[128,1024]{1,0:T(8,128)(2,1)S(1)} %get-tuple-element.16), channel_id=1, source_target_pairs={{0,4},{4,0},{8,12},{12,8},{1,5},{5,1},{9,13},{13,9},{2,6},{6,2},{1... | collective-permute-start | bytes 786440 | tf_op jit(solution)/shard_map/ppermute | solution.py:27
  46.3 5.6 %collective-permute-start.24 = (bf16[128,1024]{1,0:T(8,128)(2,1)S(1)}, bf16[128,1024]{1,0:T(8,128)(2,1)S(1)}, u32[]{:S(2)}, u32[]{:S(2)}) collective-permute-start(bf16[128,1024]{1,0:T(8,128)(2,1)S(1)} %get-tuple-element.22), channel_id=1, source_target_pairs={{0,4},{4,0},{8,12},{12,8},{1,5},{5,1},{9,13},{13,9},{2,6},{6,2},{1... | collective-permute-start | bytes 786440 | tf_op jit(solution)/shard_map/ppermute | solution.py:27
  48.7 20.3 %collective-permute-start.16 = (bf16[128,2048]{1,0:T(8,128)(2,1)S(1)}, bf16[128,2048]{1,0:T(8,128)(2,1)S(1)}, u32[]{:S(2)}, u32[]{:S(2)}) collective-permute-start(bf16[128,2048]{1,0:T(8,128)(2,1)S(1)} %get-tuple-element.18), channel_id=1, source_target_pairs={{0,4},{4,0},{8,12},{12,8},{1,5},{5,1},{9,13},{13,9},{2,6},{6,2},{1... | collective-permute-start | bytes 1572872 | tf_op jit(solution)/shard_map/ppermute | solution.py:27
  49.2 21.4 %collective-permute-start.20 = (bf16[128,2048]{1,0:T(8,128)(2,1)S(1)}, bf16[128,2048]{1,0:T(8,128)(2,1)S(1)}, u32[]{:S(2)}, u32[]{:S(2)}) collective-permute-start(bf16[128,2048]{1,0:T(8,128)(2,1)S(1)} %get-tuple-element.20), channel_id=1, source_target_pairs={{0,4},{4,0},{8,12},{12,8},{1,5},{5,1},{9,13},{13,9},{2,6},{6,2},{1... | collective-permute-start | bytes 1572872 | tf_op jit(solution)/shard_map/ppermute | solution.py:27
  49.7 2.7 %collective-permute-start.28 = (bf16[128,1024]{1,0:T(8,128)(2,1)S(1)}, bf16[128,1024]{1,0:T(8,128)(2,1)S(1)}, u32[]{:S(2)}, u32[]{:S(2)}) collective-permute-start(bf16[128,1024]{1,0:T(8,128)(2,1)S(1)} %get-tuple-element.24), channel_id=1, source_target_pairs={{0,4},{4,0},{8,12},{12,8},{1,5},{5,1},{9,13},{13,9},{2,6},{6,2},{1... | collective-permute-start | bytes 786440 | tf_op jit(solution)/shard_map/ppermute | solution.py:27
  50.3 6.4 %collective-permute-start.13 = (bf16[64,1024]{1,0:T(8,128)(2,1)S(1)}, bf16[64,1024]{1,0:T(8,128)(2,1)S(1)}, u32[]{:S(2)}, u32[]{:S(2)}) collective-permute-start(bf16[64,1024]{1,0:T(8,128)(2,1)S(1)} %add_convert_fusion.6), channel_id=1, source_target_pairs={{0,8},{4,12},{8,0},{12,4},{1,9},{5,13},{9,1},{13,5},{2,10},{6,14},... | collective-permute-start | bytes 393224 | tf_op jit(solution)/shard_map/ppermute | solution.py:27
  52.0 7.5 %collective-permute-start.25 = (bf16[64,1024]{1,0:T(8,128)(2,1)S(1)}, bf16[64,1024]{1,0:T(8,128)(2,1)S(1)}, u32[]{:S(2)}, u32[]{:S(2)}) collective-permute-start(bf16[64,1024]{1,0:T(8,128)(2,1)S(1)} %add_convert_fusion.3), channel_id=1, source_target_pairs={{0,8},{4,12},{8,0},{12,4},{1,9},{5,13},{9,1},{13,5},{2,10},{6,14},... | collective-permute-start | bytes 393224 | tf_op jit(solution)/shard_map/ppermute | solution.py:27
  52.5 8.9 %collective-permute-start.29 = (bf16[64,1024]{1,0:T(8,128)(2,1)S(1)}, bf16[64,1024]{1,0:T(8,128)(2,1)S(1)}, u32[]{:S(2)}, u32[]{:S(2)}) collective-permute-start(bf16[64,1024]{1,0:T(8,128)(2,1)S(1)} %add_convert_fusion.2), channel_id=1, source_target_pairs={{0,8},{4,12},{8,0},{12,4},{1,9},{5,13},{9,1},{13,5},{2,10},{6,14},... | collective-permute-start | bytes 393224 | tf_op jit(solution)/shard_map/ppermute | solution.py:27
  56.7 6.4 %collective-permute-start.14 = (bf16[32,1024]{1,0:T(8,128)(2,1)S(1)}, bf16[32,1024]{1,0:T(8,128)(2,1)S(1)}, u32[]{:S(2)}, u32[]{:S(2)}) collective-permute-start(bf16[32,1024]{1,0:T(8,128)(2,1)S(1)} %add_convert_fusion.13), channel_id=1, source_target_pairs={{0,1},{1,0},{2,3},{3,2},{4,5},{5,4},{6,7},{7,6},{8,9},{9,8},{10,11... | collective-permute-start | bytes 196616 | tf_op jit(solution)/shard_map/ppermute | solution.py:27
  59.5 6.3 %collective-permute-start.26 = (bf16[32,1024]{1,0:T(8,128)(2,1)S(1)}, bf16[32,1024]{1,0:T(8,128)(2,1)S(1)}, u32[]{:S(2)}, u32[]{:S(2)}) collective-permute-start(bf16[32,1024]{1,0:T(8,128)(2,1)S(1)} %add_convert_fusion.8), channel_id=1, source_target_pairs={{0,1},{1,0},{2,3},{3,2},{4,5},{5,4},{6,7},{7,6},{8,9},{9,8},{10,11... | collective-permute-start | bytes 196616 | tf_op jit(solution)/shard_map/ppermute | solution.py:27
  61.5 5.6 %collective-permute-start.30 = (bf16[32,1024]{1,0:T(8,128)(2,1)S(1)}, bf16[32,1024]{1,0:T(8,128)(2,1)S(1)}, u32[]{:S(2)}, u32[]{:S(2)}) collective-permute-start(bf16[32,1024]{1,0:T(8,128)(2,1)S(1)} %add_convert_fusion.7), channel_id=1, source_target_pairs={{0,1},{1,0},{2,3},{3,2},{4,5},{5,4},{6,7},{7,6},{8,9},{9,8},{10,11... | collective-permute-start | bytes 196616 | tf_op jit(solution)/shard_map/ppermute | solution.py:27
  63.2 5.8 %collective-permute-start.15 = (bf16[16,1024]{1,0:T(8,128)(2,1)S(1)}, bf16[16,1024]{1,0:T(8,128)(2,1)S(1)}, u32[]{:S(2)}, u32[]{:S(2)}) collective-permute-start(bf16[16,1024]{1,0:T(8,128)(2,1)S(1)} %add_convert_fusion.19), channel_id=1, source_target_pairs={{0,2},{1,3},{2,0},{3,1},{4,6},{5,7},{6,4},{7,5},{8,10},{9,11},{10,... | collective-permute-start | bytes 98312 | tf_op jit(solution)/shard_map/ppermute | solution.py:27
  65.8 25.6 %collective-permute-start.27 = (bf16[16,1024]{1,0:T(8,128)(2,1)S(1)}, bf16[16,1024]{1,0:T(8,128)(2,1)S(1)}, u32[]{:S(2)}, u32[]{:S(2)}) collective-permute-start(bf16[16,1024]{1,0:T(8,128)(2,1)S(1)} %add_convert_fusion.17), channel_id=1, source_target_pairs={{0,2},{1,3},{2,0},{3,1},{4,6},{5,7},{6,4},{7,5},{8,10},{9,11},{10,... | collective-permute-start | bytes 98312 | tf_op jit(solution)/shard_map/ppermute | solution.py:27
  67.1 24.4 %collective-permute-start.31 = (bf16[16,1024]{1,0:T(8,128)(2,1)S(1)}, bf16[16,1024]{1,0:T(8,128)(2,1)S(1)}, u32[]{:S(2)}, u32[]{:S(2)}) collective-permute-start(bf16[16,1024]{1,0:T(8,128)(2,1)S(1)} %add_convert_fusion.15), channel_id=1, source_target_pairs={{0,2},{1,3},{2,0},{3,1},{4,6},{5,7},{6,4},{7,5},{8,10},{9,11},{10,... | collective-permute-start | bytes 98312 | tf_op jit(solution)/shard_map/ppermute | solution.py:27
  69.0 9.2 %collective-permute-start.17 = (bf16[64,2048]{1,0:T(8,128)(2,1)S(1)}, bf16[64,2048]{1,0:T(8,128)(2,1)S(1)}, u32[]{:S(2)}, u32[]{:S(2)}) collective-permute-start(bf16[64,2048]{1,0:T(8,128)(2,1)S(1)} %add_convert_fusion.1), channel_id=1, source_target_pairs={{0,8},{4,12},{8,0},{12,4},{1,9},{5,13},{9,1},{13,5},{2,10},{6,14},... | collective-permute-start | bytes 786440 | tf_op jit(solution)/shard_map/ppermute | solution.py:27
  70.7 10.4 %collective-permute-start.21 = (bf16[64,2048]{1,0:T(8,128)(2,1)S(1)}, bf16[64,2048]{1,0:T(8,128)(2,1)S(1)}, u32[]{:S(2)}, u32[]{:S(2)}) collective-permute-start(bf16[64,2048]{1,0:T(8,128)(2,1)S(1)} %add_convert_fusion), channel_id=1, source_target_pairs={{0,8},{4,12},{8,0},{12,4},{1,9},{5,13},{9,1},{13,5},{2,10},{6,14},... | collective-permute-start | bytes 786440 | tf_op jit(solution)/shard_map/ppermute | solution.py:27
  78.3 6.2 %collective-permute-start.18 = (bf16[32,2048]{1,0:T(8,128)(2,1)S(1)}, bf16[32,2048]{1,0:T(8,128)(2,1)S(1)}, u32[]{:S(2)}, u32[]{:S(2)}) collective-permute-start(bf16[32,2048]{1,0:T(8,128)(2,1)S(1)} %add_convert_fusion.5), channel_id=1, source_target_pairs={{0,1},{1,0},{2,3},{3,2},{4,5},{5,4},{6,7},{7,6},{8,9},{9,8},{10,11... | collective-permute-start | bytes 393224 | tf_op jit(solution)/shard_map/ppermute | solution.py:27
  81.1 5.0 %collective-permute-start.22 = (bf16[32,2048]{1,0:T(8,128)(2,1)S(1)}, bf16[32,2048]{1,0:T(8,128)(2,1)S(1)}, u32[]{:S(2)}, u32[]{:S(2)}) collective-permute-start(bf16[32,2048]{1,0:T(8,128)(2,1)S(1)} %add_convert_fusion.4), channel_id=1, source_target_pairs={{0,1},{1,0},{2,3},{3,2},{4,5},{5,4},{6,7},{7,6},{8,9},{9,8},{10,11... | collective-permute-start | bytes 393224 | tf_op jit(solution)/shard_map/ppermute | solution.py:27
  84.5 5.2 %collective-permute-start.19 = (bf16[16,2048]{1,0:T(8,128)(2,1)S(1)}, bf16[16,2048]{1,0:T(8,128)(2,1)S(1)}, u32[]{:S(2)}, u32[]{:S(2)}) collective-permute-start(bf16[16,2048]{1,0:T(8,128)(2,1)S(1)} %add_convert_fusion.12), channel_id=1, source_target_pairs={{0,2},{1,3},{2,0},{3,1},{4,6},{5,7},{6,4},{7,5},{8,10},{9,11},{10,... | collective-permute-start | bytes 196616 | tf_op jit(solution)/shard_map/ppermute | solution.py:27
  86.2 5.2 %collective-permute-start.23 = (bf16[16,2048]{1,0:T(8,128)(2,1)S(1)}, bf16[16,2048]{1,0:T(8,128)(2,1)S(1)}, u32[]{:S(2)}, u32[]{:S(2)}) collective-permute-start(bf16[16,2048]{1,0:T(8,128)(2,1)S(1)} %add_convert_fusion.10), channel_id=1, source_target_pairs={{0,2},{1,3},{2,0},{3,1},{4,6},{5,7},{6,4},{7,5},{8,10},{9,11},{10,... | collective-permute-start | bytes 196616 | tf_op jit(solution)/shard_map/ppermute | solution.py:27
  91.5 0.7 copy-start.1

commit v2 on v0

v2 whole, which is shorter than its diff:
```python
import jax
import jax.numpy as jnp
from jax import lax
from jax.experimental import pallas as pl
from jax.experimental.pallas import tpu as pltpu
from jax.sharding import PartitionSpec as P

F32 = jnp.float32
BF16 = jnp.bfloat16
LANES = 128
VMEM_LIMIT = 16 << 20
RUN = 4
FRONT = 4
CHUNKS = [(1, ("zy", "yz"))]
DOWN_SHARES = [1, 1]


def bits_of(count):
    bits = count.bit_length() - 1
    assert 1 << bits == count
    return bits


def bit_reverse(value, bits):
    return sum(((value >> b) & 1) << (bits - 1 - b) for b in range(bits))


def exchange(x, axis, mask):
    return lax.ppermute(x, axis, [(i, i ^ mask) for i in range(lax.axis_size(axis))])


def add(*terms):
    return sum(t.astype(F32) for t in terms).astype(BF16)


def split(total, unit, shares):
    edges, whole = [0], total // unit
    for i in range(len(shares)):
        edges.append(round(whole * sum(shares[: i + 1]) / sum(shares)) * unit)
    return [(a, b - a) for a, b in zip(edges, edges[1:]) if b > a]


def after(x, *earlier):
    return lax.optimization_barrier((x, earlier))[0]


def prepare(tokens, group_ids, gates, relayed):
    rows, top = group_ids.shape
    direct = tokens.shape[1] - 2 * relayed

    def body(tokens_ref, ids_ref, gates_ref, first, second, table_ref, ids, weights, sems):
        start = pl.multiple_of((lax.axis_index("exp") % 2) * relayed, LANES)
        moves = [
            (ids_ref, ids),
            (gates_ref, weights),
            (tokens_ref.at[:, pl.ds(start, relayed)], first),
            (tokens_ref.at[:, pl.ds(2 * relayed, direct)], second.at[:, pl.ds(0, direct)]),
        ]
        copies = [pltpu.make_async_copy(*move, sems.at[i]) for i, move in enumerate(moves)]
        for copy in copies:
            copy.start()
        for copy in copies[:2]:
            copy.wait()
        expert = lax.broadcasted_iota(jnp.int32, (LANES, rows), 0)
        table = jnp.zeros((LANES, rows), F32)
        for k in range(top):
            even = weights[pl.ds(2 * k, 1), :].astype(F32)
            odd = weights[pl.ds(2 * k + 1, 1), :].astype(F32)
            gate = jnp.where(expert % 2 == 0, even, odd)
            table = jnp.where(expert // 2 == ids[pl.ds(k, 1), :], gate, table)
        table = table.T.astype(BF16)
        table_ref[...] = table
        second[:, pl.ds(direct, LANES)] = table
        for copy in copies[2:]:
            copy.wait()

    widths = [relayed, direct + LANES, LANES]
    return pl.pallas_call(
        body,
        in_specs=[whole(pl.ANY)] * 3,
        out_specs=[whole()] * 3,
        out_shape=[jax.ShapeDtypeStruct((rows, width), BF16) for width in widths],
        scratch_shapes=[
            pltpu.VMEM((top, rows), jnp.int32),
            pltpu.VMEM((2 * top, rows), BF16),
            pltpu.SemaphoreType.DMA((4,)),
        ],
        compiler_params=pltpu.CompilerParams(vmem_limit_bytes=VMEM_LIMIT),
        name="prepare",
    )(in_hbm(tokens), in_hbm(group_ids.T), in_hbm(gates.T))


def in_hbm(x):
    return pltpu.with_memory_space_constraint(x, pltpu.HBM)


def whole(memory_space=pltpu.VMEM):
    return pl.BlockSpec(memory_space=memory_space)


def near_step(xs, w_view, before, hidden, depth, first, last):
    rows, ratio = xs[0].shape[0], 2 * hidden // LANES
    halves, steps = hidden // LANES, last - first

    def body(*refs):
        x_refs, refs = refs[: len(xs)], list(refs[len(xs) :])
        w_ref = refs.pop(0)
        before_ref = None if before is None else refs.pop(0)
        clean_ref, acc_ref, held, blocks, wide, sems = refs
        own = [
            pltpu.make_async_copy(
                ref.at[:, pl.ds(first * depth, steps * depth)],
                held.at[pl.ds(i * rows, rows), :],
                sems.at[2 + i],
            )
            for i, ref in enumerate(x_refs)
        ]

        def fetch(step):
            return pltpu.make_async_copy(
                w_ref.at[:, pl.ds((first + step) * depth * ratio, depth * ratio), :],
                blocks.at[step % 2],
                sems.at[step % 2],
            )

        fetch(0).start()
        for copy in own:
            copy.start()
        for step in range(steps):
            if step + 1 < steps:
                fetch(step + 1).start()
            fetch(step).wait()
            at = step * depth
            for member in range(2):
                wide[...] = blocks[step % 2, member].astype(F32)
                for s in range(2):
                    for t in range(halves):
                        column = (2 * member + s) * hidden + t * LANES
                        clean_ref[pl.ds(at, depth), pl.ds(column, LANES)] = wide[
                            pl.ds(2 * t + s, depth, stride=2 * halves), :
                        ].astype(BF16)
            if step == 0:
                for copy in own:
                    copy.wait()
            value = jnp.dot(
                held[:, pl.ds(at, depth)],
                clean_ref[pl.ds(at, depth), :],
                preferred_element_type=F32,
            )
            if step or before is not None:
                value += (acc_ref if step else before_ref)[...]
            acc_ref[...] = value

    operands = [in_hbm(x) for x in (*xs, w_view)] + ([] if before is None else [before])
    return pl.pallas_call(
        body,
        in_specs=[whole(pl.ANY)] * (len(xs) + 1) + [whole()] * (len(operands) - len(xs) - 1),
        out_specs=[whole(), whole()],
        out_shape=[
            jax.ShapeDtypeStruct((steps * depth, 4 * hidden), BF16),
            jax.ShapeDtypeStruct((len(xs) * rows, 4 * hidden), F32),
        ],
        scratch_shapes=[
            pltpu.VMEM((len(xs) * rows, steps * depth), BF16),
            pltpu.VMEM((2, 2, depth * ratio, LANES), BF16),
            pltpu.VMEM((depth * ratio, LANES), F32),
            pltpu.SemaphoreType.DMA((2 + len(xs),)),
        ],
        compiler_params=pltpu.CompilerParams(vmem_limit_bytes=VMEM_LIMIT),
        name="near",
    )(*operands)


def far_step(before, blocks, parts):
    rows = blocks[0][0].shape[0]
    count = len(blocks[0])
    cleans = []
    for part in parts:
        if not any(part[2] is c for c in cleans):
            cleans.append(part[2])

    def body(*refs):
        refs, out_ref = list(refs[:-1]), refs[-1]
        value = None if before is None else refs.pop(0)[...]
        clean_refs, refs = refs[: len(cleans)], refs[len(cleans) :]
        for which, column, clean, start, depth, shift in parts:
            clean_ref = clean_refs[[c is clean for c in cleans].index(True)]
            x_refs = refs[which * count : (which + 1) * count]
            if shift:
                start = pl.multiple_of(start + (lax.axis_index("exp") % 2) * shift, LANES)
            x = jnp.concatenate([ref[:, pl.ds(column, depth)] for ref in x_refs], axis=0)
            term = jnp.dot(x, clean_ref[pl.ds(start, depth), :], preferred_element_type=F32)
            value = term if value is None else value + term
        out_ref[...] = value

    operands = ([] if before is None else [before]) + cleans + [x for xs in blocks for x in xs]
    return pl.pallas_call(
        body,
        in_specs=[whole()] * len(operands),
        out_specs=whole(),
        out_shape=jax.ShapeDtypeStruct((count * rows, cleans[0].shape[1]), F32),
        compiler_params=pltpu.CompilerParams(vmem_limit_bytes=VMEM_LIMIT),
        name="far",
    )(*operands)


def activate(acc, tables_ref, hidden):
    rows, group = tables_ref[0].shape[0], lax.axis_index("grp")
    lane = lax.broadcasted_iota(jnp.int32, (rows, LANES), 1)
    blocks = []
    for block, table_ref in enumerate(tables_ref):
        table = table_ref[...].astype(F32)
        members = []
        for member in range(2):
            chosen = jnp.where(lane == 2 * group + member, table, 0.0)
            gate = jnp.sum(chosen, axis=1, keepdims=True)
            both = acc[pl.ds(block * rows, rows), pl.ds(2 * member * hidden, 2 * hidden)]
            a, b = both[:, :hidden], both[:, hidden:]
            members.append(gate * (jax.nn.silu(a) * b))
        blocks.append(jnp.concatenate(members, axis=1))
    return jnp.concatenate(blocks, axis=0)


def table_specs(tables):
    return [
        pl.BlockSpec((t.shape[0], LANES), lambda i, c=t.shape[1] // LANES - 1: (0, c))
        for t in tables
    ]


def near_gated(acc, tables, hidden):
    def body(acc_ref, *refs):
        refs[-1][...] = activate(acc_ref, refs[:-1], hidden)

    return pl.pallas_call(
        body,
        grid=(1,),
        in_specs=[whole()] + table_specs(tables),
        out_specs=whole(),
        out_shape=jax.ShapeDtypeStruct((acc.shape[0], 2 * hidden), F32),
        compiler_params=pltpu.CompilerParams(vmem_limit_bytes=VMEM_LIMIT),
        name="near_gated",
    )(acc, *tables)


def far_gated(near_rows, acc, tables, hidden, plans, order):
    rows, count = tables[0].shape[0], near_rows.shape[0]
    total = count + acc.shape[0]
    parts = 1 << sum(axis == "exp" for axis, _ in plans[0][0])
    part, bits = rows // parts, len(plans[0][0])
    at_of = {r: i for i, r in enumerate(order)}

    def body(near_ref, acc_ref, *refs):
        outs, work = refs[len(tables) : -1], refs[-1]
        work[pl.ds(0, count), :] = near_ref[...]
        work[pl.ds(count, total - count), :] = activate(acc_ref, refs[: len(tables)], hidden)
        core, slot = lax.axis_index("grp") % 2, lax.axis_index("exp")
        for routes, out_ref in zip(plans, outs):
            for other in range(2):
                owner = (core + other) % 2
                pieces = []
                for p in range(1 << bits):
                    starts = []
                    for stages in routes:
                        rel = {"grp": other, "exp": 0}
                        for k, (axis, bit) in enumerate(stages):
                            rel[axis] |= ((p >> (bits - 1 - k)) & 1) << bit
                        place = jnp.bitwise_xor(slot, rel["exp"]) * part
                        starts.append(at_of[rel["grp"]] * rows + place)
                    start = jnp.where(owner == 0, *starts)
                    pieces.append(work[pl.ds(pl.multiple_of(start, part), part), :])
                out_ref[pl.ds(other * (total // 2), total // 2), :] = jnp.concatenate(
                    pieces, axis=0
                ).astype(BF16)

    return pl.pallas_call(
        body,
        grid=(1,),
        in_specs=[whole(), whole()] + table_specs(tables),
        out_specs=[whole() for _ in plans],
        out_shape=[jax.ShapeDtypeStruct((total, 2 * hidden), BF16) for _ in plans],
        scratch_shapes=[pltpu.VMEM((total, 2 * hidden), F32)],
        compiler_params=pltpu.CompilerParams(vmem_limit_bytes=VMEM_LIMIT),
        name="far_gated",
    )(near_rows, acc, *tables)


def load(x):
    def body(x_ref, out_ref, sem):
        copy = pltpu.make_async_copy(x_ref, out_ref, sem)
        copy.start()
        copy.wait()

    return pl.pallas_call(
        body,
        in_specs=[whole(pl.ANY)],
        out_specs=whole(),
        out_shape=jax.ShapeDtypeStruct(x.shape, x.dtype),
        scratch_shapes=[pltpu.SemaphoreType.DMA(())],
        compiler_params=pltpu.CompilerParams(vmem_limit_bytes=VMEM_LIMIT),
        name="load",
    )(in_hbm(x))


def down_step(hidden_rows, w_flat, first, count, start, width):
    def body(h_ref, w_ref, out_ref):
        out_ref[...] = jnp.dot(
            h_ref[pl.ds(first, count), :],
            w_ref[:, pl.ds(start, width)],
            preferred_element_type=F32,
        ).astype(BF16)

    return pl.pallas_call(
        body,
        in_specs=[whole(), whole()],
        out_specs=whole(),
        out_shape=jax.ShapeDtypeStruct((count, width), BF16),
        compiler_params=pltpu.CompilerParams(vmem_limit_bytes=VMEM_LIMIT),
        name="down",
    )(hidden_rows, w_flat)


def local(tokens, group_ids, gates, w_in, w_down):
    groups, parts = lax.axis_size("grp"), lax.axis_size("exp")
    rows, features = tokens.shape
    hidden = w_in.shape[3]
    group_bits, part_bits = bits_of(groups), bits_of(parts)
    w_view = (
        w_in.reshape(2, features, 2, hidden // LANES, LANES)
        .transpose(0, 1, 3, 2, 4)
        .reshape(2, -1, LANES)
    )
    w_flat = w_down.reshape(2 * hidden, features)
    unit = features // 7

    def far(x):
        held = {0: x}
        for bit in reversed(range(1, group_bits)):
            for r in list(held):
                held[r | 1 << bit] = exchange(held[r], "grp", 1 << bit)
        return [held[r] for r in range(2, groups, 2)]

    def both(held):
        return held + [exchange(x, "grp", 1) for x in held]

    def both(held):
        return held + [exchange(x, "grp", 1) for x in held]

    run, steps = features // 14 * RUN, features // unit
    beside = exchange(tokens, "grp", 1)
    relayed, direct, table = prepare(tokens, group_ids, gates, run)
    relayed = far(relayed)
    table_beside = exchange(table, "grp", 1)
    clean_front, near_acc = near_step(
        [tokens, beside], w_view, None, hidden, unit, 0, FRONT
    )
    direct = far(after(direct, near_acc))
    relayed, near_acc = lax.optimization_barrier((relayed, near_acc))
    passed = [exchange(x, "exp", 1) for x in relayed]
    clean_back, near_acc = near_step(
        [tokens, beside], w_view, near_acc, hidden, unit, FRONT, steps
    )
    near_rows = near_gated(near_acc, [table, table_beside], hidden)
    far_acc = far_step(None, [both(relayed)], [(0, 0, clean_front, 0, run, run)])
    w_flat = load(after(w_flat, near_rows))
    direct, passed, far_acc, w_flat = lax.optimization_barrier((direct, passed, far_acc, w_flat))
    direct, passed = both(direct), both(passed)
    middle = FRONT * unit - 2 * run
    pieces = [
        (0, 0, clean_front, 2 * run, middle, 0),
        (0, middle, clean_back, 0, features - FRONT * unit, 0),
        (1, 0, clean_front, run, run, -run),
    ]
    pieces = [piece for piece in pieces if piece[4]]
    far_acc = far_step(far_acc, [direct, passed], pieces)

    grp_stages = [("grp", b) for b in range(1, group_bits)]
    exp_stages = [("exp", b) for b in range(part_bits)]
    by_name = {"zy": exp_stages + grp_stages, "yz": grp_stages + exp_stages}
    plans = [[by_name[name] for name in names] for _, names in CHUNKS]
    order = [0, 1] + list(range(2, groups, 2)) + list(range(3, groups, 2))
    all_rows = far_gated(near_rows, far_acc, direct, hidden, plans, order)

    def turn(x, routes, stage):
        pairs = []
        for g in range(groups):
            for e in range(parts):
                axis, bit = routes[g % 2][stage]
                to_g, to_e = (g ^ 1 << bit, e) if axis == "grp" else (g, e ^ 1 << bit)
                pairs.append((g * parts + e, to_g * parts + to_e))
        return lax.ppermute(x, ("grp", "exp"), pairs)

    state = []
    half = rows * groups // 2
    spans = split(features, features // 28, [share for share, _ in CHUNKS])
    for (start, width), plan_rows in zip(spans, all_rows):
        comes = []
        for offset, piece in split(width, features // 56, DOWN_SHARES):
            send = down_step(plan_rows, w_flat, half, half, start + offset, piece)
            plan_rows = after(plan_rows, send)
            comes.append(exchange(send, "grp", 1))
        keep = down_step(plan_rows, w_flat, 0, half, start, width)
        state.append([keep, jnp.concatenate(comes, axis=1)])
    token = None
    height = rows * groups // 2
    for stage in range(len(grp_stages + exp_stages)):
        height //= 2
        for terms, routes in zip(state, plans):
            back = turn(add(*[t[height : 2 * height] for t in terms]), routes, stage)
            if token is not None:
                back = after(back, token)
            terms.append(back)
            token = back
    return jnp.concatenate([add(*[t[:height] for t in terms]) for terms in state], axis=1)


def solution(mesh):
    in_specs = (
        P(("rep", "grp"), None),
        P(("rep", "grp"), None),
        P(("rep", "grp"), None),
        P("grp", None, None, "exp"),
        P("grp", "exp", None),
    )
    out_specs = P(("rep", "grp", "exp"), None)
    return jax.shard_map(local, mesh=mesh, in_specs=in_specs, out_specs=out_specs, check_vma=False)
```

time: 137 us -> 70.6 us (0.52)
  blocking collectives: 35.2 us -> 0 us
  local copies, waits for them, and re-layouts: 25.6 us -> 1.09 us
  Pallas kernels: 0 us -> 20.9 us
  matrix products: 16.1 us -> 0 us
  between operations: 13.5 us -> 0.16 us
  starting transfers between devices: 8.85 us -> 11.8 us
    all_to_all x1 -> x0, blocking collectives: 35.2 us -> none  [local(): lax.all_to_all(parts, 'grp', split_axis=0, concat_axis=0, tiled=True)]
    ppermute x0 -> x13, waiting for transfers between devices: none -> 35 us  [the longest x3 32.3 us: turn(): return lax.ppermute(x, ('grp', 'exp'), pairs)]
    reduce_scatter x1 -> x0, waiting for transfers between devices: 26 us -> none  [local(): lax.psum_scatter(local_sum.astype(jnp.bfloat16), 'exp', scatter_dimension...]
    pallas_call x0 -> x11, Pallas kernels: none -> 20.9 us  [the longest x2 11.4 us: near_step(): pl.pallas_call(body, in_specs=[whole(pl.ANY)] * (len(xs) + 1) + [whole()]...]
    dot_general x8 -> x0, matrix products: 16.1 us -> none  [the longest x2 9.26 us: run_experts(): jnp.dot(rows, w_in[member].reshape(feature_width, 2 * hidden_dev), prefer...]
    slice x1 -> x0, local copies, waits for them, and re-layouts: 12.4 us -> none  [run_experts(): w_in[member].reshape(feature_width, 2 * hidden_dev)]
    ppermute x0 -> x13, starting transfers between devices: none -> 11.8 us  [the longest x10 7.59 us: exchange(): lax.ppermute(x, axis, [(i, i ^ mask) for i in range(lax.axis_size(axis))])]
    unnamed x12 -> x3, local copies, waits for them, and re-layouts: 11.9 us -> 1 us
  transfers between devices with their start and end apart: 3 -> 13, of which waited for: 3 -> 5; matrix products, arithmetic and copies ran while one was open for 19% -> 0% of each run, Pallas kernels for 0% -> 26%
where the time goes in v2:
time: 70.6 us; the launch traced here: 70.3 us
  waiting for transfers between devices  35 us (50%)
  Pallas kernels  20.9 us (30%)
  starting transfers between devices  11.8 us (17%)
  other arithmetic  1.34 us (2%)
  local copies, waits for them, and re-layouts  1.09 us (2%)
    ppermute x3, waiting for transfers between devices, turn(): return lax.ppermute(x, ('grp', 'exp'), pairs)  32.3 us
    pallas_call x2, Pallas kernels, near_step(): pl.pallas_call(body, in_specs=[whole(pl.ANY)] * (len(xs) + 1) + [whole()]...  11.4 us
    ppermute x10, starting transfers between devices, exchange(): lax.ppermute(x, axis, [(i, i ^ mask) for i in range(lax.axis_size(axis))])  7.59 us
    ppermute x3, starting transfers between devices, turn(): return lax.ppermute(x, ('grp', 'exp'), pairs)  4.22 us
    pallas_call x1, Pallas kernels, load(): pl.pallas_call(body, in_specs=[whole(pl.ANY)], out_specs=whole(), out_sha...  3.09 us
    ppermute x10, waiting for transfers between devices, exchange(): lax.ppermute(x, axis, [(i, i ^ mask) for i in range(lax.axis_size(axis))])  2.72 us
    pallas_call x3, Pallas kernels, down_step(): pl.pallas_call(body, in_specs=[whole(), whole()], out_specs=whole(), out_...  2.71 us
    pallas_call x2, Pallas kernels, far_step(): pl.pallas_call(body, in_specs=[whole()] * len(operands), out_specs=whole(...  2.27 us
  transfers between devices with their start and end apart: 13, of which 5 were waited for; matrix products, arithmetic and copies ran while one was open for 0% of the time, Pallas kernels for 26%

profile of v2, /device:TPU:0, one launch (start us, length us, event | category | flops | bytes accessed | tf_op | source)
XLA Modules:
  0.0 70.3 jit_solution(2274813682647637999)
XLA Ops:
  0.0 0.5 collective-permute-start
  0.5 1.1 %prepare.1 = (bf16[64,2048]{1,0:T(8,128)(2,1)S(1)}, bf16[64,3200]{1,0:T(8,128)(2,1)S(1)}, bf16[64,128]{1,0:T(8,128)(2,1)S(1)}) custom-call(bf16[64,7168]{1,0:T(8,128)(2,1)} %refs_0_.3, s32[2,64]{1,0:T(2,128)} %bitcast.11, bf16[4,64]{1,0:T(4,128)(2,1)} %bitcast.12), custom_call_target="tpu_custom_call" | custom-call | tf_op jit(solution)/shard_map/prepare/pallas_call | solution.py:78
  1.6 2.6 %collective-permute-start.1 = (bf16[64,2048]{1,0:T(8,128)(2,1)S(1)}, bf16[64,2048]{1,0:T(8,128)(2,1)S(1)}, u32[]{:S(2)}, u32[]{:S(2)}) collective-permute-start(bf16[64,2048]{1,0:T(8,128)(2,1)S(1)} %get-tuple-element.24), channel_id=1, source_target_pairs={{0,8},{4,12},{8,0},{12,4},{1,9},{5,13},{9,1},{13,5},{2,10},{6,14},... | collective-permute-start | bytes 786440 | tf_op jit(solution)/shard_map/ppermute | solution.py:29
  4.2 0.0 collective-permute-done.refs_1_
  4.2 0.0 copy-start
  4.2 0.9 %copy-done = bf16[64,7168]{1,0:T(8,128)(2,1)} copy-done((bf16[64,7168]{1,0:T(8,128)(2,1)}, bf16[64,7168]{1,0:T(8,128)(2,1)S(1)}, u32[]{:S(2)}) %copy-start) | copy-done | bytes 917528
  5.1 6.3 %near.2 = (bf16[4096,1024]{1,0:T(8,128)(2,1)S(1)}, f32[128,1024]{1,0:T(8,128)S(1)}) custom-call(bf16[64,7168]{1,0:T(8,128)(2,1)} %refs_0_.3, bf16[64,7168]{1,0:T(8,128)(2,1)} %copy-done, bf16[2,28672,128]{2,1,0:T(8,128)(2,1)} %bitcast.8), custom_call_target="tpu_custom_call" | custom-call | tf_op jit(solution)/shard_map/near/pallas_call | solution.py:155
  11.4 1.5 %collective-permute-start.3 = (bf16[64,3200]{1,0:T(8,128)(2,1)S(1)}, bf16[64,3200]{1,0:T(8,128)(2,1)S(1)}, u32[]{:S(2)}, u32[]{:S(2)}) collective-permute-start(bf16[64,3200]{1,0:T(8,128)(2,1)S(1)} %get-tuple-element.30), channel_id=1, source_target_pairs={{0,8},{4,12},{8,0},{12,4},{1,9},{5,13},{9,1},{13,5},{2,10},{6,14},... | collective-permute-start | bytes 1228808 | tf_op jit(solution)/shard_map/ppermute | solution.py:29
  12.9 0.0 collective-permute-done.1.refs_1_
  12.9 0.0 collective-permute-start.5
  13.0 1.6 %collective-permute-start.4 = (bf16[64,2048]{1,0:T(8,128)(2,1)S(1)}, bf16[64,2048]{1,0:T(8,128)(2,1)S(1)}, u32[]{:S(2)}, u32[]{:S(2)}) collective-permute-start(bf16[64,2048]{1,0:T(8,128)(2,1)S(1)} %collective-permute-done.1.refs_1_), channel_id=1, source_target_pairs={{0,1},{1,0},{2,3},{3,2},{4,5},{5,4},{6,7},{7,6},{8,9},{9,8},{10,11... | collective-permute-start | bytes 786440 | tf_op jit(solution)/shard_map/ppermute | solution.py:29
  14.5 0.2 collective-permute-start.2
  14.8 5.1 %near.3 = (bf16[3072,1024]{1,0:T(8,128)(2,1)S(1)}, f32[128,1024]{1,0:T(8,128)S(1)}) custom-call(bf16[64,7168]{1,0:T(8,128)(2,1)} %refs_0_.3, bf16[64,7168]{1,0:T(8,128)(2,1)} %copy-done, bf16[2,28672,128]{2,1,0:T(8,128)(2,1)} %bitcast.9, f32[128,1024]{1,0:T(8,128)S(1)} %get-tuple-element.26.refs_3_), custom_call_target="tpu_custom_call" | custom-call | tf_op jit(solution)/shard_map/near/pallas_call | solution.py:155
  19.8 0.0 collective-permute-done.2.refs_1_
  19.9 0.1 near_gated.1.near_ref
  20.0 3.1 %load.1.w_ref = bf16[512,7168]{1,0:T(8,128)(2,1)S(1)} custom-call(bf16[512,7168]{1,0:T(8,128)(2,1)} %bitcast.10), custom_call_target="tpu_custom_call" | custom-call | tf_op jit(solution)/shard_map/load/pallas_call | solution.py:294
  23.1 0.0 collective-permute-done.5.refs_2_
  23.1 0.7 %far.2.refs_0_ = f32[128,1024]{1,0:T(8,128)S(1)} custom-call(bf16[4096,1024]{1,0:T(8,128)(2,1)S(1)} %get-tuple-element.32.refs_0_.refs_2_, bf16[64,2048]{1,0:T(8,128)(2,1)S(1)} %collective-permute-done.1.refs_1_, bf16[64,2048]{1,0:T(8,128)(2,1)S(1)} %collective-permute-done.5.refs_2_), custom_call_target="tpu_custom_call" | custom-call | tf_op jit(solution)/shard_map/far/pallas_call | solution.py:197
  23.8 0.0 collective-permute-done.4.refs_5_
  23.8 0.0 collective-permute-done.3.refs_3_.refs_0_
  23.8 0.3 collective-permute-start.6
  24.2 0.2 collective-permute-start.7
  24.4 1.6 %collective-permute-done.7.refs_6_ = bf16[64,2048]{1,0:T(8,128)(2,1)S(1)} collective-permute-done((bf16[64,2048]{1,0:T(8,128)(2,1)S(1)}, bf16[64,2048]{1,0:T(8,128)(2,1)S(1)}, u32[]{:S(2)}, u32[]{:S(2)}) %collective-permute-start.7) | collective-permute-done | bytes 262176 | tf_op jit(solution)/shard_map/ppermute | solution.py:29
  26.0 0.0 collective-permute-done.6.refs_4_.refs_1_
  26.0 1.5 %far.3.acc_ref = f32[128,1024]{1,0:T(8,128)S(1)} custom-call(f32[128,1024]{1,0:T(8,128)S(1)} %far.2.refs_0_, bf16[3072,1024]{1,0:T(8,128)(2,1)S(1)} %get-tuple-element.35.refs_1_, bf16[4096,1024]{1,0:T(8,128)(2,1)S(1)} %get-tuple-element.32.refs_0_.refs_2_, bf16[64,3200]{1,0:T(8,128)(2,1)S(1)} %collective-permute-done.3.refs_3_.refs_0_, ...), custom_call_target="tpu_custom_call" | custom-call | tf_op jit(solution)/shard_map/far/pallas_call | solution.py:197
  27.6 0.2 far_gated.1.h_ref
  27.8 0.7 %down.3 = bf16[128,3584]{1,0:T(8,128)(2,1)S(1)} custom-call(bf16[256,512]{1,0:T(8,128)(2,1)S(1)} %far_gated.1.h_ref, bf16[512,7168]{1,0:T(8,128)(2,1)S(1)} %load.1.w_ref), custom_call_target="tpu_custom_call" | custom-call | tf_op jit(solution)/shard_map/down/pallas_call | solution.py:313
  28.5 0.3 collective-permute-start.8
  28.8 0.7 %down.4 = bf16[128,3584]{1,0:T(8,128)(2,1)S(1)} custom-call(bf16[256,512]{1,0:T(8,128)(2,1)S(1)} %far_gated.1.h_ref, bf16[512,7168]{1,0:T(8,128)(2,1)S(1)} %load.1.w_ref), custom_call_target="tpu_custom_call" | custom-call | tf_op jit(solution)/shard_map/down/pallas_call | solution.py:313
  29.5 0.3 collective-permute-start.9
  29.8 1.3 %down.5 = bf16[128,7168]{1,0:T(8,128)(2,1)S(1)} custom-call(bf16[256,512]{1,0:T(8,128)(2,1)S(1)} %far_gated.1.h_ref, bf16[512,7168]{1,0:T(8,128)(2,1)S(1)} %load.1.w_ref), custom_call_target="tpu_custom_call" | custom-call | tf_op jit(solution)/shard_map/down/pallas_call | solution.py:313
  31.1 0.0 collective-permute-done.8
  31.1 0.1 constant_dynamic-update-slice_fusion.1
  31.2 1.1 %collective-permute-done.9 = bf16[128,3584]{1,0:T(8,128)(2,1)S(1)} collective-permute-done((bf16[128,3584]{1,0:T(8,128)(2,1)S(1)}, bf16[128,3584]{1,0:T(8,128)(2,1)S(1)}, u32[]{:S(2)}, u32[]{:S(2)}) %collective-permute-start.9) | collective-permute-done | bytes 917536 | tf_op jit(solution)/shard_map/ppermute | solution.py:29
  32.3 0.1 constant_dynamic-update-slice_fusion
  32.4 0.2 add_convert_fusion
  32.6 0.8 %collective-permute-start.10 = (bf16[64,7168]{1,0:T(8,128)(2,1)S(1)}, bf16[64,7168]{1,0:T(8,128)(2,1)S(1)}, u32[]{:S(2)}, u32[]{:S(2)}) collective-permute-start(bf16[64,7168]{1,0:T(8,128)(2,1)S(1)} %add_convert_fusion), channel_id=1, source_target_pairs={{0,1},{1,0},{2,3},{3,2},{4,12},{5,13},{6,14},{7,15},{8,9},{9,8},{1... | collective-permute-start | bytes 2752520 | tf_op jit(solution)/shard_map/ppermute | solution.py:391
  33.4 12.7 %collective-permute-done.10 = bf16[64,7168]{1,0:T(8,128)(2,1)S(1)} collective-permute-done((bf16[64,7168]{1,0:T(8,128)(2,1)S(1)}, bf16[64,7168]{1,0:T(8,128)(2,1)S(1)}, u32[]{:S(2)}, u32[]{:S(2)}) %collective-permute-start.10) | collective-permute-done | bytes 917536 | tf_op jit(solution)/shard_map/ppermute | solution.py:391
  46.1 0.2 add_convert_fusion.1
  46.3 2.6 %collective-permute-start.11 = (bf16[32,7168]{1,0:T(8,128)(2,1)S(1)}, bf16[32,7168]{1,0:T(8,128)(2,1)S(1)}, u32[]{:S(2)}, u32[]{:S(2)}) collective-permute-start(bf16[32,7168]{1,0:T(8,128)(2,1)S(1)} %add_convert_fusion.1), channel_id=1, source_target_pairs={{0,2},{1,3},{2,0},{3,1},{4,5},{5,4},{6,7},{7,6},{8,10},{9,11},{10,... | collective-permute-start | bytes 1376264 | tf_op jit(solution)/shard_map/ppermute | solution.py:391
  48.9 14.4 %collective-permute-done.11 = bf16[32,7168]{1,0:T(8,128)(2,1)S(1)} collective-permute-done((bf16[32,7168]{1,0:T(8,128)(2,1)S(1)}, bf16[32,7168]{1,0:T(8,128)(2,1)S(1)}, u32[]{:S(2)}, u32[]{:S(2)}) %collective-permute-start.11) | collective-permute-done | bytes 458784 | tf_op jit(solution)/shard_map/ppermute | solution.py:391
  63.3 0.1 add_convert_fusion.3
  63.4 0.8 %collective-permute-start.12 = (bf16[16,7168]{1,0:T(8,128)(2,1)S(1)}, bf16[16,7168]{1,0:T(8,128)(2,1)S(1)}, u32[]{:S(2)}, u32[]{:S(2)}) collective-permute-start(bf16[16,7168]{1,0:T(8,128)(2,1)S(1)} %add_convert_fusion.3), channel_id=1, source_target_pairs={{0,8},{1,9},{2,10},{3,11},{4,6},{5,7},{6,4},{7,5},{8,0},{9,1},{10,... | collective-permute-start | bytes 688136 | tf_op jit(solution)/shard_map/ppermute | solution.py:391
  64.2 5.3 %collective-permute-done.12 = bf16[16,7168]{1,0:T(8,128)(2,1)S(1)} collective-permute-done((bf16[16,7168]{1,0:T(8,128)(2,1)S(1)}, bf16[16,7168]{1,0:T(8,128)(2,1)S(1)}, u32[]{:S(2)}, u32[]{:S(2)}) %collective-permute-start.12) | collective-permute-done | bytes 229408 | tf_op jit(solution)/shard_map/ppermute | solution.py:391
  69.5 0.8 %add_convert_fusion.2 = bf16[16,7168]{1,0:T(8,128)(2,1)} fusion(bf16[16,7168]{1,0:T(8,128)(2,1)S(1)} %collective-permute-done.12, bf16[64,7168]{1,0:T(8,128)(2,1)S(1)} %collective-permute-done.10, bf16[128,7168]{1,0:T(8,128)(2,1)S(1)} %constant_dynamic-update-slice_fusion, bf16[128,7168]{1,0:T(8,128)(2,1)S(1)} %down.5, ...), kind=kLoop, calls=%fused_computation.2 | loop fusion | flops 1146880 | bytes 1376256 | tf_op jit(solution)/shard_map/convert_element_type | solution.py:33
Async XLA Ops:
  0.0 4.2 %collective-permute-start = (bf16[64,7168]{1,0:T(8,128)(2,1)}, bf16[64,7168]{1,0:T(8,128)(2,1)S(1)}, u32[]{:S(2)}, u32[]{:S(2)}) collective-permute-start(bf16[64,7168]{1,0:T(8,128)(2,1)} %refs_0_.3), channel_id=1, source_target_pairs={{0,4},{4,0},{8,12},{12,8},{1,5},{5,1},{9,13},{13,9},{2,6},{6,2},{1... | collective-permute-start | bytes 2752520 | tf_op jit(solution)/shard_map/ppermute | solution.py:29
  1.6 11.3 %collective-permute-start.1 = (bf16[64,2048]{1,0:T(8,128)(2,1)S(1)}, bf16[64,2048]{1,0:T(8,128)(2,1)S(1)}, u32[]{:S(2)}, u32[]{:S(2)}) collective-permute-start(bf16[64,2048]{1,0:T(8,128)(2,1)S(1)} %get-tuple-element.24), channel_id=1, source_target_pairs={{0,8},{4,12},{8,0},{12,4},{1,9},{5,13},{9,1},{13,5},{2,10},{6,14},... | collective-permute-start | bytes 786440 | tf_op jit(solution)/shard_map/ppermute | solution.py:29
  4.2 0.9 %copy-start = (bf16[64,7168]{1,0:T(8,128)(2,1)}, bf16[64,7168]{1,0:T(8,128)(2,1)S(1)}, u32[]{:S(2)}) copy-start(bf16[64,7168]{1,0:T(8,128)(2,1)S(1)} %collective-permute-done.refs_1_) | copy-start | bytes 2752516
  11.4 12.4 %collective-permute-start.3 = (bf16[64,3200]{1,0:T(8,128)(2,1)S(1)}, bf16[64,3200]{1,0:T(8,128)(2,1)S(1)}, u32[]{:S(2)}, u32[]{:S(2)}) collective-permute-start(bf16[64,3200]{1,0:T(8,128)(2,1)S(1)} %get-tuple-element.30), channel_id=1, source_target_pairs={{0,8},{4,12},{8,0},{12,4},{1,9},{5,13},{9,1},{13,5},{2,10},{6,14},... | collective-permute-start | bytes 1228808 | tf_op jit(solution)/shard_map/ppermute | solution.py:29
  12.9 10.1 %collective-permute-start.5 = (bf16[64,2048]{1,0:T(8,128)(2,1)S(1)}, bf16[64,2048]{1,0:T(8,128)(2,1)S(1)}, u32[]{:S(2)}, u32[]{:S(2)}) collective-permute-start(bf16[64,2048]{1,0:T(8,128)(2,1)S(1)} %collective-permute-done.1.refs_1_), channel_id=1, source_target_pairs={{0,4},{4,0},{8,12},{12,8},{1,5},{5,1},{9,13},{13,9},{2,6},{6,2},{1... | collective-permute-start | bytes 786440 | tf_op jit(solution)/shard_map/ppermute | solution.py:29
  13.0 10.9 %collective-permute-start.4 = (bf16[64,2048]{1,0:T(8,128)(2,1)S(1)}, bf16[64,2048]{1,0:T(8,128)(2,1)S(1)}, u32[]{:S(2)}, u32[]{:S(2)}) collective-permute-start(bf16[64,2048]{1,0:T(8,128)(2,1)S(1)} %collective-permute-done.1.refs_1_), channel_id=1, source_target_pairs={{0,1},{1,0},{2,3},{3,2},{4,5},{5,4},{6,7},{7,6},{8,9},{9,8},{10,11... | collective-permute-start | bytes 786440 | tf_op jit(solution)/shard_map/ppermute | solution.py:29
  14.5 5.3 %collective-permute-start.2 = (bf16[64,128]{1,0:T(8,128)(2,1)S(1)}, bf16[64,128]{1,0:T(8,128)(2,1)S(1)}, u32[]{:S(2)}, u32[]{:S(2)}) collective-permute-start(bf16[64,128]{1,0:T(8,128)(2,1)S(1)} %get-tuple-element.28.refs_0_), channel_id=1, source_target_pairs={{0,4},{4,0},{8,12},{12,8},{1,5},{5,1},{9,13},{13,9},{2,6},{6,2},{1... | collective-permute-start | bytes 49160 | tf_op jit(solution)/shard_map/ppermute | solution.py:29
  23.8 2.2 %collective-permute-start.6 = (bf16[64,3200]{1,0:T(8,128)(2,1)S(1)}, bf16[64,3200]{1,0:T(8,128)(2,1)S(1)}, u32[]{:S(2)}, u32[]{:S(2)}) collective-permute-start(bf16[64,3200]{1,0:T(8,128)(2,1)S(1)} %collective-permute-done.3.refs_3_.refs_0_), channel_id=1, source_target_pairs={{0,4},{4,0},{8,12},{12,8},{1,5},{5,1},{9,13},{13,9},{2,6},{6,2},{1... | collective-permute-start | bytes 1228808 | tf_op jit(solution)/shard_map/ppermute | solution.py:29
  24.2 1.8 %collective-permute-start.7 = (bf16[64,2048]{1,0:T(8,128)(2,1)S(1)}, bf16[64,2048]{1,0:T(8,128)(2,1)S(1)}, u32[]{:S(2)}, u32[]{:S(2)}) collective-permute-start(bf16[64,2048]{1,0:T(8,128)(2,1)S(1)} %collective-permute-done.4.refs_5_), channel_id=1, source_target_pairs={{0,4},{4,0},{8,12},{12,8},{1,5},{5,1},{9,13},{13,9},{2,6},{6,2},{1... | collective-permute-start | bytes 786440 | tf_op jit(solution)/shard_map/ppermute | solution.py:29
  28.5 2.7 %collective-permute-start.8 = (bf16[128,3584]{1,0:T(8,128)(2,1)S(1)}, bf16[128,3584]{1,0:T(8,128)(2,1)S(1)}, u32[]{:S(2)}, u32[]{:S(2)}) collective-permute-start(bf16[128,3584]{1,0:T(8,128)(2,1)S(1)} %down.3), channel_id=1, source_target_pairs={{0,4},{4,0},{8,12},{12,8},{1,5},{5,1},{9,13},{13,9},{2,6},{6,2},{1... | collective-permute-start | bytes 2752520 | tf_op jit(solution)/shard_map/ppermute | solution.py:29
  29.5 2.8 %collective-permute-start.9 = (bf16[128,3584]{1,0:T(8,128)(2,1)S(1)}, bf16[128,3584]{1,0:T(8,128)(2,1)S(1)}, u32[]{:S(2)}, u32[]{:S(2)}) collective-permute-start(bf16[128,3584]{1,0:T(8,128)(2,1)S(1)} %down.4), channel_id=1, source_target_pairs={{0,4},{4,0},{8,12},{12,8},{1,5},{5,1},{9,13},{13,9},{2,6},{6,2},{1... | collective-permute-start | bytes 2752520 | tf_op jit(solution)/shard_map/ppermute | solution.py:29
  32.6 13.5 %collective-permute-start.10 = (bf16[64,7168]{1,0:T(8,128)(2,1)S(1)}, bf16[64,7168]{1,0:T(8,128)(2,1)S(1)}, u32[]{:S(2)}, u32[]{:S(2)}) collective-permute-start(bf16[64,7168]{1,0:T(8,128)(2,1)S(1)} %add_convert_fusion), channel_id=1, source_target_pairs={{0,1},{1,0},{2,3},{3,2},{4,12},{5,13},{6,14},{7,15},{8,9},{9,8},{1... | collective-permute-start | bytes 2752520 | tf_op jit(solution)/shard_map/ppermute | solution.py:391
  46.3 17.0 %collective-permute-start.11 = (bf16[32,7168]{1,0:T(8,128)(2,1)S(1)}, bf16[32,7168]{1,0:T(8,128)(2,1)S(1)}, u32[]{:S(2)}, u32[]{:S(2)}) collective-permute-start(bf16[32,7168]{1,0:T(8,128)(2,1)S(1)} %add_convert_fusion.1), channel_id=1, source_target_pairs={{0,2},{1,3},{2,0},{3,1},{4,5},{5,4},{6,7},{7,6},{8,10},{9,11},{10,... | collective-permute-start | bytes 1376264 | tf_op jit(solution)/shard_map/ppermute | solution.py:391
  63.4 6.1 %collective-permute-start.12 = (bf16[16,7168]{1,0:T(8,128)(2,1)S(1)}, bf16[16,7168]{1,0:T(8,128)(2,1)S(1)}, u32[]{:S(2)}, u32[]{:S(2)}) collective-permute-start(bf16[16,7168]{1,0:T(8,128)(2,1)S(1)} %add_convert_fusion.3), channel_id=1, source_target_pairs={{0,8},{1,9},{2,10},{3,11},{4,6},{5,7},{6,4},{7,5},{8,0},{9,1},{10,... | collective-permute-start | bytes 688136 | tf_op jit(solution)/shard_map/ppermute | solution.py:391

commit v3 on v2

--- a/solution.py
+++ b/solution.py
@@ -10,9 +10,8 @@
 LANES = 128
 VMEM_LIMIT = 16 << 20
 RUN = 4
-FRONT = 4
-CHUNKS = [(1, ("zy", "yz"))]
-DOWN_SHARES = [1, 1]
+FRONT = 3
+CHUNKS = [(6, ("zyz", "yz")), (5, ("Zyz", "yZ"))]
 
 
 def bits_of(count):
@@ -98,20 +97,26 @@
     return pl.BlockSpec(memory_space=memory_space)
 
 
-def near_step(xs, w_view, before, hidden, depth, first, last):
+def near_step(xs, w_view, before, hidden, depth, first, last, extra=None, spans=()):
     rows, ratio = xs[0].shape[0], 2 * hidden // LANES
+    features = w_view.shape[1] // ratio
     halves, steps = hidden // LANES, last - first
 
     def body(*refs):
         x_refs, refs = refs[: len(xs)], list(refs[len(xs) :])
         w_ref = refs.pop(0)
-        before_ref = None if before is None else refs.pop(0)
-        clean_ref, acc_ref, held, blocks, wide, sems = refs
+        if extra is not None:
+            extra_ref = refs.pop(0)
+        if before is not None:
+            before_ref, _ = refs.pop(0), refs.pop(0)
+        acc_ref, clean_ref = refs.pop(0), refs.pop(0)
+        extra_outs = [refs.pop(0) for _ in spans]
+        held, blocks, sems = refs
         own = [
             pltpu.make_async_copy(
                 ref.at[:, pl.ds(first * depth, steps * depth)],
                 held.at[pl.ds(i * rows, rows), :],
-                sems.at[2 + i],
+                sems.at[i],
             )
             for i, ref in enumerate(x_refs)
         ]
@@ -119,52 +124,73 @@
         def fetch(step):
             return pltpu.make_async_copy(
                 w_ref.at[:, pl.ds((first + step) * depth * ratio, depth * ratio), :],
-                blocks.at[step % 2],
-                sems.at[step % 2],
+                blocks.at[step],
+                sems.at[len(xs) + step],
             )
 
+        pieces = [
+            pltpu.make_async_copy(
+                extra_ref.at[:, pl.ds(*span)], out, sems.at[len(xs) + steps + i]
+            )
+            for i, (span, out) in enumerate(zip(spans, extra_outs))
+        ]
         fetch(0).start()
         for copy in own:
             copy.start()
+        for step in range(1, steps):
+            fetch(step).start()
+        for copy in pieces:
+            copy.start()
         for step in range(steps):
-            if step + 1 < steps:
-                fetch(step + 1).start()
             fetch(step).wait()
-            at = step * depth
+            here = pl.ds((first + step) * depth, depth)
             for member in range(2):
-                wide[...] = blocks[step % 2, member].astype(F32)
                 for s in range(2):
                     for t in range(halves):
                         column = (2 * member + s) * hidden + t * LANES
-                        clean_ref[pl.ds(at, depth), pl.ds(column, LANES)] = wide[
-                            pl.ds(2 * t + s, depth, stride=2 * halves), :
-                        ].astype(BF16)
+                        clean_ref[here, pl.ds(column, LANES)] = blocks[
+                            step, member, pl.ds(2 * t + s, depth, stride=2 * halves), :
+                        ]
             if step == 0:
                 for copy in own:
                     copy.wait()
             value = jnp.dot(
-                held[:, pl.ds(at, depth)],
-                clean_ref[pl.ds(at, depth), :],
+                held[:, pl.ds(step * depth, depth)],
+                clean_ref[here, :],
                 preferred_element_type=F32,
             )
             if step or before is not None:
                 value += (acc_ref if step else before_ref)[...]
             acc_ref[...] = value
-
-    operands = [in_hbm(x) for x in (*xs, w_view)] + ([] if before is None else [before])
-    return pl.pallas_call(
-        body,
-        in_specs=[whole(pl.ANY)] * (len(xs) + 1) + [whole()] * (len(operands) - len(xs) - 1),
-        out_specs=[whole(), whole()],
-        out_shape=[
-            jax.ShapeDtypeStruct((steps * depth, 4 * hidden), BF16),
-            jax.ShapeDtypeStruct((len(xs) * rows, 4 * hidden), F32),
-        ],
+        for copy in pieces:
+            copy.wait()
+
+    operands = [in_hbm(xs[0]), *xs[1:], in_hbm(w_view)]
+    specs = [whole(pl.ANY)] * len(operands)
+    if extra is not None:
+        operands.append(in_hbm(extra))
+        specs.append(whole(pl.ANY))
+    aliases = {}
+    if before is not None:
+        aliases = {len(operands): 0, len(operands) + 1: 1}
+        operands += before
+        specs += [whole()] * 2
+    shapes = [
+        jax.ShapeDtypeStruct((len(xs) * rows, 4 * hidden), F32),
+        jax.ShapeDtypeStruct((features, 4 * hidden), BF16),
+    ]
+    for _, width in spans:
+        shapes.append(jax.ShapeDtypeStruct((extra.shape[0], width), extra.dtype))
+    return pl.pallas_call(
+        body,
+        in_specs=specs,
+        out_specs=[whole()] * len(shapes),
+        out_shape=shapes,
+        input_output_aliases=aliases,
         scratch_shapes=[
             pltpu.VMEM((len(xs) * rows, steps * depth), BF16),
-            pltpu.VMEM((2, 2, depth * ratio, LANES), BF16),
-            pltpu.VMEM((depth * ratio, LANES), F32),
-            pltpu.SemaphoreType.DMA((2 + len(xs),)),
+            pltpu.VMEM((steps, 2, depth * ratio, LANES), BF16),
+            pltpu.SemaphoreType.DMA((len(xs) + steps + len(spans),)),
         ],
         compiler_params=pltpu.CompilerParams(vmem_limit_bytes=VMEM_LIMIT),
         name="near",
@@ -285,39 +311,20 @@
     )(near_rows, acc, *tables)
 
 
-def load(x):
-    def body(x_ref, out_ref, sem):
-        copy = pltpu.make_async_copy(x_ref, out_ref, sem)
-        copy.start()
-        copy.wait()
-
-    return pl.pallas_call(
-        body,
-        in_specs=[whole(pl.ANY)],
-        out_specs=whole(),
-        out_shape=jax.ShapeDtypeStruct(x.shape, x.dtype),
-        scratch_shapes=[pltpu.SemaphoreType.DMA(())],
-        compiler_params=pltpu.CompilerParams(vmem_limit_bytes=VMEM_LIMIT),
-        name="load",
-    )(in_hbm(x))
-
-
-def down_step(hidden_rows, w_flat, first, count, start, width):
+def down_step(hidden_rows, weights, first, count):
     def body(h_ref, w_ref, out_ref):
         out_ref[...] = jnp.dot(
-            h_ref[pl.ds(first, count), :],
-            w_ref[:, pl.ds(start, width)],
-            preferred_element_type=F32,
+            h_ref[pl.ds(first, count), :], w_ref[...], preferred_element_type=F32
         ).astype(BF16)
 
     return pl.pallas_call(
         body,
         in_specs=[whole(), whole()],
         out_specs=whole(),
-        out_shape=jax.ShapeDtypeStruct((count, width), BF16),
+        out_shape=jax.ShapeDtypeStruct((count, weights.shape[1]), BF16),
         compiler_params=pltpu.CompilerParams(vmem_limit_bytes=VMEM_LIMIT),
         name="down",
-    )(hidden_rows, w_flat)
+    )(hidden_rows, weights)
 
 
 def local(tokens, group_ids, gates, w_in, w_down):
@@ -351,32 +358,34 @@
     relayed, direct, table = prepare(tokens, group_ids, gates, run)
     relayed = far(relayed)
     table_beside = exchange(table, "grp", 1)
-    clean_front, near_acc = near_step(
-        [tokens, beside], w_view, None, hidden, unit, 0, FRONT
-    )
-    direct = far(after(direct, near_acc))
-    relayed, near_acc = lax.optimization_barrier((relayed, near_acc))
+    held = [tokens, beside]
+    spans = split(features, features // 28, [share for share, _ in CHUNKS])
+    near = near_step(held, w_view, None, hidden, unit, 0, FRONT)
+    direct = far(after(direct, near[0]))
+    relayed, near = lax.optimization_barrier((relayed, near))
     passed = [exchange(x, "exp", 1) for x in relayed]
-    clean_back, near_acc = near_step(
-        [tokens, beside], w_view, near_acc, hidden, unit, FRONT, steps
+    near_acc, clean, *w_flats = near_step(
+        held, w_view, near, hidden, unit, FRONT, steps, w_flat, spans
     )
     near_rows = near_gated(near_acc, [table, table_beside], hidden)
-    far_acc = far_step(None, [both(relayed)], [(0, 0, clean_front, 0, run, run)])
-    w_flat = load(after(w_flat, near_rows))
-    direct, passed, far_acc, w_flat = lax.optimization_barrier((direct, passed, far_acc, w_flat))
-    direct, passed = both(direct), both(passed)
-    middle = FRONT * unit - 2 * run
-    pieces = [
-        (0, 0, clean_front, 2 * run, middle, 0),
-        (0, middle, clean_back, 0, features - FRONT * unit, 0),
-        (1, 0, clean_front, run, run, -run),
-    ]
-    pieces = [piece for piece in pieces if piece[4]]
-    far_acc = far_step(far_acc, [direct, passed], pieces)
+    far_acc = far_step(None, [both(relayed)], [(0, 0, clean, 0, run, run)])
+    direct, passed, far_acc, near_rows = lax.optimization_barrier(
+        (direct, passed, far_acc, near_rows)
+    )
+    passed, direct = both(passed), both(direct)
+    far_acc = far_step(far_acc, [passed], [(0, 0, clean, run, run, -run)])
+    direct[-1] = after(direct[-1], far_acc)
+    far_acc = far_step(far_acc, [direct], [(0, 0, clean, 2 * run, features - 2 * run, 0)])
 
     grp_stages = [("grp", b) for b in range(1, group_bits)]
     exp_stages = [("exp", b) for b in range(part_bits)]
-    by_name = {"zy": exp_stages + grp_stages, "yz": grp_stages + exp_stages}
+    turned = exp_stages[::-1]
+    by_name = {
+        "yz": grp_stages + exp_stages,
+        "yZ": grp_stages + turned,
+        "zyz": exp_stages[:1] + grp_stages + exp_stages[1:],
+        "Zyz": turned[:1] + grp_stages + turned[1:],
+    }
     plans = [[by_name[name] for name in names] for _, names in CHUNKS]
     order = [0, 1] + list(range(2, groups, 2)) + list(range(3, groups, 2))
     all_rows = far_gated(near_rows, far_acc, direct, hidden, plans, order)
@@ -392,26 +401,29 @@
 
     state = []
     half = rows * groups // 2
-    spans = split(features, features // 28, [share for share, _ in CHUNKS])
-    for (start, width), plan_rows in zip(spans, all_rows):
-        comes = []
-        for offset, piece in split(width, features // 56, DOWN_SHARES):
-            send = down_step(plan_rows, w_flat, half, half, start + offset, piece)
-            plan_rows = after(plan_rows, send)
-            comes.append(exchange(send, "grp", 1))
-        keep = down_step(plan_rows, w_flat, 0, half, start, width)
-        state.append([keep, jnp.concatenate(comes, axis=1)])
-    token = None
-    height = rows * groups // 2
+    done = None
+    for weights, plan_rows in zip(w_flats, all_rows):
+        plan_rows = plan_rows if done is None else after(plan_rows, done)
+        done = down_step(plan_rows, weights, half, half)
+        state.append([exchange(done, "grp", 1)])
+    for weights, plan_rows, terms in zip(w_flats, all_rows, state):
+        done = down_step(after(plan_rows, done), weights, 0, half)
+        terms.append(done)
+    send = None
+    height = half
     for stage in range(len(grp_stages + exp_stages)):
         height //= 2
         for terms, routes in zip(state, plans):
-            back = turn(add(*[t[height : 2 * height] for t in terms]), routes, stage)
-            if token is not None:
-                back = after(back, token)
-            terms.append(back)
-            token = back
-    return jnp.concatenate([add(*[t[:height] for t in terms]) for terms in state], axis=1)
+            if send is not None:
+                terms[-1] = after(terms[-1], send)
+            send = add(*[t[height : 2 * height] for t in terms])
+            terms.append(turn(send, routes, stage))
+    outs = []
+    for terms in state:
+        if outs:
+            terms[-1] = after(terms[-1], outs[-1])
+        outs.append(add(*[t[:height] for t in terms]))
+    return jnp.concatenate(outs, axis=1)
 
 
 def solution(mesh):

time: 70.6 us -> 58.5 us (0.83)
  waiting for transfers between devices: 35 us -> 24.8 us
  Pallas kernels: 20.9 us -> 16.2 us
  starting transfers between devices: 11.8 us -> 15.8 us
  local copies, waits for them, and re-layouts: 1.09 us -> 0 us
    ppermute x3 -> x6, waiting for transfers between devices: 32.3 us -> 21.5 us  [turn(): return lax.ppermute(x, ('grp', 'exp'), pairs)]
    pallas_call x3 -> x2, Pallas kernels: 14.5 us -> 9.74 us  [near_step(): pl.pallas_call(body, in_specs=specs, out_specs=[whole()] * len(shapes), o...]
    ppermute x3 -> x6, starting transfers between devices: 4.22 us -> 7.81 us  [turn(): return lax.ppermute(x, ('grp', 'exp'), pairs)]
    unnamed x3 -> x0, local copies, waits for them, and re-layouts: 1 us -> none
    pallas_call x2 -> x3, Pallas kernels: 2.27 us -> 2.44 us  [far_step(): pl.pallas_call(body, in_specs=[whole()] * len(operands), out_specs=whole(...]
    pallas_call x3 -> x4, Pallas kernels: 2.71 us -> 2.59 us  [down_step(): pl.pallas_call(body, in_specs=[whole(), whole()], out_specs=whole(), out_...]
  transfers between devices with their start and end apart: 13 -> 16, of which waited for: 5 -> 9; matrix products, arithmetic and copies ran while one was open for 0% -> 1% of each run, Pallas kernels for 26% -> 25%
where the time goes in v3:
time: 58.5 us; the launch traced here: 58.3 us
  waiting for transfers between devices  24.8 us (42%)
  Pallas kernels  16.2 us (28%)
  starting transfers between devices  15.8 us (27%)
  other arithmetic  1.36 us (2%)
    ppermute x6, waiting for transfers between devices, turn(): return lax.ppermute(x, ('grp', 'exp'), pairs)  21.5 us
    pallas_call x2, Pallas kernels, near_step(): pl.pallas_call(body, in_specs=specs, out_specs=[whole()] * len(shapes), o...  9.74 us
    ppermute x10, starting transfers between devices, exchange(): lax.ppermute(x, axis, [(i, i ^ mask) for i in range(lax.axis_size(axis))])  7.96 us
    ppermute x6, starting transfers between devices, turn(): return lax.ppermute(x, ('grp', 'exp'), pairs)  7.81 us
    ppermute x10, waiting for transfers between devices, exchange(): lax.ppermute(x, axis, [(i, i ^ mask) for i in range(lax.axis_size(axis))])  3.3 us
    pallas_call x4, Pallas kernels, down_step(): pl.pallas_call(body, in_specs=[whole(), whole()], out_specs=whole(), out_...  2.59 us
    pallas_call x3, Pallas kernels, far_step(): pl.pallas_call(body, in_specs=[whole()] * len(operands), out_specs=whole(...  2.44 us
  transfers between devices with their start and end apart: 16, of which 9 were waited for; matrix products, arithmetic and copies ran while one was open for 1% of the time, Pallas kernels for 25%

profile of v3, /device:TPU:0, one launch (start us, length us, event | category | flops | bytes accessed | tf_op | source)
XLA Modules:
  0.0 58.3 jit_solution(6538507919645345405)
XLA Ops:
  0.0 0.5 collective-permute-start
  0.5 1.1 %prepare.1 = (bf16[64,2048]{1,0:T(8,128)(2,1)S(1)}, bf16[64,3200]{1,0:T(8,128)(2,1)S(1)}, bf16[64,128]{1,0:T(8,128)(2,1)S(1)}) custom-call(bf16[64,7168]{1,0:T(8,128)(2,1)} %refs_0_.3, s32[2,64]{1,0:T(2,128)} %bitcast.11, bf16[4,64]{1,0:T(4,128)(2,1)} %bitcast.12), custom_call_target="tpu_custom_call" | custom-call | tf_op jit(solution)/shard_map/prepare/pallas_call | solution.py:77
  1.6 2.6 %collective-permute-start.2 = (bf16[64,2048]{1,0:T(8,128)(2,1)S(1)}, bf16[64,2048]{1,0:T(8,128)(2,1)S(1)}, u32[]{:S(2)}, u32[]{:S(2)}) collective-permute-start(bf16[64,2048]{1,0:T(8,128)(2,1)S(1)} %get-tuple-element.37), channel_id=1, source_target_pairs={{0,8},{4,12},{8,0},{12,4},{1,9},{5,13},{9,1},{13,5},{2,10},{6,14},... | collective-permute-start | bytes 786440 | tf_op jit(solution)/shard_map/ppermute | solution.py:28
  4.2 4.0 %near.2 = (f32[128,1024]{1,0:T(8,128)S(1)}, bf16[7168,1024]{1,0:T(8,128)(2,1)S(1)}) custom-call(bf16[64,7168]{1,0:T(8,128)(2,1)} %refs_0_.3, bf16[64,7168]{1,0:T(8,128)(2,1)S(1)} %collective-permute-done.refs_1_, bf16[2,28672,128]{2,1,0:T(8,128)(2,1)} %bitcast.8), custom_call_target="tpu_custom_call" | custom-call | tf_op jit(solution)/shard_map/near/pallas_call | solution.py:184
  8.2 1.5 %collective-permute-start.1 = (bf16[64,3200]{1,0:T(8,128)(2,1)S(1)}, bf16[64,3200]{1,0:T(8,128)(2,1)S(1)}, u32[]{:S(2)}, u32[]{:S(2)}) collective-permute-start(bf16[64,3200]{1,0:T(8,128)(2,1)S(1)} %get-tuple-element.36), channel_id=1, source_target_pairs={{0,8},{4,12},{8,0},{12,4},{1,9},{5,13},{9,1},{13,5},{2,10},{6,14},... | collective-permute-start | bytes 1228808 | tf_op jit(solution)/shard_map/ppermute | solution.py:28
  9.7 1.5 %collective-permute-done.2.refs_1_ = bf16[64,2048]{1,0:T(8,128)(2,1)S(1)} collective-permute-done((bf16[64,2048]{1,0:T(8,128)(2,1)S(1)}, bf16[64,2048]{1,0:T(8,128)(2,1)S(1)}, u32[]{:S(2)}, u32[]{:S(2)}) %collective-permute-start.2) | collective-permute-done | bytes 262176 | tf_op jit(solution)/shard_map/ppermute | solution.py:28
  11.2 0.0 collective-permute-start.4
  11.2 2.0 %collective-permute-start.3 = (bf16[64,2048]{1,0:T(8,128)(2,1)S(1)}, bf16[64,2048]{1,0:T(8,128)(2,1)S(1)}, u32[]{:S(2)}, u32[]{:S(2)}) collective-permute-start(bf16[64,2048]{1,0:T(8,128)(2,1)S(1)} %collective-permute-done.2.refs_1_), channel_id=1, source_target_pairs={{0,1},{1,0},{2,3},{3,2},{4,5},{5,4},{6,7},{7,6},{8,9},{9,8},{10,11... | collective-permute-start | bytes 786440 | tf_op jit(solution)/shard_map/ppermute | solution.py:28
  13.2 0.2 collective-permute-start.5
  13.5 5.8 %near.3 = (f32[128,1024]{1,0:T(8,128)S(1)}, bf16[7168,1024]{1,0:T(8,128)(2,1)S(1)}, bf16[512,3840]{1,0:T(8,128)(2,1)S(1)}, bf16[512,3328]{1,0:T(8,128)(2,1)S(1)}) custom-call(bf16[64,7168]{1,0:T(8,128)(2,1)} %refs_0_.3, bf16[64,7168]{1,0:T(8,128)(2,1)S(1)} %collective-permute-done.refs_1_, ...), custom_call_target="tpu_custom_call", output_to_operand_aliasing={{0}: (4, {}), {1}: (5, {})} | custom-call | tf_op jit(solution)/shard_map/near/pallas_call | solution.py:184
  19.3 0.1 near_gated.1.near_ref
  19.4 0.0 collective-permute-done.4.refs_2_
  19.4 0.7 %far.3.refs_0_ = f32[128,1024]{1,0:T(8,128)S(1)} custom-call(bf16[7168,1024]{1,0:T(8,128)(2,1)S(1)} %get-tuple-element.42.refs_0_.refs_1_, bf16[64,2048]{1,0:T(8,128)(2,1)S(1)} %collective-permute-done.2.refs_1_, bf16[64,2048]{1,0:T(8,128)(2,1)S(1)} %collective-permute-done.4.refs_2_), custom_call_target="tpu_custom_call" | custom-call | tf_op jit(solution)/shard_map/far/pallas_call | solution.py:223
  20.1 0.1 collective-permute-done.3.refs_2_
  20.2 0.3 collective-permute-start.7
  20.5 0.2 collective-permute-start.6
  20.7 1.6 %collective-permute-done.6.refs_3_ = bf16[64,2048]{1,0:T(8,128)(2,1)S(1)} collective-permute-done((bf16[64,2048]{1,0:T(8,128)(2,1)S(1)}, bf16[64,2048]{1,0:T(8,128)(2,1)S(1)}, u32[]{:S(2)}, u32[]{:S(2)}) %collective-permute-start.6) | collective-permute-done | bytes 262176 | tf_op jit(solution)/shard_map/ppermute | solution.py:28
  22.3 0.7 %far.4.refs_0_ = f32[128,1024]{1,0:T(8,128)S(1)} custom-call(f32[128,1024]{1,0:T(8,128)S(1)} %far.3.refs_0_, bf16[7168,1024]{1,0:T(8,128)(2,1)S(1)} %get-tuple-element.42.refs_0_.refs_1_, bf16[64,2048]{1,0:T(8,128)(2,1)S(1)} %collective-permute-done.3.refs_2_, bf16[64,2048]{1,0:T(8,128)(2,1)S(1)} %collective-permute-done.6.refs_3_), custom_call_target="tpu_custom_call" | custom-call | tf_op jit(solution)/shard_map/far/pallas_call | solution.py:223
  23.1 0.0 collective-permute-done.7.refs_3_.refs_1_
  23.1 1.0 %far.5.acc_ref = f32[128,1024]{1,0:T(8,128)S(1)} custom-call(f32[128,1024]{1,0:T(8,128)S(1)} %far.4.refs_0_, bf16[7168,1024]{1,0:T(8,128)(2,1)S(1)} %get-tuple-element.42.refs_0_.refs_1_, bf16[64,3200]{1,0:T(8,128)(2,1)S(1)} %collective-permute-done.1.refs_2_.refs_0_, bf16[64,3200]{1,0:T(8,128)(2,1)S(1)} %collective-permute-done.7.refs_3_.refs_1_), custom_call_target="tpu_custom_call" | custom-call | tf_op jit(solution)/shard_map/far/pallas_call | solution.py:223
  24.1 0.2 far_gated.1
  24.3 0.7 %down.4 = bf16[128,3840]{1,0:T(8,128)(2,1)S(1)} custom-call(bf16[256,512]{1,0:T(8,128)(2,1)S(1)} %get-tuple-element.55.h_ref, bf16[512,3840]{1,0:T(8,128)(2,1)S(1)} %get-tuple-element.51.w_ref), custom_call_target="tpu_custom_call" | custom-call | tf_op jit(solution)/shard_map/down/pallas_call | solution.py:320
  25.0 0.3 collective-permute-start.8
  25.3 0.6 %down.5 = bf16[128,3328]{1,0:T(8,128)(2,1)S(1)} custom-call(bf16[256,512]{1,0:T(8,128)(2,1)S(1)} %get-tuple-element.56.h_ref, bf16[512,3328]{1,0:T(8,128)(2,1)S(1)} %get-tuple-element.54.w_ref), custom_call_target="tpu_custom_call" | custom-call | tf_op jit(solution)/shard_map/down/pallas_call | solution.py:320
  25.9 0.3 collective-permute-start.10
  26.2 0.7 %down.6 = bf16[128,3840]{1,0:T(8,128)(2,1)S(1)} custom-call(bf16[256,512]{1,0:T(8,128)(2,1)S(1)} %get-tuple-element.55.h_ref, bf16[512,3840]{1,0:T(8,128)(2,1)S(1)} %get-tuple-element.51.w_ref), custom_call_target="tpu_custom_call" | custom-call | tf_op jit(solution)/shard_map/down/pallas_call | solution.py:320
  26.9 0.6 %down.7 = bf16[128,3328]{1,0:T(8,128)(2,1)S(1)} custom-call(bf16[256,512]{1,0:T(8,128)(2,1)S(1)} %get-tuple-element.56.h_ref, bf16[512,3328]{1,0:T(8,128)(2,1)S(1)} %get-tuple-element.54.w_ref), custom_call_target="tpu_custom_call" | custom-call | tf_op jit(solution)/shard_map/down/pallas_call | solution.py:320
  27.5 0.1 collective-permute-done.8
  27.6 0.1 add_convert_fusion
  27.7 1.8 %collective-permute-start.9 = (bf16[64,3840]{1,0:T(8,128)(2,1)S(1)}, bf16[64,3840]{1,0:T(8,128)(2,1)S(1)}, u32[]{:S(2)}, u32[]{:S(2)}) collective-permute-start(bf16[64,3840]{1,0:T(8,128)(2,1)S(1)} %add_convert_fusion), channel_id=1, source_target_pairs={{0,1},{1,0},{2,3},{3,2},{4,12},{5,13},{6,14},{7,15},{8,9},{9,8},{1... | collective-permute-start | bytes 1474568 | tf_op jit(solution)/shard_map/ppermute | solution.py:400
  29.5 0.1 add_convert_fusion.1
  29.6 2.7 %collective-permute-start.12 = (bf16[64,3328]{1,0:T(8,128)(2,1)S(1)}, bf16[64,3328]{1,0:T(8,128)(2,1)S(1)}, u32[]{:S(2)}, u32[]{:S(2)}) collective-permute-start(bf16[64,3328]{1,0:T(8,128)(2,1)S(1)} %add_convert_fusion.1), channel_id=1, source_target_pairs={{0,2},{1,3},{2,0},{3,1},{4,12},{5,13},{6,14},{7,15},{8,10},{9,11},... | collective-permute-start | bytes 1277960 | tf_op jit(solution)/shard_map/ppermute | solution.py:400
  32.3 11.2 %collective-permute-done.9 = bf16[64,3840]{1,0:T(8,128)(2,1)S(1)} collective-permute-done((bf16[64,3840]{1,0:T(8,128)(2,1)S(1)}, bf16[64,3840]{1,0:T(8,128)(2,1)S(1)}, u32[]{:S(2)}, u32[]{:S(2)}) %collective-permute-start.9) | collective-permute-done | bytes 491552 | tf_op jit(solution)/shard_map/ppermute | solution.py:400
  43.5 0.1 add_convert_fusion.2
  43.6 2.0 %collective-permute-start.11 = (bf16[32,3840]{1,0:T(8,128)(2,1)S(1)}, bf16[32,3840]{1,0:T(8,128)(2,1)S(1)}, u32[]{:S(2)}, u32[]{:S(2)}) collective-permute-start(bf16[32,3840]{1,0:T(8,128)(2,1)S(1)} %add_convert_fusion.2), channel_id=1, source_target_pairs={{0,8},{1,9},{2,10},{3,11},{4,5},{5,4},{6,7},{7,6},{8,0},{9,1},{10,... | collective-permute-start | bytes 737288 | tf_op jit(solution)/shard_map/ppermute | solution.py:400
  45.6 0.1 add_convert_fusion.3
  45.7 0.1 collective-permute-start.14
  45.8 4.0 %collective-permute-done.11 = bf16[32,3840]{1,0:T(8,128)(2,1)S(1)} collective-permute-done((bf16[32,3840]{1,0:T(8,128)(2,1)S(1)}, bf16[32,3840]{1,0:T(8,128)(2,1)S(1)}, u32[]{:S(2)}, u32[]{:S(2)}) %collective-permute-start.11) | collective-permute-done | bytes 245792 | tf_op jit(solution)/shard_map/ppermute | solution.py:400
  49.8 0.1 add_convert_fusion.5
  49.9 0.3 collective-permute-start.13
  50.2 1.9 %collective-permute-done.14 = bf16[32,3328]{1,0:T(8,128)(2,1)S(1)} collective-permute-done((bf16[32,3328]{1,0:T(8,128)(2,1)S(1)}, bf16[32,3328]{1,0:T(8,128)(2,1)S(1)}, u32[]{:S(2)}, u32[]{:S(2)}) %collective-permute-start.14) | collective-permute-done | bytes 213024 | tf_op jit(solution)/shard_map/ppermute | solution.py:400
  52.1 0.1 add_convert_fusion.7
  52.2 0.9 %collective-permute-start.15 = (bf16[16,3328]{1,0:T(8,128)(2,1)S(1)}, bf16[16,3328]{1,0:T(8,128)(2,1)S(1)}, u32[]{:S(2)}, u32[]{:S(2)}) collective-permute-start(bf16[16,3328]{1,0:T(8,128)(2,1)S(1)} %add_convert_fusion.7), channel_id=1, source_target_pairs={{0,1},{1,0},{2,3},{3,2},{4,5},{5,4},{6,7},{7,6},{8,9},{9,8},{10,11... | collective-permute-start | bytes 319496 | tf_op jit(solution)/shard_map/ppermute | solution.py:400
  53.0 3.5 %collective-permute-done.13 = bf16[16,3840]{1,0:T(8,128)(2,1)S(1)} collective-permute-done((bf16[16,3840]{1,0:T(8,128)(2,1)S(1)}, bf16[16,3840]{1,0:T(8,128)(2,1)S(1)}, u32[]{:S(2)}, u32[]{:S(2)}) %collective-permute-start.13) | collective-permute-done | bytes 122912 | tf_op jit(solution)/shard_map/ppermute | solution.py:400
  56.6 0.1 add_convert_fusion.4
  56.6 0.9 %collective-permute-done.15 = bf16[16,3328]{1,0:T(8,128)(2,1)S(1)} collective-permute-done((bf16[16,3328]{1,0:T(8,128)(2,1)S(1)}, bf16[16,3328]{1,0:T(8,128)(2,1)S(1)}, u32[]{:S(2)}, u32[]{:S(2)}) %collective-permute-start.15) | collective-permute-done | bytes 106528 | tf_op jit(solution)/shard_map/ppermute | solution.py:400
  57.5 0.1 add_convert_fusion.6
  57.6 0.7 %pad_maximum_fusion = bf16[16,7168]{1,0:T(8,128)(2,1)} fusion(bf16[16,3328]{1,0:T(8,128)(2,1)S(1)} %add_convert_fusion.6, bf16[16,3840]{1,0:T(8,128)(2,1)S(1)} %add_convert_fusion.4), kind=kLoop, calls=%fused_computation.6 | loop fusion | flops 458752 | bytes 458752 | tf_op jit(solution)/shard_map/concatenate | solution.py:426
  (5 shorter events, 0.0 us)
Async XLA Ops:
  0.0 4.2 %collective-permute-start = (bf16[64,7168]{1,0:T(8,128)(2,1)}, bf16[64,7168]{1,0:T(8,128)(2,1)S(1)}, u32[]{:S(2)}, u32[]{:S(2)}) collective-permute-start(bf16[64,7168]{1,0:T(8,128)(2,1)} %refs_0_.3), channel_id=1, source_target_pairs={{0,4},{4,0},{8,12},{12,8},{1,5},{5,1},{9,13},{13,9},{2,6},{6,2},{1... | collective-permute-start | bytes 2752520 | tf_op jit(solution)/shard_map/ppermute | solution.py:28
  1.6 9.6 %collective-permute-start.2 = (bf16[64,2048]{1,0:T(8,128)(2,1)S(1)}, bf16[64,2048]{1,0:T(8,128)(2,1)S(1)}, u32[]{:S(2)}, u32[]{:S(2)}) collective-permute-start(bf16[64,2048]{1,0:T(8,128)(2,1)S(1)} %get-tuple-element.37), channel_id=1, source_target_pairs={{0,8},{4,12},{8,0},{12,4},{1,9},{5,13},{9,1},{13,5},{2,10},{6,14},... | collective-permute-start | bytes 786440 | tf_op jit(solution)/shard_map/ppermute | solution.py:28
  8.2 12.1 %collective-permute-start.1 = (bf16[64,3200]{1,0:T(8,128)(2,1)S(1)}, bf16[64,3200]{1,0:T(8,128)(2,1)S(1)}, u32[]{:S(2)}, u32[]{:S(2)}) collective-permute-start(bf16[64,3200]{1,0:T(8,128)(2,1)S(1)} %get-tuple-element.36), channel_id=1, source_target_pairs={{0,8},{4,12},{8,0},{12,4},{1,9},{5,13},{9,1},{13,5},{2,10},{6,14},... | collective-permute-start | bytes 1228808 | tf_op jit(solution)/shard_map/ppermute | solution.py:28
  11.2 8.2 %collective-permute-start.4 = (bf16[64,2048]{1,0:T(8,128)(2,1)S(1)}, bf16[64,2048]{1,0:T(8,128)(2,1)S(1)}, u32[]{:S(2)}, u32[]{:S(2)}) collective-permute-start(bf16[64,2048]{1,0:T(8,128)(2,1)S(1)} %collective-permute-done.2.refs_1_), channel_id=1, source_target_pairs={{0,4},{4,0},{8,12},{12,8},{1,5},{5,1},{9,13},{13,9},{2,6},{6,2},{1... | collective-permute-start | bytes 786440 | tf_op jit(solution)/shard_map/ppermute | solution.py:28
  11.2 9.0 %collective-permute-start.3 = (bf16[64,2048]{1,0:T(8,128)(2,1)S(1)}, bf16[64,2048]{1,0:T(8,128)(2,1)S(1)}, u32[]{:S(2)}, u32[]{:S(2)}) collective-permute-start(bf16[64,2048]{1,0:T(8,128)(2,1)S(1)} %collective-permute-done.2.refs_1_), channel_id=1, source_target_pairs={{0,1},{1,0},{2,3},{3,2},{4,5},{5,4},{6,7},{7,6},{8,9},{9,8},{10,11... | collective-permute-start | bytes 786440 | tf_op jit(solution)/shard_map/ppermute | solution.py:28
  13.2 6.0 %collective-permute-start.5 = (bf16[64,128]{1,0:T(8,128)(2,1)S(1)}, bf16[64,128]{1,0:T(8,128)(2,1)S(1)}, u32[]{:S(2)}, u32[]{:S(2)}) collective-permute-start(bf16[64,128]{1,0:T(8,128)(2,1)S(1)} %get-tuple-element.44.refs_0_), channel_id=1, source_target_pairs={{0,4},{4,0},{8,12},{12,8},{1,5},{5,1},{9,13},{13,9},{2,6},{6,2},{1... | collective-permute-start | bytes 49160 | tf_op jit(solution)/shard_map/ppermute | solution.py:28
  20.2 2.9 %collective-permute-start.7 = (bf16[64,3200]{1,0:T(8,128)(2,1)S(1)}, bf16[64,3200]{1,0:T(8,128)(2,1)S(1)}, u32[]{:S(2)}, u32[]{:S(2)}) collective-permute-start(bf16[64,3200]{1,0:T(8,128)(2,1)S(1)} %collective-permute-done.1.refs_2_.refs_0_), channel_id=1, source_target_pairs={{0,4},{4,0},{8,12},{12,8},{1,5},{5,1},{9,13},{13,9},{2,6},{6,2},{1... | collective-permute-start | bytes 1228808 | tf_op jit(solution)/shard_map/ppermute | solution.py:28
  20.5 1.8 %collective-permute-start.6 = (bf16[64,2048]{1,0:T(8,128)(2,1)S(1)}, bf16[64,2048]{1,0:T(8,128)(2,1)S(1)}, u32[]{:S(2)}, u32[]{:S(2)}) collective-permute-start(bf16[64,2048]{1,0:T(8,128)(2,1)S(1)} %collective-permute-done.3.refs_2_), channel_id=1, source_target_pairs={{0,4},{4,0},{8,12},{12,8},{1,5},{5,1},{9,13},{13,9},{2,6},{6,2},{1... | collective-permute-start | bytes 786440 | tf_op jit(solution)/shard_map/ppermute | solution.py:28
  25.0 2.6 %collective-permute-start.8 = (bf16[128,3840]{1,0:T(8,128)(2,1)S(1)}, bf16[128,3840]{1,0:T(8,128)(2,1)S(1)}, u32[]{:S(2)}, u32[]{:S(2)}) collective-permute-start(bf16[128,3840]{1,0:T(8,128)(2,1)S(1)} %down.4), channel_id=1, source_target_pairs={{0,4},{4,0},{8,12},{12,8},{1,5},{5,1},{9,13},{13,9},{2,6},{6,2},{1... | collective-permute-start | bytes 2949128 | tf_op jit(solution)/shard_map/ppermute | solution.py:28
  25.9 3.6 %collective-permute-start.10 = (bf16[128,3328]{1,0:T(8,128)(2,1)S(1)}, bf16[128,3328]{1,0:T(8,128)(2,1)S(1)}, u32[]{:S(2)}, u32[]{:S(2)}) collective-permute-start(bf16[128,3328]{1,0:T(8,128)(2,1)S(1)} %down.5), channel_id=1, source_target_pairs={{0,4},{4,0},{8,12},{12,8},{1,5},{5,1},{9,13},{13,9},{2,6},{6,2},{1... | collective-permute-start | bytes 2555912 | tf_op jit(solution)/shard_map/ppermute | solution.py:28
  27.7 15.8 %collective-permute-start.9 = (bf16[64,3840]{1,0:T(8,128)(2,1)S(1)}, bf16[64,3840]{1,0:T(8,128)(2,1)S(1)}, u32[]{:S(2)}, u32[]{:S(2)}) collective-permute-start(bf16[64,3840]{1,0:T(8,128)(2,1)S(1)} %add_convert_fusion), channel_id=1, source_target_pairs={{0,1},{1,0},{2,3},{3,2},{4,12},{5,13},{6,14},{7,15},{8,9},{9,8},{1... | collective-permute-start | bytes 1474568 | tf_op jit(solution)/shard_map/ppermute | solution.py:400
  29.6 16.0 %collective-permute-start.12 = (bf16[64,3328]{1,0:T(8,128)(2,1)S(1)}, bf16[64,3328]{1,0:T(8,128)(2,1)S(1)}, u32[]{:S(2)}, u32[]{:S(2)}) collective-permute-start(bf16[64,3328]{1,0:T(8,128)(2,1)S(1)} %add_convert_fusion.1), channel_id=1, source_target_pairs={{0,2},{1,3},{2,0},{3,1},{4,12},{5,13},{6,14},{7,15},{8,10},{9,11},... | collective-permute-start | bytes 1277960 | tf_op jit(solution)/shard_map/ppermute | solution.py:400
  43.6 6.3 %collective-permute-start.11 = (bf16[32,3840]{1,0:T(8,128)(2,1)S(1)}, bf16[32,3840]{1,0:T(8,128)(2,1)S(1)}, u32[]{:S(2)}, u32[]{:S(2)}) collective-permute-start(bf16[32,3840]{1,0:T(8,128)(2,1)S(1)} %add_convert_fusion.2), channel_id=1, source_target_pairs={{0,8},{1,9},{2,10},{3,11},{4,5},{5,4},{6,7},{7,6},{8,0},{9,1},{10,... | collective-permute-start | bytes 737288 | tf_op jit(solution)/shard_map/ppermute | solution.py:400
  45.7 6.4 %collective-permute-start.14 = (bf16[32,3328]{1,0:T(8,128)(2,1)S(1)}, bf16[32,3328]{1,0:T(8,128)(2,1)S(1)}, u32[]{:S(2)}, u32[]{:S(2)}) collective-permute-start(bf16[32,3328]{1,0:T(8,128)(2,1)S(1)} %add_convert_fusion.3), channel_id=1, source_target_pairs={{0,8},{1,9},{2,10},{3,11},{4,6},{5,7},{6,4},{7,5},{8,0},{9,1},{10,... | collective-permute-start | bytes 638984 | tf_op jit(solution)/shard_map/ppermute | solution.py:400
  49.9 6.7 %collective-permute-start.13 = (bf16[16,3840]{1,0:T(8,128)(2,1)S(1)}, bf16[16,3840]{1,0:T(8,128)(2,1)S(1)}, u32[]{:S(2)}, u32[]{:S(2)}) collective-permute-start(bf16[16,3840]{1,0:T(8,128)(2,1)S(1)} %add_convert_fusion.5), channel_id=1, source_target_pairs={{0,2},{1,3},{2,0},{3,1},{4,6},{5,7},{6,4},{7,5},{8,10},{9,11},{10,... | collective-permute-start | bytes 368648 | tf_op jit(solution)/shard_map/ppermute | solution.py:400
  52.2 5.4 %collective-permute-start.15 = (bf16[16,3328]{1,0:T(8,128)(2,1)S(1)}, bf16[16,3328]{1,0:T(8,128)(2,1)S(1)}, u32[]{:S(2)}, u32[]{:S(2)}) collective-permute-start(bf16[16,3328]{1,0:T(8,128)(2,1)S(1)} %add_convert_fusion.7), channel_id=1, source_target_pairs={{0,1},{1,0},{2,3},{3,2},{4,5},{5,4},{6,7},{7,6},{8,9},{9,8},{10,11... | collective-permute-start | bytes 319496 | tf_op jit(solution)/shard_map/ppermute | solution.py:400

commit v4 on v3

--- a/solution.py
+++ b/solution.py
@@ -9,9 +9,10 @@
 BF16 = jnp.bfloat16
 LANES = 128
 VMEM_LIMIT = 16 << 20
+NEAR_COST = 3_000_000_000
 RUN = 4
 FRONT = 3
-CHUNKS = [(6, ("zyz", "yz")), (5, ("Zyz", "yZ"))]
+CHUNKS = [(17, ('yZ', 'zyz')), (11, ('yz', 'Zyz'))]
 
 
 def bits_of(count):
@@ -193,38 +194,39 @@
             pltpu.SemaphoreType.DMA((len(xs) + steps + len(spans),)),
         ],
         compiler_params=pltpu.CompilerParams(vmem_limit_bytes=VMEM_LIMIT),
+        cost_estimate=pl.CostEstimate(
+            flops=NEAR_COST, bytes_accessed=NEAR_COST // 300, transcendentals=0
+        ),
         name="near",
     )(*operands)
 
 
-def far_step(before, blocks, parts):
-    rows = blocks[0][0].shape[0]
-    count = len(blocks[0])
-    cleans = []
-    for part in parts:
-        if not any(part[2] is c for c in cleans):
-            cleans.append(part[2])
+def add_far(value, clean_ref, x_refs, parts, count):
+    for which, column, start, depth, shift in parts:
+        refs = x_refs[which * count : (which + 1) * count]
+        if shift:
+            start = pl.multiple_of(start + (lax.axis_index("exp") % 2) * shift, LANES)
+        x = jnp.concatenate([ref[:, pl.ds(column, depth)] for ref in refs], axis=0)
+        term = jnp.dot(x, clean_ref[pl.ds(start, depth), :], preferred_element_type=F32)
+        value = term if value is None else value + term
+    return value
+
+
+def far_step(before, clean, blocks, parts):
+    rows, count = blocks[0][0].shape[0], len(blocks[0])
+    first = [] if before is None else [before]
 
     def body(*refs):
-        refs, out_ref = list(refs[:-1]), refs[-1]
-        value = None if before is None else refs.pop(0)[...]
-        clean_refs, refs = refs[: len(cleans)], refs[len(cleans) :]
-        for which, column, clean, start, depth, shift in parts:
-            clean_ref = clean_refs[[c is clean for c in cleans].index(True)]
-            x_refs = refs[which * count : (which + 1) * count]
-            if shift:
-                start = pl.multiple_of(start + (lax.axis_index("exp") % 2) * shift, LANES)
-            x = jnp.concatenate([ref[:, pl.ds(column, depth)] for ref in x_refs], axis=0)
-            term = jnp.dot(x, clean_ref[pl.ds(start, depth), :], preferred_element_type=F32)
-            value = term if value is None else value + term
-        out_ref[...] = value
-
-    operands = ([] if before is None else [before]) + cleans + [x for xs in blocks for x in xs]
+        value = None if before is None else refs[0][...]
+        clean_ref, x_refs = refs[len(first)], refs[len(first) + 1 : -1]
+        refs[-1][...] = add_far(value, clean_ref, x_refs, parts, count)
+
+    operands = first + [clean] + [x for xs in blocks for x in xs]
     return pl.pallas_call(
         body,
         in_specs=[whole()] * len(operands),
         out_specs=whole(),
-        out_shape=jax.ShapeDtypeStruct((count * rows, cleans[0].shape[1]), F32),
+        out_shape=jax.ShapeDtypeStruct((count * rows, clean.shape[1]), F32),
         compiler_params=pltpu.CompilerParams(vmem_limit_bytes=VMEM_LIMIT),
         name="far",
     )(*operands)
@@ -269,17 +271,20 @@
     )(acc, *tables)
 
 
-def far_gated(near_rows, acc, tables, hidden, plans, order):
+def far_gated(near_rows, acc, clean, blocks, far_parts, tables, hidden, plans, order):
     rows, count = tables[0].shape[0], near_rows.shape[0]
     total = count + acc.shape[0]
     parts = 1 << sum(axis == "exp" for axis, _ in plans[0][0])
     part, bits = rows // parts, len(plans[0][0])
     at_of = {r: i for i, r in enumerate(order)}
-
-    def body(near_ref, acc_ref, *refs):
-        outs, work = refs[len(tables) : -1], refs[-1]
+    xs = [x for block in blocks for x in block]
+
+    def body(near_ref, acc_ref, clean_ref, *refs):
+        x_refs, refs = refs[: len(xs)], refs[len(xs) :]
+        table_refs, outs, (work, sums) = refs[: len(tables)], refs[len(tables) : -2], refs[-2:]
+        sums[...] = add_far(acc_ref[...], clean_ref, x_refs, far_parts, len(blocks[0]))
         work[pl.ds(0, count), :] = near_ref[...]
-        work[pl.ds(count, total - count), :] = activate(acc_ref, refs[: len(tables)], hidden)
+        work[pl.ds(count, total - count), :] = activate(sums, table_refs, hidden)
         core, slot = lax.axis_index("grp") % 2, lax.axis_index("exp")
         for routes, out_ref in zip(plans, outs):
             for other in range(2):
@@ -302,13 +307,13 @@
     return pl.pallas_call(
         body,
         grid=(1,),
-        in_specs=[whole(), whole()] + table_specs(tables),
+        in_specs=[whole()] * (3 + len(xs)) + table_specs(tables),
         out_specs=[whole() for _ in plans],
         out_shape=[jax.ShapeDtypeStruct((total, 2 * hidden), BF16) for _ in plans],
-        scratch_shapes=[pltpu.VMEM((total, 2 * hidden), F32)],
+        scratch_shapes=[pltpu.VMEM((total, 2 * hidden), F32), pltpu.VMEM(acc.shape, F32)],
         compiler_params=pltpu.CompilerParams(vmem_limit_bytes=VMEM_LIMIT),
         name="far_gated",
-    )(near_rows, acc, *tables)
+    )(near_rows, acc, clean, *xs, *tables)
 
 
 def down_step(hidden_rows, weights, first, count):
@@ -368,14 +373,13 @@
         held, w_view, near, hidden, unit, FRONT, steps, w_flat, spans
     )
     near_rows = near_gated(near_acc, [table, table_beside], hidden)
-    far_acc = far_step(None, [both(relayed)], [(0, 0, clean, 0, run, run)])
-    direct, passed, far_acc, near_rows = lax.optimization_barrier(
-        (direct, passed, far_acc, near_rows)
-    )
-    passed, direct = both(passed), both(direct)
-    far_acc = far_step(far_acc, [passed], [(0, 0, clean, run, run, -run)])
-    direct[-1] = after(direct[-1], far_acc)
-    far_acc = far_step(far_acc, [direct], [(0, 0, clean, 2 * run, features - 2 * run, 0)])
+    direct, near_rows = lax.optimization_barrier((direct, near_rows))
+    direct = both(direct)
+    far_acc = far_step(None, clean, [both(relayed)], [(0, 0, 0, run, run)])
+    passed, far_acc = lax.optimization_barrier((passed, far_acc))
+    passed = both(passed)
+    far_acc = far_step(far_acc, clean, [direct], [(0, 0, 2 * run, features - 2 * run, 0)])
+    passed[-1] = after(passed[-1], far_acc)
 
     grp_stages = [("grp", b) for b in range(1, group_bits)]
     exp_stages = [("exp", b) for b in range(part_bits)]
@@ -388,7 +392,10 @@
     }
     plans = [[by_name[name] for name in names] for _, names in CHUNKS]
     order = [0, 1] + list(range(2, groups, 2)) + list(range(3, groups, 2))
-    all_rows = far_gated(near_rows, far_acc, direct, hidden, plans, order)
+    last_parts = [(0, 0, run, run, -run)]
+    all_rows = far_gated(
+        near_rows, far_acc, clean, [passed], last_parts, direct, hidden, plans, order
+    )
 
     def turn(x, routes, stage):
         pairs = []

time: 58.5 us -> 55.8 us (0.954)
  waiting for transfers between devices: 24.8 us -> 19 us
  starting transfers between devices: 15.8 us -> 19 us
    ppermute x6, waiting for transfers between devices: 21.5 us -> 15.9 us  [turn(): return lax.ppermute(x, ('grp', 'exp'), pairs)]
    ppermute x6, starting transfers between devices: 7.81 us -> 11.2 us  [turn(): return lax.ppermute(x, ('grp', 'exp'), pairs)]
    pallas_call x3 -> x2, Pallas kernels: 2.44 us -> 1.71 us  [far_step(): pl.pallas_call(body, in_specs=[whole()] * len(operands), out_specs=whole(...]
    pallas_call x1, Pallas kernels: 0.19 us -> 0.82 us  [far_gated(): pl.pallas_call(body, grid=(1,), in_specs=[whole()] * (3 + len(xs)) + tabl...]
  transfers between devices with their start and end apart: 16 -> 16, of which waited for: 9 -> 9; matrix products, arithmetic and copies ran while one was open for 1% -> 1% of each run, Pallas kernels for 25% -> 26%
where the time goes in v4:
time: 55.8 us; the launch traced here: 55.7 us
  starting transfers between devices  19 us (34%)
  waiting for transfers between devices  19 us (34%)
  Pallas kernels  16.1 us (29%)
  other arithmetic  1.39 us (2%)
    ppermute x6, waiting for transfers between devices, turn(): return lax.ppermute(x, ('grp', 'exp'), pairs)  15.9 us
    ppermute x6, starting transfers between devices, turn(): return lax.ppermute(x, ('grp', 'exp'), pairs)  11.2 us
    pallas_call x2, Pallas kernels, near_step(): pl.pallas_call(body, in_specs=specs, out_specs=[whole()] * len(shapes), o...  9.74 us
    ppermute x10, starting transfers between devices, exchange(): lax.ppermute(x, axis, [(i, i ^ mask) for i in range(lax.axis_size(axis))])  7.79 us
    ppermute x10, waiting for transfers between devices, exchange(): lax.ppermute(x, axis, [(i, i ^ mask) for i in range(lax.axis_size(axis))])  3.07 us
    pallas_call x4, Pallas kernels, down_step(): pl.pallas_call(body, in_specs=[whole(), whole()], out_specs=whole(), out_...  2.59 us
    pallas_call x2, Pallas kernels, far_step(): pl.pallas_call(body, in_specs=[whole()] * len(operands), out_specs=whole(...  1.71 us
    pallas_call x1, Pallas kernels, prepare(): pl.pallas_call(body, in_specs=[whole(pl.ANY)] * 3, out_specs=[whole()] *...  1.14 us
  transfers between devices with their start and end apart: 16, of which 9 were waited for; matrix products, arithmetic and copies ran while one was open for 1% of the time, Pallas kernels for 26%

profile of v4, /device:TPU:0, one launch (start us, length us, event | category | flops | bytes accessed | tf_op | source)
XLA Modules:
  0.0 55.7 jit_solution(16696522597562109298)
XLA Ops:
  0.0 0.5 collective-permute-start
  0.5 1.1 %prepare.1 = (bf16[64,2048]{1,0:T(8,128)(2,1)S(1)}, bf16[64,3200]{1,0:T(8,128)(2,1)S(1)}, bf16[64,128]{1,0:T(8,128)(2,1)S(1)}) custom-call(bf16[64,7168]{1,0:T(8,128)(2,1)} %refs_0_.3, s32[2,64]{1,0:T(2,128)} %bitcast.11, bf16[4,64]{1,0:T(4,128)(2,1)} %bitcast.12), custom_call_target="tpu_custom_call" | custom-call | tf_op jit(solution)/shard_map/prepare/pallas_call | solution.py:78
  1.6 2.6 %collective-permute-start.2 = (bf16[64,2048]{1,0:T(8,128)(2,1)S(1)}, bf16[64,2048]{1,0:T(8,128)(2,1)S(1)}, u32[]{:S(2)}, u32[]{:S(2)}) collective-permute-start(bf16[64,2048]{1,0:T(8,128)(2,1)S(1)} %get-tuple-element.37), channel_id=1, source_target_pairs={{0,8},{4,12},{8,0},{12,4},{1,9},{5,13},{9,1},{13,5},{2,10},{6,14},... | collective-permute-start | bytes 786440 | tf_op jit(solution)/shard_map/ppermute | solution.py:29
  4.2 0.0 collective-permute-done.refs_1_
  4.2 4.0 %near.2 = (f32[128,1024]{1,0:T(8,128)S(1)}, bf16[7168,1024]{1,0:T(8,128)(2,1)S(1)}) custom-call(bf16[64,7168]{1,0:T(8,128)(2,1)} %refs_0_.3, bf16[64,7168]{1,0:T(8,128)(2,1)S(1)} %collective-permute-done.refs_1_, bf16[2,28672,128]{2,1,0:T(8,128)(2,1)} %bitcast.8), custom_call_target="tpu_custom_call" | custom-call | flops 3000000000 | bytes 10000000 | tf_op jit(solution)/shard_map/near/pallas_call | solution.py:185
  8.2 1.5 %collective-permute-start.1 = (bf16[64,3200]{1,0:T(8,128)(2,1)S(1)}, bf16[64,3200]{1,0:T(8,128)(2,1)S(1)}, u32[]{:S(2)}, u32[]{:S(2)}) collective-permute-start(bf16[64,3200]{1,0:T(8,128)(2,1)S(1)} %get-tuple-element.36), channel_id=1, source_target_pairs={{0,8},{4,12},{8,0},{12,4},{1,9},{5,13},{9,1},{13,5},{2,10},{6,14},... | collective-permute-start | bytes 1228808 | tf_op jit(solution)/shard_map/ppermute | solution.py:29
  9.7 0.0 collective-permute-start.3
  9.7 1.5 %collective-permute-done.2.refs_1_ = bf16[64,2048]{1,0:T(8,128)(2,1)S(1)} collective-permute-done((bf16[64,2048]{1,0:T(8,128)(2,1)S(1)}, bf16[64,2048]{1,0:T(8,128)(2,1)S(1)}, u32[]{:S(2)}, u32[]{:S(2)}) %collective-permute-start.2) | collective-permute-done | bytes 262176 | tf_op jit(solution)/shard_map/ppermute | solution.py:29
  11.2 2.0 %collective-permute-start.4 = (bf16[64,2048]{1,0:T(8,128)(2,1)S(1)}, bf16[64,2048]{1,0:T(8,128)(2,1)S(1)}, u32[]{:S(2)}, u32[]{:S(2)}) collective-permute-start(bf16[64,2048]{1,0:T(8,128)(2,1)S(1)} %collective-permute-done.2.refs_1_), channel_id=1, source_target_pairs={{0,1},{1,0},{2,3},{3,2},{4,5},{5,4},{6,7},{7,6},{8,9},{9,8},{10,11... | collective-permute-start | bytes 786440 | tf_op jit(solution)/shard_map/ppermute | solution.py:29
  13.2 0.0 collective-permute-start.5
  13.2 5.8 %near.3 = (f32[128,1024]{1,0:T(8,128)S(1)}, bf16[7168,1024]{1,0:T(8,128)(2,1)S(1)}, bf16[512,4352]{1,0:T(8,128)(2,1)S(1)}, bf16[512,2816]{1,0:T(8,128)(2,1)S(1)}) custom-call(bf16[64,7168]{1,0:T(8,128)(2,1)} %refs_0_.3, bf16[64,7168]{1,0:T(8,128)(2,1)S(1)} %collective-permute-done.refs_1_, ...), custom_call_target="tpu_custom_call", output_to_operand_aliasing={{0}: (4, {}), {1}: (5, {})} | custom-call | flops 3000000000 | bytes 10000000 | tf_op jit(solution)/shard_map/near/pallas_call | solution.py:185
  19.0 0.0 collective-permute-done.3.refs_1_
  19.0 0.1 near_gated.1.near_ref
  19.2 0.8 %collective-permute-done.1.refs_2_ = bf16[64,3200]{1,0:T(8,128)(2,1)S(1)} collective-permute-done((bf16[64,3200]{1,0:T(8,128)(2,1)S(1)}, bf16[64,3200]{1,0:T(8,128)(2,1)S(1)}, u32[]{:S(2)}, u32[]{:S(2)}) %collective-permute-start.1) | collective-permute-done | bytes 409632 | tf_op jit(solution)/shard_map/ppermute | solution.py:29
  19.9 0.0 collective-permute-start.6
  19.9 0.0 collective-permute-done.5.refs_2_
  19.9 0.7 %far.2.refs_0_ = f32[128,1024]{1,0:T(8,128)S(1)} custom-call(bf16[7168,1024]{1,0:T(8,128)(2,1)S(1)} %get-tuple-element.45.refs_0_.refs_1_.clean_ref, bf16[64,2048]{1,0:T(8,128)(2,1)S(1)} %collective-permute-done.2.refs_1_, bf16[64,2048]{1,0:T(8,128)(2,1)S(1)} %collective-permute-done.5.refs_2_), custom_call_target="tpu_custom_call" | custom-call | tf_op jit(solution)/shard_map/far/pallas_call | solution.py:225
  20.7 0.6 %collective-permute-start.7 = (bf16[64,2048]{1,0:T(8,128)(2,1)S(1)}, bf16[64,2048]{1,0:T(8,128)(2,1)S(1)}, u32[]{:S(2)}, u32[]{:S(2)}) collective-permute-start(bf16[64,2048]{1,0:T(8,128)(2,1)S(1)} %collective-permute-done.4.refs_0_), channel_id=1, source_target_pairs={{0,4},{4,0},{8,12},{12,8},{1,5},{5,1},{9,13},{13,9},{2,6},{6,2},{1... | collective-permute-start | bytes 786440 | tf_op jit(solution)/shard_map/ppermute | solution.py:29
  21.3 0.4 collective-permute-done.6.refs_3_
  21.7 1.0 %far.3.acc_ref = f32[128,1024]{1,0:T(8,128)S(1)} custom-call(f32[128,1024]{1,0:T(8,128)S(1)} %far.2.refs_0_, bf16[7168,1024]{1,0:T(8,128)(2,1)S(1)} %get-tuple-element.45.refs_0_.refs_1_.clean_ref, bf16[64,3200]{1,0:T(8,128)(2,1)S(1)} %collective-permute-done.1.refs_2_, bf16[64,3200]{1,0:T(8,128)(2,1)S(1)} %collective-permute-done.6.refs_3_), custom_call_target="tpu_custom_call" | custom-call | tf_op jit(solution)/shard_map/far/pallas_call | solution.py:225
  22.7 0.0 collective-permute-done.7.refs_1_
  22.7 0.8 %far_gated.1 = (bf16[256,512]{1,0:T(8,128)(2,1)S(1)}, bf16[256,512]{1,0:T(8,128)(2,1)S(1)}) custom-call(f32[128,512]{1,0:T(8,128)S(1)} %near_gated.1.near_ref, f32[128,1024]{1,0:T(8,128)S(1)} %far.3.acc_ref, bf16[7168,1024]{1,0:T(8,128)(2,1)S(1)} %get-tuple-element.45.refs_0_.refs_1_.clean_ref, bf16[64,2048]{1,0:T(8,128)(2,1)S(1)} %collective-permute-done.4.refs_0_, ...), custom_call_target="tpu_custom_call" | custom-call | tf_op jit(solution)/shard_map/far_gated/pallas_call | solution.py:307
  23.5 0.7 %down.4 = bf16[128,4352]{1,0:T(8,128)(2,1)S(1)} custom-call(bf16[256,512]{1,0:T(8,128)(2,1)S(1)} %get-tuple-element.55.h_ref, bf16[512,4352]{1,0:T(8,128)(2,1)S(1)} %get-tuple-element.51.w_ref), custom_call_target="tpu_custom_call" | custom-call | tf_op jit(solution)/shard_map/down/pallas_call | solution.py:325
  24.3 0.2 collective-permute-start.8
  24.5 0.5 down.5
  25.0 0.4 collective-permute-start.10
  25.5 0.7 %down.6 = bf16[128,4352]{1,0:T(8,128)(2,1)S(1)} custom-call(bf16[256,512]{1,0:T(8,128)(2,1)S(1)} %get-tuple-element.55.h_ref, bf16[512,4352]{1,0:T(8,128)(2,1)S(1)} %get-tuple-element.51.w_ref), custom_call_target="tpu_custom_call" | custom-call | tf_op jit(solution)/shard_map/down/pallas_call | solution.py:325
  26.2 0.5 down.7
  26.8 0.3 collective-permute-done.8
  27.1 0.1 add_convert_fusion
  27.2 1.8 %collective-permute-start.9 = (bf16[64,4352]{1,0:T(8,128)(2,1)S(1)}, bf16[64,4352]{1,0:T(8,128)(2,1)S(1)}, u32[]{:S(2)}, u32[]{:S(2)}) collective-permute-start(bf16[64,4352]{1,0:T(8,128)(2,1)S(1)} %add_convert_fusion), channel_id=1, source_target_pairs={{0,8},{1,9},{2,10},{3,11},{4,5},{5,4},{6,7},{7,6},{8,0},{9,1},{10,... | collective-permute-start | bytes 1671176 | tf_op jit(solution)/shard_map/ppermute | solution.py:407
  29.0 0.1 add_convert_fusion.1
  29.1 0.9 %collective-permute-start.12 = (bf16[64,2816]{1,0:T(8,128)(2,1)S(1)}, bf16[64,2816]{1,0:T(8,128)(2,1)S(1)}, u32[]{:S(2)}, u32[]{:S(2)}) collective-permute-start(bf16[64,2816]{1,0:T(8,128)(2,1)S(1)} %add_convert_fusion.1), channel_id=1, source_target_pairs={{0,8},{1,9},{2,10},{3,11},{4,6},{5,7},{6,4},{7,5},{8,0},{9,1},{10,... | collective-permute-start | bytes 1081352 | tf_op jit(solution)/shard_map/ppermute | solution.py:407
  30.0 6.8 %collective-permute-done.9 = bf16[64,4352]{1,0:T(8,128)(2,1)S(1)} collective-permute-done((bf16[64,4352]{1,0:T(8,128)(2,1)S(1)}, bf16[64,4352]{1,0:T(8,128)(2,1)S(1)}, u32[]{:S(2)}, u32[]{:S(2)}) %collective-permute-start.9) | collective-permute-done | bytes 557088 | tf_op jit(solution)/shard_map/ppermute | solution.py:407
  36.8 0.1 add_convert_fusion.2
  36.9 2.9 %collective-permute-start.11 = (bf16[32,4352]{1,0:T(8,128)(2,1)S(1)}, bf16[32,4352]{1,0:T(8,128)(2,1)S(1)}, u32[]{:S(2)}, u32[]{:S(2)}) collective-permute-start(bf16[32,4352]{1,0:T(8,128)(2,1)S(1)} %add_convert_fusion.2), channel_id=1, source_target_pairs={{0,2},{1,3},{2,0},{3,1},{4,12},{5,13},{6,14},{7,15},{8,10},{9,11},... | collective-permute-start | bytes 835592 | tf_op jit(solution)/shard_map/ppermute | solution.py:407
  39.8 0.9 %collective-permute-done.12 = bf16[64,2816]{1,0:T(8,128)(2,1)S(1)} collective-permute-done((bf16[64,2816]{1,0:T(8,128)(2,1)S(1)}, bf16[64,2816]{1,0:T(8,128)(2,1)S(1)}, u32[]{:S(2)}, u32[]{:S(2)}) %collective-permute-start.12) | collective-permute-done | bytes 360480 | tf_op jit(solution)/shard_map/ppermute | solution.py:407
  40.7 0.1 add_convert_fusion.3
  40.8 1.9 %collective-permute-start.14 = (bf16[32,2816]{1,0:T(8,128)(2,1)S(1)}, bf16[32,2816]{1,0:T(8,128)(2,1)S(1)}, u32[]{:S(2)}, u32[]{:S(2)}) collective-permute-start(bf16[32,2816]{1,0:T(8,128)(2,1)S(1)} %add_convert_fusion.3), channel_id=1, source_target_pairs={{0,1},{1,0},{2,3},{3,2},{4,12},{5,13},{6,14},{7,15},{8,9},{9,8},{1... | collective-permute-start | bytes 540680 | tf_op jit(solution)/shard_map/ppermute | solution.py:407
  42.7 5.5 %collective-permute-done.11 = bf16[32,4352]{1,0:T(8,128)(2,1)S(1)} collective-permute-done((bf16[32,4352]{1,0:T(8,128)(2,1)S(1)}, bf16[32,4352]{1,0:T(8,128)(2,1)S(1)}, u32[]{:S(2)}, u32[]{:S(2)}) %collective-permute-start.11) | collective-permute-done | bytes 278560 | tf_op jit(solution)/shard_map/ppermute | solution.py:407
  48.2 0.1 add_convert_fusion.5
  48.3 0.3 collective-permute-start.13
  48.5 0.1 collective-permute-done.14
  48.7 3.4 %collective-permute-start.15 = (bf16[16,2816]{1,0:T(8,128)(2,1)S(1)}, bf16[16,2816]{1,0:T(8,128)(2,1)S(1)}, u32[]{:S(2)}, u32[]{:S(2)}) collective-permute-start(bf16[16,2816]{1,0:T(8,128)(2,1)S(1)} %add_convert_fusion.7), channel_id=1, source_target_pairs={{0,2},{1,3},{2,0},{3,1},{4,5},{5,4},{6,7},{7,6},{8,10},{9,11},{10,... | collective-permute-start | bytes 270344 | tf_op jit(solution)/shard_map/ppermute | solution.py:407
  52.1 2.7 %collective-permute-done.13 = bf16[16,4352]{1,0:T(8,128)(2,1)S(1)} collective-permute-done((bf16[16,4352]{1,0:T(8,128)(2,1)S(1)}, bf16[16,4352]{1,0:T(8,128)(2,1)S(1)}, u32[]{:S(2)}, u32[]{:S(2)}) %collective-permute-start.13) | collective-permute-done | bytes 139296 | tf_op jit(solution)/shard_map/ppermute | solution.py:407
  54.8 0.1 add_convert_fusion.4
  54.9 0.1 add_convert_fusion.6
  55.0 0.7 %pad_maximum_fusion = bf16[16,7168]{1,0:T(8,128)(2,1)} fusion(bf16[16,2816]{1,0:T(8,128)(2,1)S(1)} %add_convert_fusion.6, bf16[16,4352]{1,0:T(8,128)(2,1)S(1)} %add_convert_fusion.4), kind=kLoop, calls=%fused_computation.6 | loop fusion | flops 458752 | bytes 458752 | tf_op jit(solution)/shard_map/concatenate | solution.py:433
  (4 shorter events, 0.1 us)
Async XLA Ops:
  0.0 4.2 %collective-permute-start = (bf16[64,7168]{1,0:T(8,128)(2,1)}, bf16[64,7168]{1,0:T(8,128)(2,1)S(1)}, u32[]{:S(2)}, u32[]{:S(2)}) collective-permute-start(bf16[64,7168]{1,0:T(8,128)(2,1)} %refs_0_.3), channel_id=1, source_target_pairs={{0,4},{4,0},{8,12},{12,8},{1,5},{5,1},{9,13},{13,9},{2,6},{6,2},{1... | collective-permute-start | bytes 2752520 | tf_op jit(solution)/shard_map/ppermute | solution.py:29
  1.6 9.6 %collective-permute-start.2 = (bf16[64,2048]{1,0:T(8,128)(2,1)S(1)}, bf16[64,2048]{1,0:T(8,128)(2,1)S(1)}, u32[]{:S(2)}, u32[]{:S(2)}) collective-permute-start(bf16[64,2048]{1,0:T(8,128)(2,1)S(1)} %get-tuple-element.37), channel_id=1, source_target_pairs={{0,8},{4,12},{8,0},{12,4},{1,9},{5,13},{9,1},{13,5},{2,10},{6,14},... | collective-permute-start | bytes 786440 | tf_op jit(solution)/shard_map/ppermute | solution.py:29
  8.2 11.8 %collective-permute-start.1 = (bf16[64,3200]{1,0:T(8,128)(2,1)S(1)}, bf16[64,3200]{1,0:T(8,128)(2,1)S(1)}, u32[]{:S(2)}, u32[]{:S(2)}) collective-permute-start(bf16[64,3200]{1,0:T(8,128)(2,1)S(1)} %get-tuple-element.36), channel_id=1, source_target_pairs={{0,8},{4,12},{8,0},{12,4},{1,9},{5,13},{9,1},{13,5},{2,10},{6,14},... | collective-permute-start | bytes 1228808 | tf_op jit(solution)/shard_map/ppermute | solution.py:29
  9.7 9.3 %collective-permute-start.3 = (bf16[64,128]{1,0:T(8,128)(2,1)S(1)}, bf16[64,128]{1,0:T(8,128)(2,1)S(1)}, u32[]{:S(2)}, u32[]{:S(2)}) collective-permute-start(bf16[64,128]{1,0:T(8,128)(2,1)S(1)} %get-tuple-element.42.refs_0_), channel_id=1, source_target_pairs={{0,4},{4,0},{8,12},{12,8},{1,5},{5,1},{9,13},{13,9},{2,6},{6,2},{1... | collective-permute-start | bytes 49160 | tf_op jit(solution)/shard_map/ppermute | solution.py:29
  11.2 9.5 %collective-permute-start.4 = (bf16[64,2048]{1,0:T(8,128)(2,1)S(1)}, bf16[64,2048]{1,0:T(8,128)(2,1)S(1)}, u32[]{:S(2)}, u32[]{:S(2)}) collective-permute-start(bf16[64,2048]{1,0:T(8,128)(2,1)S(1)} %collective-permute-done.2.refs_1_), channel_id=1, source_target_pairs={{0,1},{1,0},{2,3},{3,2},{4,5},{5,4},{6,7},{7,6},{8,9},{9,8},{10,11... | collective-permute-start | bytes 786440 | tf_op jit(solution)/shard_map/ppermute | solution.py:29
  13.2 6.7 %collective-permute-start.5 = (bf16[64,2048]{1,0:T(8,128)(2,1)S(1)}, bf16[64,2048]{1,0:T(8,128)(2,1)S(1)}, u32[]{:S(2)}, u32[]{:S(2)}) collective-permute-start(bf16[64,2048]{1,0:T(8,128)(2,1)S(1)} %collective-permute-done.2.refs_1_), channel_id=1, source_target_pairs={{0,4},{4,0},{8,12},{12,8},{1,5},{5,1},{9,13},{13,9},{2,6},{6,2},{1... | collective-permute-start | bytes 786440 | tf_op jit(solution)/shard_map/ppermute | solution.py:29
  19.9 1.7 %collective-permute-start.6 = (bf16[64,3200]{1,0:T(8,128)(2,1)S(1)}, bf16[64,3200]{1,0:T(8,128)(2,1)S(1)}, u32[]{:S(2)}, u32[]{:S(2)}) collective-permute-start(bf16[64,3200]{1,0:T(8,128)(2,1)S(1)} %collective-permute-done.1.refs_2_), channel_id=1, source_target_pairs={{0,4},{4,0},{8,12},{12,8},{1,5},{5,1},{9,13},{13,9},{2,6},{6,2},{1... | collective-permute-start | bytes 1228808 | tf_op jit(solution)/shard_map/ppermute | solution.py:29
  20.7 2.0 %collective-permute-start.7 = (bf16[64,2048]{1,0:T(8,128)(2,1)S(1)}, bf16[64,2048]{1,0:T(8,128)(2,1)S(1)}, u32[]{:S(2)}, u32[]{:S(2)}) collective-permute-start(bf16[64,2048]{1,0:T(8,128)(2,1)S(1)} %collective-permute-done.4.refs_0_), channel_id=1, source_target_pairs={{0,4},{4,0},{8,12},{12,8},{1,5},{5,1},{9,13},{13,9},{2,6},{6,2},{1... | collective-permute-start | bytes 786440 | tf_op jit(solution)/shard_map/ppermute | solution.py:29
  24.3 2.8 %collective-permute-start.8 = (bf16[128,4352]{1,0:T(8,128)(2,1)S(1)}, bf16[128,4352]{1,0:T(8,128)(2,1)S(1)}, u32[]{:S(2)}, u32[]{:S(2)}) collective-permute-start(bf16[128,4352]{1,0:T(8,128)(2,1)S(1)} %down.4), channel_id=1, source_target_pairs={{0,4},{4,0},{8,12},{12,8},{1,5},{5,1},{9,13},{13,9},{2,6},{6,2},{1... | collective-permute-start | bytes 3342344 | tf_op jit(solution)/shard_map/ppermute | solution.py:29
  25.0 4.0 %collective-permute-start.10 = (bf16[128,2816]{1,0:T(8,128)(2,1)S(1)}, bf16[128,2816]{1,0:T(8,128)(2,1)S(1)}, u32[]{:S(2)}, u32[]{:S(2)}) collective-permute-start(bf16[128,2816]{1,0:T(8,128)(2,1)S(1)} %down.5), channel_id=1, source_target_pairs={{0,4},{4,0},{8,12},{12,8},{1,5},{5,1},{9,13},{13,9},{2,6},{6,2},{1... | collective-permute-start | bytes 2162696 | tf_op jit(solution)/shard_map/ppermute | solution.py:29
  27.2 9.6 %collective-permute-start.9 = (bf16[64,4352]{1,0:T(8,128)(2,1)S(1)}, bf16[64,4352]{1,0:T(8,128)(2,1)S(1)}, u32[]{:S(2)}, u32[]{:S(2)}) collective-permute-start(bf16[64,4352]{1,0:T(8,128)(2,1)S(1)} %add_convert_fusion), channel_id=1, source_target_pairs={{0,8},{1,9},{2,10},{3,11},{4,5},{5,4},{6,7},{7,6},{8,0},{9,1},{10,... | collective-permute-start | bytes 1671176 | tf_op jit(solution)/shard_map/ppermute | solution.py:407
  29.1 11.6 %collective-permute-start.12 = (bf16[64,2816]{1,0:T(8,128)(2,1)S(1)}, bf16[64,2816]{1,0:T(8,128)(2,1)S(1)}, u32[]{:S(2)}, u32[]{:S(2)}) collective-permute-start(bf16[64,2816]{1,0:T(8,128)(2,1)S(1)} %add_convert_fusion.1), channel_id=1, source_target_pairs={{0,8},{1,9},{2,10},{3,11},{4,6},{5,7},{6,4},{7,5},{8,0},{9,1},{10,... | collective-permute-start | bytes 1081352 | tf_op jit(solution)/shard_map/ppermute | solution.py:407
  36.9 11.2 %collective-permute-start.11 = (bf16[32,4352]{1,0:T(8,128)(2,1)S(1)}, bf16[32,4352]{1,0:T(8,128)(2,1)S(1)}, u32[]{:S(2)}, u32[]{:S(2)}) collective-permute-start(bf16[32,4352]{1,0:T(8,128)(2,1)S(1)} %add_convert_fusion.2), channel_id=1, source_target_pairs={{0,2},{1,3},{2,0},{3,1},{4,12},{5,13},{6,14},{7,15},{8,10},{9,11},... | collective-permute-start | bytes 835592 | tf_op jit(solution)/shard_map/ppermute | solution.py:407
  40.8 7.8 %collective-permute-start.14 = (bf16[32,2816]{1,0:T(8,128)(2,1)S(1)}, bf16[32,2816]{1,0:T(8,128)(2,1)S(1)}, u32[]{:S(2)}, u32[]{:S(2)}) collective-permute-start(bf16[32,2816]{1,0:T(8,128)(2,1)S(1)} %add_convert_fusion.3), channel_id=1, source_target_pairs={{0,1},{1,0},{2,3},{3,2},{4,12},{5,13},{6,14},{7,15},{8,9},{9,8},{1... | collective-permute-start | bytes 540680 | tf_op jit(solution)/shard_map/ppermute | solution.py:407
  48.3 6.5 %collective-permute-start.13 = (bf16[16,4352]{1,0:T(8,128)(2,1)S(1)}, bf16[16,4352]{1,0:T(8,128)(2,1)S(1)}, u32[]{:S(2)}, u32[]{:S(2)}) collective-permute-start(bf16[16,4352]{1,0:T(8,128)(2,1)S(1)} %add_convert_fusion.5), channel_id=1, source_target_pairs={{0,1},{1,0},{2,3},{3,2},{4,6},{5,7},{6,4},{7,5},{8,9},{9,8},{10,11... | collective-permute-start | bytes 417800 | tf_op jit(solution)/shard_map/ppermute | solution.py:407
  48.7 6.2 %collective-permute-start.15 = (bf16[16,2816]{1,0:T(8,128)(2,1)S(1)}, bf16[16,2816]{1,0:T(8,128)(2,1)S(1)}, u32[]{:S(2)}, u32[]{:S(2)}) collective-permute-start(bf16[16,2816]{1,0:T(8,128)(2,1)S(1)} %add_convert_fusion.7), channel_id=1, source_target_pairs={{0,2},{1,3},{2,0},{3,1},{4,5},{5,4},{6,7},{7,6},{8,10},{9,11},{10,... | collective-permute-start | bytes 270344 | tf_op jit(solution)/shard_map/ppermute | solution.py:407

commit v5 on v4

--- a/solution.py
+++ b/solution.py
@@ -100,7 +100,6 @@
 
 def near_step(xs, w_view, before, hidden, depth, first, last, extra=None, spans=()):
     rows, ratio = xs[0].shape[0], 2 * hidden // LANES
-    features = w_view.shape[1] // ratio
     halves, steps = hidden // LANES, last - first
 
     def body(*refs):
@@ -109,7 +108,7 @@
         if extra is not None:
             extra_ref = refs.pop(0)
         if before is not None:
-            before_ref, _ = refs.pop(0), refs.pop(0)
+            before_ref, made_ref = refs.pop(0), refs.pop(0)
         acc_ref, clean_ref = refs.pop(0), refs.pop(0)
         extra_outs = [refs.pop(0) for _ in spans]
         held, blocks, sems = refs
@@ -142,6 +141,10 @@
             fetch(step).start()
         for copy in pieces:
             copy.start()
+        if before is not None:
+            for step in range(first):
+                here = pl.ds(step * depth, depth)
+                clean_ref[here, :] = made_ref[here, :]
         for step in range(steps):
             fetch(step).wait()
             here = pl.ds((first + step) * depth, depth)
@@ -171,14 +174,12 @@
     if extra is not None:
         operands.append(in_hbm(extra))
         specs.append(whole(pl.ANY))
-    aliases = {}
     if before is not None:
-        aliases = {len(operands): 0, len(operands) + 1: 1}
         operands += before
         specs += [whole()] * 2
     shapes = [
         jax.ShapeDtypeStruct((len(xs) * rows, 4 * hidden), F32),
-        jax.ShapeDtypeStruct((features, 4 * hidden), BF16),
+        jax.ShapeDtypeStruct((last * depth, 4 * hidden), BF16),
     ]
     for _, width in spans:
         shapes.append(jax.ShapeDtypeStruct((extra.shape[0], width), extra.dtype))
@@ -187,7 +188,6 @@
         in_specs=specs,
         out_specs=[whole()] * len(shapes),
         out_shape=shapes,
-        input_output_aliases=aliases,
         scratch_shapes=[
             pltpu.VMEM((len(xs) * rows, steps * depth), BF16),
             pltpu.VMEM((steps, 2, depth * ratio, LANES), BF16),

time: 55.8 us -> 55.8 us (level)
  no operation moved by 1% of the time
where the time goes in v5:
time: 55.8 us; the launch traced here: 55.6 us
  starting transfers between devices  19 us (34%)
  waiting for transfers between devices  19 us (34%)
  Pallas kernels  16.1 us (29%)
  other arithmetic  1.37 us (2%)
    ppermute x6, waiting for transfers between devices, turn(): return lax.ppermute(x, ('grp', 'exp'), pairs)  15.9 us
    ppermute x6, starting transfers between devices, turn(): return lax.ppermute(x, ('grp', 'exp'), pairs)  11.2 us
    pallas_call x2, Pallas kernels, near_step(): pl.pallas_call(body, in_specs=specs, out_specs=[whole()] * len(shapes), o...  9.74 us
    ppermute x10, starting transfers between devices, exchange(): lax.ppermute(x, axis, [(i, i ^ mask) for i in range(lax.axis_size(axis))])  7.79 us
    ppermute x10, waiting for transfers between devices, exchange(): lax.ppermute(x, axis, [(i, i ^ mask) for i in range(lax.axis_size(axis))])  3.07 us
    pallas_call x4, Pallas kernels, down_step(): pl.pallas_call(body, in_specs=[whole(), whole()], out_specs=whole(), out_...  2.59 us
    pallas_call x2, Pallas kernels, far_step(): pl.pallas_call(body, in_specs=[whole()] * len(operands), out_specs=whole(...  1.71 us
    pallas_call x1, Pallas kernels, prepare(): pl.pallas_call(body, in_specs=[whole(pl.ANY)] * 3, out_specs=[whole()] *...  1.14 us
  transfers between devices with their start and end apart: 16, of which 9 were waited for; matrix products, arithmetic and copies ran while one was open for 1% of the time, Pallas kernels for 26%

profile of v5, /device:TPU:0, one launch (start us, length us, event | category | flops | bytes accessed | tf_op | source)
XLA Modules:
  0.0 55.6 jit_solution(13701474603745932323)
XLA Ops:
  0.0 0.5 collective-permute-start
  0.5 1.1 %prepare.1 = (bf16[64,2048]{1,0:T(8,128)(2,1)S(1)}, bf16[64,3200]{1,0:T(8,128)(2,1)S(1)}, bf16[64,128]{1,0:T(8,128)(2,1)S(1)}) custom-call(bf16[64,7168]{1,0:T(8,128)(2,1)} %refs_0_.3, s32[2,64]{1,0:T(2,128)} %bitcast.11, bf16[4,64]{1,0:T(4,128)(2,1)} %bitcast.12), custom_call_target="tpu_custom_call" | custom-call | tf_op jit(solution)/shard_map/prepare/pallas_call | solution.py:78
  1.6 2.6 %collective-permute-start.2 = (bf16[64,2048]{1,0:T(8,128)(2,1)S(1)}, bf16[64,2048]{1,0:T(8,128)(2,1)S(1)}, u32[]{:S(2)}, u32[]{:S(2)}) collective-permute-start(bf16[64,2048]{1,0:T(8,128)(2,1)S(1)} %get-tuple-element.37), channel_id=1, source_target_pairs={{0,8},{4,12},{8,0},{12,4},{1,9},{5,13},{9,1},{13,5},{2,10},{6,14},... | collective-permute-start | bytes 786440 | tf_op jit(solution)/shard_map/ppermute | solution.py:29
  4.2 4.0 %near.2 = (f32[128,1024]{1,0:T(8,128)S(1)}, bf16[3072,1024]{1,0:T(8,128)(2,1)S(1)}) custom-call(bf16[64,7168]{1,0:T(8,128)(2,1)} %refs_0_.3, bf16[64,7168]{1,0:T(8,128)(2,1)S(1)} %collective-permute-done.refs_1_, bf16[2,28672,128]{2,1,0:T(8,128)(2,1)} %bitcast.8), custom_call_target="tpu_custom_call" | custom-call | flops 3000000000 | bytes 10000000 | tf_op jit(solution)/shard_map/near/pallas_call | solution.py:186
  8.2 1.5 %collective-permute-start.1 = (bf16[64,3200]{1,0:T(8,128)(2,1)S(1)}, bf16[64,3200]{1,0:T(8,128)(2,1)S(1)}, u32[]{:S(2)}, u32[]{:S(2)}) collective-permute-start(bf16[64,3200]{1,0:T(8,128)(2,1)S(1)} %get-tuple-element.36), channel_id=1, source_target_pairs={{0,8},{4,12},{8,0},{12,4},{1,9},{5,13},{9,1},{13,5},{2,10},{6,14},... | collective-permute-start | bytes 1228808 | tf_op jit(solution)/shard_map/ppermute | solution.py:29
  9.7 1.5 %collective-permute-done.2.refs_1_ = bf16[64,2048]{1,0:T(8,128)(2,1)S(1)} collective-permute-done((bf16[64,2048]{1,0:T(8,128)(2,1)S(1)}, bf16[64,2048]{1,0:T(8,128)(2,1)S(1)}, u32[]{:S(2)}, u32[]{:S(2)}) %collective-permute-start.2) | collective-permute-done | bytes 262176 | tf_op jit(solution)/shard_map/ppermute | solution.py:29
  11.2 0.0 collective-permute-start.5
  11.2 2.0 %collective-permute-start.4 = (bf16[64,2048]{1,0:T(8,128)(2,1)S(1)}, bf16[64,2048]{1,0:T(8,128)(2,1)S(1)}, u32[]{:S(2)}, u32[]{:S(2)}) collective-permute-start(bf16[64,2048]{1,0:T(8,128)(2,1)S(1)} %collective-permute-done.2.refs_1_), channel_id=1, source_target_pairs={{0,1},{1,0},{2,3},{3,2},{4,5},{5,4},{6,7},{7,6},{8,9},{9,8},{10,11... | collective-permute-start | bytes 786440 | tf_op jit(solution)/shard_map/ppermute | solution.py:29
  13.2 5.8 %near.3 = (f32[128,1024]{1,0:T(8,128)S(1)}, bf16[7168,1024]{1,0:T(8,128)(2,1)S(1)}, bf16[512,4352]{1,0:T(8,128)(2,1)S(1)}, bf16[512,2816]{1,0:T(8,128)(2,1)S(1)}) custom-call(bf16[64,7168]{1,0:T(8,128)(2,1)} %refs_0_.3, bf16[64,7168]{1,0:T(8,128)(2,1)S(1)} %collective-permute-done.refs_1_, bf16[2,28672,128]{2,1,0:T(8,128)(2,1)} %bitcast.9, ...), custom_call_target="tpu_custom_call" | custom-call | flops 3000000000 | bytes 10000000 | tf_op jit(solution)/shard_map/near/pallas_call | solution.py:186
  19.0 0.0 collective-permute-done.3.refs_1_
  19.0 0.1 near_gated.1.near_ref
  19.2 0.8 %collective-permute-done.1.refs_2_ = bf16[64,3200]{1,0:T(8,128)(2,1)S(1)} collective-permute-done((bf16[64,3200]{1,0:T(8,128)(2,1)S(1)}, bf16[64,3200]{1,0:T(8,128)(2,1)S(1)}, u32[]{:S(2)}, u32[]{:S(2)}) %collective-permute-start.1) | collective-permute-done | bytes 409632 | tf_op jit(solution)/shard_map/ppermute | solution.py:29
  19.9 0.0 collective-permute-start.6
  19.9 0.0 collective-permute-done.5.refs_2_
  19.9 0.7 %far.2.refs_0_ = f32[128,1024]{1,0:T(8,128)S(1)} custom-call(bf16[7168,1024]{1,0:T(8,128)(2,1)S(1)} %get-tuple-element.45.refs_0_.refs_1_.clean_ref, bf16[64,2048]{1,0:T(8,128)(2,1)S(1)} %collective-permute-done.2.refs_1_, bf16[64,2048]{1,0:T(8,128)(2,1)S(1)} %collective-permute-done.5.refs_2_), custom_call_target="tpu_custom_call" | custom-call | tf_op jit(solution)/shard_map/far/pallas_call | solution.py:225
  20.7 0.6 %collective-permute-start.7 = (bf16[64,2048]{1,0:T(8,128)(2,1)S(1)}, bf16[64,2048]{1,0:T(8,128)(2,1)S(1)}, u32[]{:S(2)}, u32[]{:S(2)}) collective-permute-start(bf16[64,2048]{1,0:T(8,128)(2,1)S(1)} %collective-permute-done.4.refs_0_), channel_id=1, source_target_pairs={{0,4},{4,0},{8,12},{12,8},{1,5},{5,1},{9,13},{13,9},{2,6},{6,2},{1... | collective-permute-start | bytes 786440 | tf_op jit(solution)/shard_map/ppermute | solution.py:29
  21.3 0.4 collective-permute-done.6.refs_3_
  21.7 1.0 %far.3.acc_ref = f32[128,1024]{1,0:T(8,128)S(1)} custom-call(f32[128,1024]{1,0:T(8,128)S(1)} %far.2.refs_0_, bf16[7168,1024]{1,0:T(8,128)(2,1)S(1)} %get-tuple-element.45.refs_0_.refs_1_.clean_ref, bf16[64,3200]{1,0:T(8,128)(2,1)S(1)} %collective-permute-done.1.refs_2_, bf16[64,3200]{1,0:T(8,128)(2,1)S(1)} %collective-permute-done.6.refs_3_), custom_call_target="tpu_custom_call" | custom-call | tf_op jit(solution)/shard_map/far/pallas_call | solution.py:225
  22.7 0.0 collective-permute-done.7.refs_1_
  22.7 0.8 %far_gated.1 = (bf16[256,512]{1,0:T(8,128)(2,1)S(1)}, bf16[256,512]{1,0:T(8,128)(2,1)S(1)}) custom-call(f32[128,512]{1,0:T(8,128)S(1)} %near_gated.1.near_ref, f32[128,1024]{1,0:T(8,128)S(1)} %far.3.acc_ref, bf16[7168,1024]{1,0:T(8,128)(2,1)S(1)} %get-tuple-element.45.refs_0_.refs_1_.clean_ref, bf16[64,2048]{1,0:T(8,128)(2,1)S(1)} %collective-permute-done.4.refs_0_, ...), custom_call_target="tpu_custom_call" | custom-call | tf_op jit(solution)/shard_map/far_gated/pallas_call | solution.py:307
  23.5 0.7 %down.4 = bf16[128,4352]{1,0:T(8,128)(2,1)S(1)} custom-call(bf16[256,512]{1,0:T(8,128)(2,1)S(1)} %get-tuple-element.55.h_ref, bf16[512,4352]{1,0:T(8,128)(2,1)S(1)} %get-tuple-element.51.w_ref), custom_call_target="tpu_custom_call" | custom-call | tf_op jit(solution)/shard_map/down/pallas_call | solution.py:325
  24.3 0.2 collective-permute-start.8
  24.5 0.5 down.5
  25.0 0.4 collective-permute-start.10
  25.5 0.7 %down.6 = bf16[128,4352]{1,0:T(8,128)(2,1)S(1)} custom-call(bf16[256,512]{1,0:T(8,128)(2,1)S(1)} %get-tuple-element.55.h_ref, bf16[512,4352]{1,0:T(8,128)(2,1)S(1)} %get-tuple-element.51.w_ref), custom_call_target="tpu_custom_call" | custom-call | tf_op jit(solution)/shard_map/down/pallas_call | solution.py:325
  26.2 0.5 down.7
  26.8 0.3 collective-permute-done.8
  27.1 0.1 add_convert_fusion
  27.2 1.8 %collective-permute-start.9 = (bf16[64,4352]{1,0:T(8,128)(2,1)S(1)}, bf16[64,4352]{1,0:T(8,128)(2,1)S(1)}, u32[]{:S(2)}, u32[]{:S(2)}) collective-permute-start(bf16[64,4352]{1,0:T(8,128)(2,1)S(1)} %add_convert_fusion), channel_id=1, source_target_pairs={{0,8},{1,9},{2,10},{3,11},{4,5},{5,4},{6,7},{7,6},{8,0},{9,1},{10,... | collective-permute-start | bytes 1671176 | tf_op jit(solution)/shard_map/ppermute | solution.py:407
  29.0 0.0 collective-permute-done.10
  29.0 0.1 add_convert_fusion.1
  29.1 0.9 %collective-permute-start.12 = (bf16[64,2816]{1,0:T(8,128)(2,1)S(1)}, bf16[64,2816]{1,0:T(8,128)(2,1)S(1)}, u32[]{:S(2)}, u32[]{:S(2)}) collective-permute-start(bf16[64,2816]{1,0:T(8,128)(2,1)S(1)} %add_convert_fusion.1), channel_id=1, source_target_pairs={{0,8},{1,9},{2,10},{3,11},{4,6},{5,7},{6,4},{7,5},{8,0},{9,1},{10,... | collective-permute-start | bytes 1081352 | tf_op jit(solution)/shard_map/ppermute | solution.py:407
  30.0 6.8 %collective-permute-done.9 = bf16[64,4352]{1,0:T(8,128)(2,1)S(1)} collective-permute-done((bf16[64,4352]{1,0:T(8,128)(2,1)S(1)}, bf16[64,4352]{1,0:T(8,128)(2,1)S(1)}, u32[]{:S(2)}, u32[]{:S(2)}) %collective-permute-start.9) | collective-permute-done | bytes 557088 | tf_op jit(solution)/shard_map/ppermute | solution.py:407
  36.8 0.1 add_convert_fusion.2
  36.9 2.9 %collective-permute-start.11 = (bf16[32,4352]{1,0:T(8,128)(2,1)S(1)}, bf16[32,4352]{1,0:T(8,128)(2,1)S(1)}, u32[]{:S(2)}, u32[]{:S(2)}) collective-permute-start(bf16[32,4352]{1,0:T(8,128)(2,1)S(1)} %add_convert_fusion.2), channel_id=1, source_target_pairs={{0,2},{1,3},{2,0},{3,1},{4,12},{5,13},{6,14},{7,15},{8,10},{9,11},... | collective-permute-start | bytes 835592 | tf_op jit(solution)/shard_map/ppermute | solution.py:407
  39.8 0.9 %collective-permute-done.12 = bf16[64,2816]{1,0:T(8,128)(2,1)S(1)} collective-permute-done((bf16[64,2816]{1,0:T(8,128)(2,1)S(1)}, bf16[64,2816]{1,0:T(8,128)(2,1)S(1)}, u32[]{:S(2)}, u32[]{:S(2)}) %collective-permute-start.12) | collective-permute-done | bytes 360480 | tf_op jit(solution)/shard_map/ppermute | solution.py:407
  40.7 0.1 add_convert_fusion.3
  40.8 1.9 %collective-permute-start.14 = (bf16[32,2816]{1,0:T(8,128)(2,1)S(1)}, bf16[32,2816]{1,0:T(8,128)(2,1)S(1)}, u32[]{:S(2)}, u32[]{:S(2)}) collective-permute-start(bf16[32,2816]{1,0:T(8,128)(2,1)S(1)} %add_convert_fusion.3), channel_id=1, source_target_pairs={{0,1},{1,0},{2,3},{3,2},{4,12},{5,13},{6,14},{7,15},{8,9},{9,8},{1... | collective-permute-start | bytes 540680 | tf_op jit(solution)/shard_map/ppermute | solution.py:407
  42.7 5.5 %collective-permute-done.11 = bf16[32,4352]{1,0:T(8,128)(2,1)S(1)} collective-permute-done((bf16[32,4352]{1,0:T(8,128)(2,1)S(1)}, bf16[32,4352]{1,0:T(8,128)(2,1)S(1)}, u32[]{:S(2)}, u32[]{:S(2)}) %collective-permute-start.11) | collective-permute-done | bytes 278560 | tf_op jit(solution)/shard_map/ppermute | solution.py:407
  48.2 0.1 add_convert_fusion.5
  48.3 0.3 collective-permute-start.13
  48.5 0.1 collective-permute-done.14
  48.6 0.1 add_convert_fusion.7
  48.7 3.4 %collective-permute-start.15 = (bf16[16,2816]{1,0:T(8,128)(2,1)S(1)}, bf16[16,2816]{1,0:T(8,128)(2,1)S(1)}, u32[]{:S(2)}, u32[]{:S(2)}) collective-permute-start(bf16[16,2816]{1,0:T(8,128)(2,1)S(1)} %add_convert_fusion.7), channel_id=1, source_target_pairs={{0,2},{1,3},{2,0},{3,1},{4,5},{5,4},{6,7},{7,6},{8,10},{9,11},{10,... | collective-permute-start | bytes 270344 | tf_op jit(solution)/shard_map/ppermute | solution.py:407
  52.1 2.7 %collective-permute-done.13 = bf16[16,4352]{1,0:T(8,128)(2,1)S(1)} collective-permute-done((bf16[16,4352]{1,0:T(8,128)(2,1)S(1)}, bf16[16,4352]{1,0:T(8,128)(2,1)S(1)}, u32[]{:S(2)}, u32[]{:S(2)}) %collective-permute-start.13) | collective-permute-done | bytes 139296 | tf_op jit(solution)/shard_map/ppermute | solution.py:407
  54.8 0.1 add_convert_fusion.4
  54.9 0.1 add_convert_fusion.6
  54.9 0.7 %pad_maximum_fusion = bf16[16,7168]{1,0:T(8,128)(2,1)} fusion(bf16[16,2816]{1,0:T(8,128)(2,1)S(1)} %add_convert_fusion.6, bf16[16,4352]{1,0:T(8,128)(2,1)S(1)} %add_convert_fusion.4), kind=kLoop, calls=%fused_computation.6 | loop fusion | flops 458752 | bytes 458752 | tf_op jit(solution)/shard_map/concatenate | solution.py:433
  (4 shorter events, 0.0 us)
Async XLA Ops:
  0.0 4.2 %collective-permute-start = (bf16[64,7168]{1,0:T(8,128)(2,1)}, bf16[64,7168]{1,0:T(8,128)(2,1)S(1)}, u32[]{:S(2)}, u32[]{:S(2)}) collective-permute-start(bf16[64,7168]{1,0:T(8,128)(2,1)} %refs_0_.3), channel_id=1, source_target_pairs={{0,4},{4,0},{8,12},{12,8},{1,5},{5,1},{9,13},{13,9},{2,6},{6,2},{1... | collective-permute-start | bytes 2752520 | tf_op jit(solution)/shard_map/ppermute | solution.py:29
  1.6 9.6 %collective-permute-start.2 = (bf16[64,2048]{1,0:T(8,128)(2,1)S(1)}, bf16[64,2048]{1,0:T(8,128)(2,1)S(1)}, u32[]{:S(2)}, u32[]{:S(2)}) collective-permute-start(bf16[64,2048]{1,0:T(8,128)(2,1)S(1)} %get-tuple-element.37), channel_id=1, source_target_pairs={{0,8},{4,12},{8,0},{12,4},{1,9},{5,13},{9,1},{13,5},{2,10},{6,14},... | collective-permute-start | bytes 786440 | tf_op jit(solution)/shard_map/ppermute | solution.py:29
  8.2 11.8 %collective-permute-start.1 = (bf16[64,3200]{1,0:T(8,128)(2,1)S(1)}, bf16[64,3200]{1,0:T(8,128)(2,1)S(1)}, u32[]{:S(2)}, u32[]{:S(2)}) collective-permute-start(bf16[64,3200]{1,0:T(8,128)(2,1)S(1)} %get-tuple-element.36), channel_id=1, source_target_pairs={{0,8},{4,12},{8,0},{12,4},{1,9},{5,13},{9,1},{13,5},{2,10},{6,14},... | collective-permute-start | bytes 1228808 | tf_op jit(solution)/shard_map/ppermute | solution.py:29
  9.7 9.4 %collective-permute-start.3 = (bf16[64,128]{1,0:T(8,128)(2,1)S(1)}, bf16[64,128]{1,0:T(8,128)(2,1)S(1)}, u32[]{:S(2)}, u32[]{:S(2)}) collective-permute-start(bf16[64,128]{1,0:T(8,128)(2,1)S(1)} %get-tuple-element.42.refs_0_), channel_id=1, source_target_pairs={{0,4},{4,0},{8,12},{12,8},{1,5},{5,1},{9,13},{13,9},{2,6},{6,2},{1... | collective-permute-start | bytes 49160 | tf_op jit(solution)/shard_map/ppermute | solution.py:29
  11.2 8.7 %collective-permute-start.5 = (bf16[64,2048]{1,0:T(8,128)(2,1)S(1)}, bf16[64,2048]{1,0:T(8,128)(2,1)S(1)}, u32[]{:S(2)}, u32[]{:S(2)}) collective-permute-start(bf16[64,2048]{1,0:T(8,128)(2,1)S(1)} %collective-permute-done.2.refs_1_), channel_id=1, source_target_pairs={{0,4},{4,0},{8,12},{12,8},{1,5},{5,1},{9,13},{13,9},{2,6},{6,2},{1... | collective-permute-start | bytes 786440 | tf_op jit(solution)/shard_map/ppermute | solution.py:29
  11.2 9.5 %collective-permute-start.4 = (bf16[64,2048]{1,0:T(8,128)(2,1)S(1)}, bf16[64,2048]{1,0:T(8,128)(2,1)S(1)}, u32[]{:S(2)}, u32[]{:S(2)}) collective-permute-start(bf16[64,2048]{1,0:T(8,128)(2,1)S(1)} %collective-permute-done.2.refs_1_), channel_id=1, source_target_pairs={{0,1},{1,0},{2,3},{3,2},{4,5},{5,4},{6,7},{7,6},{8,9},{9,8},{10,11... | collective-permute-start | bytes 786440 | tf_op jit(solution)/shard_map/ppermute | solution.py:29
  19.9 1.7 %collective-permute-start.6 = (bf16[64,3200]{1,0:T(8,128)(2,1)S(1)}, bf16[64,3200]{1,0:T(8,128)(2,1)S(1)}, u32[]{:S(2)}, u32[]{:S(2)}) collective-permute-start(bf16[64,3200]{1,0:T(8,128)(2,1)S(1)} %collective-permute-done.1.refs_2_), channel_id=1, source_target_pairs={{0,4},{4,0},{8,12},{12,8},{1,5},{5,1},{9,13},{13,9},{2,6},{6,2},{1... | collective-permute-start | bytes 1228808 | tf_op jit(solution)/shard_map/ppermute | solution.py:29
  20.7 2.0 %collective-permute-start.7 = (bf16[64,2048]{1,0:T(8,128)(2,1)S(1)}, bf16[64,2048]{1,0:T(8,128)(2,1)S(1)}, u32[]{:S(2)}, u32[]{:S(2)}) collective-permute-start(bf16[64,2048]{1,0:T(8,128)(2,1)S(1)} %collective-permute-done.4.refs_0_), channel_id=1, source_target_pairs={{0,4},{4,0},{8,12},{12,8},{1,5},{5,1},{9,13},{13,9},{2,6},{6,2},{1... | collective-permute-start | bytes 786440 | tf_op jit(solution)/shard_map/ppermute | solution.py:29
  24.3 2.8 %collective-permute-start.8 = (bf16[128,4352]{1,0:T(8,128)(2,1)S(1)}, bf16[128,4352]{1,0:T(8,128)(2,1)S(1)}, u32[]{:S(2)}, u32[]{:S(2)}) collective-permute-start(bf16[128,4352]{1,0:T(8,128)(2,1)S(1)} %down.4), channel_id=1, source_target_pairs={{0,4},{4,0},{8,12},{12,8},{1,5},{5,1},{9,13},{13,9},{2,6},{6,2},{1... | collective-permute-start | bytes 3342344 | tf_op jit(solution)/shard_map/ppermute | solution.py:29
  25.0 4.0 %collective-permute-start.10 = (bf16[128,2816]{1,0:T(8,128)(2,1)S(1)}, bf16[128,2816]{1,0:T(8,128)(2,1)S(1)}, u32[]{:S(2)}, u32[]{:S(2)}) collective-permute-start(bf16[128,2816]{1,0:T(8,128)(2,1)S(1)} %down.5), channel_id=1, source_target_pairs={{0,4},{4,0},{8,12},{12,8},{1,5},{5,1},{9,13},{13,9},{2,6},{6,2},{1... | collective-permute-start | bytes 2162696 | tf_op jit(solution)/shard_map/ppermute | solution.py:29
  27.2 9.6 %collective-permute-start.9 = (bf16[64,4352]{1,0:T(8,128)(2,1)S(1)}, bf16[64,4352]{1,0:T(8,128)(2,1)S(1)}, u32[]{:S(2)}, u32[]{:S(2)}) collective-permute-start(bf16[64,4352]{1,0:T(8,128)(2,1)S(1)} %add_convert_fusion), channel_id=1, source_target_pairs={{0,8},{1,9},{2,10},{3,11},{4,5},{5,4},{6,7},{7,6},{8,0},{9,1},{10,... | collective-permute-start | bytes 1671176 | tf_op jit(solution)/shard_map/ppermute | solution.py:407
  29.1 11.6 %collective-permute-start.12 = (bf16[64,2816]{1,0:T(8,128)(2,1)S(1)}, bf16[64,2816]{1,0:T(8,128)(2,1)S(1)}, u32[]{:S(2)}, u32[]{:S(2)}) collective-permute-start(bf16[64,2816]{1,0:T(8,128)(2,1)S(1)} %add_convert_fusion.1), channel_id=1, source_target_pairs={{0,8},{1,9},{2,10},{3,11},{4,6},{5,7},{6,4},{7,5},{8,0},{9,1},{10,... | collective-permute-start | bytes 1081352 | tf_op jit(solution)/shard_map/ppermute | solution.py:407
  36.9 11.3 %collective-permute-start.11 = (bf16[32,4352]{1,0:T(8,128)(2,1)S(1)}, bf16[32,4352]{1,0:T(8,128)(2,1)S(1)}, u32[]{:S(2)}, u32[]{:S(2)}) collective-permute-start(bf16[32,4352]{1,0:T(8,128)(2,1)S(1)} %add_convert_fusion.2), channel_id=1, source_target_pairs={{0,2},{1,3},{2,0},{3,1},{4,12},{5,13},{6,14},{7,15},{8,10},{9,11},... | collective-permute-start | bytes 835592 | tf_op jit(solution)/shard_map/ppermute | solution.py:407
  40.8 7.9 %collective-permute-start.14 = (bf16[32,2816]{1,0:T(8,128)(2,1)S(1)}, bf16[32,2816]{1,0:T(8,128)(2,1)S(1)}, u32[]{:S(2)}, u32[]{:S(2)}) collective-permute-start(bf16[32,2816]{1,0:T(8,128)(2,1)S(1)} %add_convert_fusion.3), channel_id=1, source_target_pairs={{0,1},{1,0},{2,3},{3,2},{4,12},{5,13},{6,14},{7,15},{8,9},{9,8},{1... | collective-permute-start | bytes 540680 | tf_op jit(solution)/shard_map/ppermute | solution.py:407
  48.3 6.5 %collective-permute-start.13 = (bf16[16,4352]{1,0:T(8,128)(2,1)S(1)}, bf16[16,4352]{1,0:T(8,128)(2,1)S(1)}, u32[]{:S(2)}, u32[]{:S(2)}) collective-permute-start(bf16[16,4352]{1,0:T(8,128)(2,1)S(1)} %add_convert_fusion.5), channel_id=1, source_target_pairs={{0,1},{1,0},{2,3},{3,2},{4,6},{5,7},{6,4},{7,5},{8,9},{9,8},{10,11... | collective-permute-start | bytes 417800 | tf_op jit(solution)/shard_map/ppermute | solution.py:407
  48.7 6.2 %collective-permute-start.15 = (bf16[16,2816]{1,0:T(8,128)(2,1)S(1)}, bf16[16,2816]{1,0:T(8,128)(2,1)S(1)}, u32[]{:S(2)}, u32[]{:S(2)}) collective-permute-start(bf16[16,2816]{1,0:T(8,128)(2,1)S(1)} %add_convert_fusion.7), channel_id=1, source_target_pairs={{0,2},{1,3},{2,0},{3,1},{4,5},{5,4},{6,7},{7,6},{8,10},{9,11},{10,... | collective-permute-start | bytes 270344 | tf_op jit(solution)/shard_map/ppermute | solution.py:407

commit v6 on v5

--- a/solution.py
+++ b/solution.py
@@ -332,6 +332,32 @@
     )(hidden_rows, weights)
 
 
+def finish(state, rows):
+    counts = [len(terms) for terms in state]
+
+    def body(*refs):
+        refs, out_ref = list(refs[:-1]), refs[-1]
+        start = 0
+        for count in counts:
+            terms, refs = refs[:count], refs[count:]
+            width = terms[0].shape[1]
+            total = sum(ref[...].astype(F32) for ref in terms)
+            out_ref[:, pl.ds(start, width)] = total.astype(BF16)
+            start += width
+
+    operands = [t for terms in state for t in terms]
+    width = sum(terms[0].shape[1] for terms in state)
+    return pl.pallas_call(
+        body,
+        grid=(1,),
+        in_specs=[pl.BlockSpec((rows, t.shape[1]), lambda i: (0, 0)) for t in operands],
+        out_specs=whole(),
+        out_shape=jax.ShapeDtypeStruct((rows, width), BF16),
+        compiler_params=pltpu.CompilerParams(vmem_limit_bytes=VMEM_LIMIT),
+        name="finish",
+    )(*operands)
+
+
 def local(tokens, group_ids, gates, w_in, w_down):
     groups, parts = lax.axis_size("grp"), lax.axis_size("exp")
     rows, features = tokens.shape
@@ -406,31 +432,27 @@
                 pairs.append((g * parts + e, to_g * parts + to_e))
         return lax.ppermute(x, ("grp", "exp"), pairs)
 
-    state = []
     half = rows * groups // 2
-    done = None
-    for weights, plan_rows in zip(w_flats, all_rows):
-        plan_rows = plan_rows if done is None else after(plan_rows, done)
-        done = down_step(plan_rows, weights, half, half)
-        state.append([exchange(done, "grp", 1)])
-    for weights, plan_rows, terms in zip(w_flats, all_rows, state):
-        done = down_step(after(plan_rows, done), weights, 0, half)
-        terms.append(done)
+    (first_w, second_w), (first_rows, second_rows) = w_flats, all_rows
+    send = down_step(first_rows, first_w, half, half)
+    first_terms = [exchange(send, "grp", 1)]
+    keep = down_step(after(first_rows, send), first_w, 0, half)
+    first_terms.insert(0, keep)
+    send = down_step(after(second_rows, keep), second_w, half, half)
+    second_terms = [exchange(send, "grp", 1)]
+    state = [first_terms, second_terms]
     send = None
     height = half
     for stage in range(len(grp_stages + exp_stages)):
         height //= 2
         for terms, routes in zip(state, plans):
-            if send is not None:
+            if len(terms) == 1:
+                terms.insert(0, down_step(after(second_rows, send), second_w, 0, half))
+            else:
                 terms[-1] = after(terms[-1], send)
             send = add(*[t[height : 2 * height] for t in terms])
             terms.append(turn(send, routes, stage))
-    outs = []
-    for terms in state:
-        if outs:
-            terms[-1] = after(terms[-1], outs[-1])
-        outs.append(add(*[t[:height] for t in terms]))
-    return jnp.concatenate(outs, axis=1)
+    return finish(state, height)
 
 
 def solution(mesh):

time: 55.8 us -> 55.8 us (level)
  other arithmetic: 1.37 us -> 0.51 us
  Pallas kernels: 16.1 us -> 16.9 us
  starting transfers between devices: 19 us -> 18.4 us
    pallas_call x0 -> x1, Pallas kernels: none -> 0.83 us  [finish(): pl.pallas_call(body, grid=(1,), in_specs=[pl.BlockSpec((rows, t.shape[1])...]
    concatenate x1 -> x0, other arithmetic: 0.7 us -> none  [local(): return jnp.concatenate(outs, axis=1)]
  transfers between devices with their start and end apart: 16 -> 16, of which waited for: 9 -> 10; matrix products, arithmetic and copies ran while one was open for 1% -> 1% of each run, Pallas kernels for 26% -> 26%
where the time goes in v6:
time: 55.8 us; the launch traced here: 55.6 us
  waiting for transfers between devices  19.5 us (35%)
  starting transfers between devices  18.4 us (33%)
  Pallas kernels  16.9 us (30%)
    ppermute x6, waiting for transfers between devices, turn(): return lax.ppermute(x, ('grp', 'exp'), pairs)  15.9 us
    ppermute x6, starting transfers between devices, turn(): return lax.ppermute(x, ('grp', 'exp'), pairs)  10.6 us
    pallas_call x2, Pallas kernels, near_step(): pl.pallas_call(body, in_specs=specs, out_specs=[whole()] * len(shapes), o...  9.74 us
    ppermute x10, starting transfers between devices, exchange(): lax.ppermute(x, axis, [(i, i ^ mask) for i in range(lax.axis_size(axis))])  7.8 us
    ppermute x10, waiting for transfers between devices, exchange(): lax.ppermute(x, axis, [(i, i ^ mask) for i in range(lax.axis_size(axis))])  3.62 us
    pallas_call x4, Pallas kernels, down_step(): pl.pallas_call(body, in_specs=[whole(), whole()], out_specs=whole(), out_...  2.59 us
    pallas_call x2, Pallas kernels, far_step(): pl.pallas_call(body, in_specs=[whole()] * len(operands), out_specs=whole(...  1.71 us
    pallas_call x1, Pallas kernels, prepare(): pl.pallas_call(body, in_specs=[whole(pl.ANY)] * 3, out_specs=[whole()] *...  1.14 us
  transfers between devices with their start and end apart: 16, of which 10 were waited for; matrix products, arithmetic and copies ran while one was open for 1% of the time, Pallas kernels for 26%

profile of v6, /device:TPU:0, one launch (start us, length us, event | category | flops | bytes accessed | tf_op | source)
XLA Modules:
  0.0 55.6 jit_solution(6650288202354224490)
XLA Ops:
  0.0 0.5 collective-permute-start
  0.5 1.1 %prepare.1 = (bf16[64,2048]{1,0:T(8,128)(2,1)S(1)}, bf16[64,3200]{1,0:T(8,128)(2,1)S(1)}, bf16[64,128]{1,0:T(8,128)(2,1)S(1)}) custom-call(bf16[64,7168]{1,0:T(8,128)(2,1)} %refs_0_.3, s32[2,64]{1,0:T(2,128)} %bitcast.11, bf16[4,64]{1,0:T(4,128)(2,1)} %bitcast.12), custom_call_target="tpu_custom_call" | custom-call | tf_op jit(solution)/shard_map/prepare/pallas_call | solution.py:78
  1.6 2.6 %collective-permute-start.2 = (bf16[64,2048]{1,0:T(8,128)(2,1)S(1)}, bf16[64,2048]{1,0:T(8,128)(2,1)S(1)}, u32[]{:S(2)}, u32[]{:S(2)}) collective-permute-start(bf16[64,2048]{1,0:T(8,128)(2,1)S(1)} %get-tuple-element.35), channel_id=1, source_target_pairs={{0,8},{4,12},{8,0},{12,4},{1,9},{5,13},{9,1},{13,5},{2,10},{6,14},... | collective-permute-start | bytes 786440 | tf_op jit(solution)/shard_map/ppermute | solution.py:29
  4.2 0.0 collective-permute-done.refs_1_
  4.2 4.0 %near.2 = (f32[128,1024]{1,0:T(8,128)S(1)}, bf16[3072,1024]{1,0:T(8,128)(2,1)S(1)}) custom-call(bf16[64,7168]{1,0:T(8,128)(2,1)} %refs_0_.3, bf16[64,7168]{1,0:T(8,128)(2,1)S(1)} %collective-permute-done.refs_1_, bf16[2,28672,128]{2,1,0:T(8,128)(2,1)} %bitcast.8), custom_call_target="tpu_custom_call" | custom-call | flops 3000000000 | bytes 10000000 | tf_op jit(solution)/shard_map/near/pallas_call | solution.py:186
  8.2 1.5 %collective-permute-start.1 = (bf16[64,3200]{1,0:T(8,128)(2,1)S(1)}, bf16[64,3200]{1,0:T(8,128)(2,1)S(1)}, u32[]{:S(2)}, u32[]{:S(2)}) collective-permute-start(bf16[64,3200]{1,0:T(8,128)(2,1)S(1)} %get-tuple-element.34), channel_id=1, source_target_pairs={{0,8},{4,12},{8,0},{12,4},{1,9},{5,13},{9,1},{13,5},{2,10},{6,14},... | collective-permute-start | bytes 1228808 | tf_op jit(solution)/shard_map/ppermute | solution.py:29
  9.7 0.0 collective-permute-start.3
  9.7 1.5 %collective-permute-done.2.refs_1_ = bf16[64,2048]{1,0:T(8,128)(2,1)S(1)} collective-permute-done((bf16[64,2048]{1,0:T(8,128)(2,1)S(1)}, bf16[64,2048]{1,0:T(8,128)(2,1)S(1)}, u32[]{:S(2)}, u32[]{:S(2)}) %collective-permute-start.2) | collective-permute-done | bytes 262176 | tf_op jit(solution)/shard_map/ppermute | solution.py:29
  11.2 0.0 collective-permute-start.5
  11.2 2.0 %collective-permute-start.4 = (bf16[64,2048]{1,0:T(8,128)(2,1)S(1)}, bf16[64,2048]{1,0:T(8,128)(2,1)S(1)}, u32[]{:S(2)}, u32[]{:S(2)}) collective-permute-start(bf16[64,2048]{1,0:T(8,128)(2,1)S(1)} %collective-permute-done.2.refs_1_), channel_id=1, source_target_pairs={{0,1},{1,0},{2,3},{3,2},{4,5},{5,4},{6,7},{7,6},{8,9},{9,8},{10,11... | collective-permute-start | bytes 786440 | tf_op jit(solution)/shard_map/ppermute | solution.py:29
  13.2 5.8 %near.3 = (f32[128,1024]{1,0:T(8,128)S(1)}, bf16[7168,1024]{1,0:T(8,128)(2,1)S(1)}, bf16[512,4352]{1,0:T(8,128)(2,1)S(1)}, bf16[512,2816]{1,0:T(8,128)(2,1)S(1)}) custom-call(bf16[64,7168]{1,0:T(8,128)(2,1)} %refs_0_.3, bf16[64,7168]{1,0:T(8,128)(2,1)S(1)} %collective-permute-done.refs_1_, bf16[2,28672,128]{2,1,0:T(8,128)(2,1)} %bitcast.9, ...), custom_call_target="tpu_custom_call" | custom-call | flops 3000000000 | bytes 10000000 | tf_op jit(solution)/shard_map/near/pallas_call | solution.py:186
  19.0 0.0 collective-permute-done.3.refs_1_
  19.0 0.1 near_gated.1.near_ref
  19.2 0.8 %collective-permute-done.1.refs_2_ = bf16[64,3200]{1,0:T(8,128)(2,1)S(1)} collective-permute-done((bf16[64,3200]{1,0:T(8,128)(2,1)S(1)}, bf16[64,3200]{1,0:T(8,128)(2,1)S(1)}, u32[]{:S(2)}, u32[]{:S(2)}) %collective-permute-start.1) | collective-permute-done | bytes 409632 | tf_op jit(solution)/shard_map/ppermute | solution.py:29
  19.9 0.0 collective-permute-start.6
  19.9 0.0 collective-permute-done.5.refs_2_
  19.9 0.7 %far.2.refs_0_ = f32[128,1024]{1,0:T(8,128)S(1)} custom-call(bf16[7168,1024]{1,0:T(8,128)(2,1)S(1)} %get-tuple-element.43.refs_0_.refs_1_.clean_ref, bf16[64,2048]{1,0:T(8,128)(2,1)S(1)} %collective-permute-done.2.refs_1_, bf16[64,2048]{1,0:T(8,128)(2,1)S(1)} %collective-permute-done.5.refs_2_), custom_call_target="tpu_custom_call" | custom-call | tf_op jit(solution)/shard_map/far/pallas_call | solution.py:225
  20.7 0.0 collective-permute-done.4.refs_0_
  20.7 0.6 %collective-permute-start.7 = (bf16[64,2048]{1,0:T(8,128)(2,1)S(1)}, bf16[64,2048]{1,0:T(8,128)(2,1)S(1)}, u32[]{:S(2)}, u32[]{:S(2)}) collective-permute-start(bf16[64,2048]{1,0:T(8,128)(2,1)S(1)} %collective-permute-done.4.refs_0_), channel_id=1, source_target_pairs={{0,4},{4,0},{8,12},{12,8},{1,5},{5,1},{9,13},{13,9},{2,6},{6,2},{1... | collective-permute-start | bytes 786440 | tf_op jit(solution)/shard_map/ppermute | solution.py:29
  21.3 0.4 collective-permute-done.6.refs_3_
  21.7 1.0 %far.3.acc_ref = f32[128,1024]{1,0:T(8,128)S(1)} custom-call(f32[128,1024]{1,0:T(8,128)S(1)} %far.2.refs_0_, bf16[7168,1024]{1,0:T(8,128)(2,1)S(1)} %get-tuple-element.43.refs_0_.refs_1_.clean_ref, bf16[64,3200]{1,0:T(8,128)(2,1)S(1)} %collective-permute-done.1.refs_2_, bf16[64,3200]{1,0:T(8,128)(2,1)S(1)} %collective-permute-done.6.refs_3_), custom_call_target="tpu_custom_call" | custom-call | tf_op jit(solution)/shard_map/far/pallas_call | solution.py:225
  22.7 0.8 %far_gated.1 = (bf16[256,512]{1,0:T(8,128)(2,1)S(1)}, bf16[256,512]{1,0:T(8,128)(2,1)S(1)}) custom-call(f32[128,512]{1,0:T(8,128)S(1)} %near_gated.1.near_ref, f32[128,1024]{1,0:T(8,128)S(1)} %far.3.acc_ref, bf16[7168,1024]{1,0:T(8,128)(2,1)S(1)} %get-tuple-element.43.refs_0_.refs_1_.clean_ref, bf16[64,2048]{1,0:T(8,128)(2,1)S(1)} %collective-permute-done.4.refs_0_, ...), custom_call_target="tpu_custom_call" | custom-call | tf_op jit(solution)/shard_map/far_gated/pallas_call | solution.py:307
  23.5 0.7 %down.4 = bf16[128,4352]{1,0:T(8,128)(2,1)S(1)} custom-call(bf16[256,512]{1,0:T(8,128)(2,1)S(1)} %get-tuple-element.50.h_ref, bf16[512,4352]{1,0:T(8,128)(2,1)S(1)} %get-tuple-element.49.w_ref), custom_call_target="tpu_custom_call" | custom-call | tf_op jit(solution)/shard_map/down/pallas_call | solution.py:325
  24.3 0.2 collective-permute-start.8
  24.5 0.7 %down.5.refs_0_ = bf16[128,4352]{1,0:T(8,128)(2,1)S(1)} custom-call(bf16[256,512]{1,0:T(8,128)(2,1)S(1)} %get-tuple-element.50.h_ref, bf16[512,4352]{1,0:T(8,128)(2,1)S(1)} %get-tuple-element.49.w_ref), custom_call_target="tpu_custom_call" | custom-call | tf_op jit(solution)/shard_map/down/pallas_call | solution.py:325
  25.2 0.5 down.7
  25.8 0.4 collective-permute-start.10
  26.2 0.9 %collective-permute-done.8.refs_1_ = bf16[128,4352]{1,0:T(8,128)(2,1)S(1)} collective-permute-done((bf16[128,4352]{1,0:T(8,128)(2,1)S(1)}, bf16[128,4352]{1,0:T(8,128)(2,1)S(1)}, u32[]{:S(2)}, u32[]{:S(2)}) %collective-permute-start.8) | collective-permute-done | bytes 1114144 | tf_op jit(solution)/shard_map/ppermute | solution.py:29
  27.1 0.1 add_convert_fusion
  27.2 1.8 %collective-permute-start.9 = (bf16[64,4352]{1,0:T(8,128)(2,1)S(1)}, bf16[64,4352]{1,0:T(8,128)(2,1)S(1)}, u32[]{:S(2)}, u32[]{:S(2)}) collective-permute-start(bf16[64,4352]{1,0:T(8,128)(2,1)S(1)} %add_convert_fusion), channel_id=1, source_target_pairs={{0,8},{1,9},{2,10},{3,11},{4,5},{5,4},{6,7},{7,6},{8,0},{9,1},{10,... | collective-permute-start | bytes 1671176 | tf_op jit(solution)/shard_map/ppermute | solution.py:433
  29.0 0.5 down.6.refs_5_
  29.6 0.0 collective-permute-done.10.refs_6_
  29.6 0.1 add_convert_fusion.1
  29.7 0.3 collective-permute-start.12
  30.0 6.8 %collective-permute-done.9.refs_2_ = bf16[64,4352]{1,0:T(8,128)(2,1)S(1)} collective-permute-done((bf16[64,4352]{1,0:T(8,128)(2,1)S(1)}, bf16[64,4352]{1,0:T(8,128)(2,1)S(1)}, u32[]{:S(2)}, u32[]{:S(2)}) %collective-permute-start.9) | collective-permute-done | bytes 557088 | tf_op jit(solution)/shard_map/ppermute | solution.py:433
  36.8 0.1 add_convert_fusion.2
  36.9 2.9 %collective-permute-start.11 = (bf16[32,4352]{1,0:T(8,128)(2,1)S(1)}, bf16[32,4352]{1,0:T(8,128)(2,1)S(1)}, u32[]{:S(2)}, u32[]{:S(2)}) collective-permute-start(bf16[32,4352]{1,0:T(8,128)(2,1)S(1)} %add_convert_fusion.2), channel_id=1, source_target_pairs={{0,2},{1,3},{2,0},{3,1},{4,12},{5,13},{6,14},{7,15},{8,10},{9,11},... | collective-permute-start | bytes 835592 | tf_op jit(solution)/shard_map/ppermute | solution.py:433
  39.8 0.9 %collective-permute-done.12.refs_7_ = bf16[64,2816]{1,0:T(8,128)(2,1)S(1)} collective-permute-done((bf16[64,2816]{1,0:T(8,128)(2,1)S(1)}, bf16[64,2816]{1,0:T(8,128)(2,1)S(1)}, u32[]{:S(2)}, u32[]{:S(2)}) %collective-permute-start.12) | collective-permute-done | bytes 360480 | tf_op jit(solution)/shard_map/ppermute | solution.py:433
  40.7 0.1 add_convert_fusion.3
  40.8 1.9 %collective-permute-start.14 = (bf16[32,2816]{1,0:T(8,128)(2,1)S(1)}, bf16[32,2816]{1,0:T(8,128)(2,1)S(1)}, u32[]{:S(2)}, u32[]{:S(2)}) collective-permute-start(bf16[32,2816]{1,0:T(8,128)(2,1)S(1)} %add_convert_fusion.3), channel_id=1, source_target_pairs={{0,1},{1,0},{2,3},{3,2},{4,12},{5,13},{6,14},{7,15},{8,9},{9,8},{1... | collective-permute-start | bytes 540680 | tf_op jit(solution)/shard_map/ppermute | solution.py:433
  42.7 5.5 %collective-permute-done.11.refs_3_ = bf16[32,4352]{1,0:T(8,128)(2,1)S(1)} collective-permute-done((bf16[32,4352]{1,0:T(8,128)(2,1)S(1)}, bf16[32,4352]{1,0:T(8,128)(2,1)S(1)}, u32[]{:S(2)}, u32[]{:S(2)}) %collective-permute-start.11) | collective-permute-done | bytes 278560 | tf_op jit(solution)/shard_map/ppermute | solution.py:433
  48.2 0.1 add_convert_fusion.4
  48.3 0.3 collective-permute-start.13
  48.5 0.1 collective-permute-done.14.refs_8_
  48.7 3.4 %collective-permute-start.15 = (bf16[16,2816]{1,0:T(8,128)(2,1)S(1)}, bf16[16,2816]{1,0:T(8,128)(2,1)S(1)}, u32[]{:S(2)}, u32[]{:S(2)}) collective-permute-start(bf16[16,2816]{1,0:T(8,128)(2,1)S(1)} %add_convert_fusion.5), channel_id=1, source_target_pairs={{0,2},{1,3},{2,0},{3,1},{4,5},{5,4},{6,7},{7,6},{8,10},{9,11},{10,... | collective-permute-start | bytes 270344 | tf_op jit(solution)/shard_map/ppermute | solution.py:433
  52.1 2.6 %collective-permute-done.15.refs_9_ = bf16[16,2816]{1,0:T(8,128)(2,1)S(1)} collective-permute-done((bf16[16,2816]{1,0:T(8,128)(2,1)S(1)}, bf16[16,2816]{1,0:T(8,128)(2,1)S(1)}, u32[]{:S(2)}, u32[]{:S(2)}) %collective-permute-start.15) | collective-permute-done | bytes 90144 | tf_op jit(solution)/shard_map/ppermute | solution.py:433
  54.7 0.1 collective-permute-done.13.refs_4_
  54.8 0.8 %finish.1 = bf16[16,7168]{1,0:T(8,128)(2,1)} custom-call(bf16[128,4352]{1,0:T(8,128)(2,1)S(1)} %down.5.refs_0_, bf16[128,4352]{1,0:T(8,128)(2,1)S(1)} %collective-permute-done.8.refs_1_, bf16[64,4352]{1,0:T(8,128)(2,1)S(1)} %collective-permute-done.9.refs_2_, bf16[32,4352]{1,0:T(8,128)(2,1)S(1)} %collective-permute-done.11.refs_3_, ...), custom_call_target="tpu_custom_call" | custom-call | tf_op jit(solution)/shard_map/finish/pallas_call | solution.py:350
  (2 shorter events, 0.1 us)
Async XLA Ops:
  0.0 4.2 %collective-permute-start = (bf16[64,7168]{1,0:T(8,128)(2,1)}, bf16[64,7168]{1,0:T(8,128)(2,1)S(1)}, u32[]{:S(2)}, u32[]{:S(2)}) collective-permute-start(bf16[64,7168]{1,0:T(8,128)(2,1)} %refs_0_.3), channel_id=1, source_target_pairs={{0,4},{4,0},{8,12},{12,8},{1,5},{5,1},{9,13},{13,9},{2,6},{6,2},{1... | collective-permute-start | bytes 2752520 | tf_op jit(solution)/shard_map/ppermute | solution.py:29
  1.6 9.6 %collective-permute-start.2 = (bf16[64,2048]{1,0:T(8,128)(2,1)S(1)}, bf16[64,2048]{1,0:T(8,128)(2,1)S(1)}, u32[]{:S(2)}, u32[]{:S(2)}) collective-permute-start(bf16[64,2048]{1,0:T(8,128)(2,1)S(1)} %get-tuple-element.35), channel_id=1, source_target_pairs={{0,8},{4,12},{8,0},{12,4},{1,9},{5,13},{9,1},{13,5},{2,10},{6,14},... | collective-permute-start | bytes 786440 | tf_op jit(solution)/shard_map/ppermute | solution.py:29
  8.2 11.8 %collective-permute-start.1 = (bf16[64,3200]{1,0:T(8,128)(2,1)S(1)}, bf16[64,3200]{1,0:T(8,128)(2,1)S(1)}, u32[]{:S(2)}, u32[]{:S(2)}) collective-permute-start(bf16[64,3200]{1,0:T(8,128)(2,1)S(1)} %get-tuple-element.34), channel_id=1, source_target_pairs={{0,8},{4,12},{8,0},{12,4},{1,9},{5,13},{9,1},{13,5},{2,10},{6,14},... | collective-permute-start | bytes 1228808 | tf_op jit(solution)/shard_map/ppermute | solution.py:29
  9.7 9.4 %collective-permute-start.3 = (bf16[64,128]{1,0:T(8,128)(2,1)S(1)}, bf16[64,128]{1,0:T(8,128)(2,1)S(1)}, u32[]{:S(2)}, u32[]{:S(2)}) collective-permute-start(bf16[64,128]{1,0:T(8,128)(2,1)S(1)} %get-tuple-element.40.refs_0_), channel_id=1, source_target_pairs={{0,4},{4,0},{8,12},{12,8},{1,5},{5,1},{9,13},{13,9},{2,6},{6,2},{1... | collective-permute-start | bytes 49160 | tf_op jit(solution)/shard_map/ppermute | solution.py:29
  11.2 8.7 %collective-permute-start.5 = (bf16[64,2048]{1,0:T(8,128)(2,1)S(1)}, bf16[64,2048]{1,0:T(8,128)(2,1)S(1)}, u32[]{:S(2)}, u32[]{:S(2)}) collective-permute-start(bf16[64,2048]{1,0:T(8,128)(2,1)S(1)} %collective-permute-done.2.refs_1_), channel_id=1, source_target_pairs={{0,4},{4,0},{8,12},{12,8},{1,5},{5,1},{9,13},{13,9},{2,6},{6,2},{1... | collective-permute-start | bytes 786440 | tf_op jit(solution)/shard_map/ppermute | solution.py:29
  11.2 9.5 %collective-permute-start.4 = (bf16[64,2048]{1,0:T(8,128)(2,1)S(1)}, bf16[64,2048]{1,0:T(8,128)(2,1)S(1)}, u32[]{:S(2)}, u32[]{:S(2)}) collective-permute-start(bf16[64,2048]{1,0:T(8,128)(2,1)S(1)} %collective-permute-done.2.refs_1_), channel_id=1, source_target_pairs={{0,1},{1,0},{2,3},{3,2},{4,5},{5,4},{6,7},{7,6},{8,9},{9,8},{10,11... | collective-permute-start | bytes 786440 | tf_op jit(solution)/shard_map/ppermute | solution.py:29
  19.9 1.7 %collective-permute-start.6 = (bf16[64,3200]{1,0:T(8,128)(2,1)S(1)}, bf16[64,3200]{1,0:T(8,128)(2,1)S(1)}, u32[]{:S(2)}, u32[]{:S(2)}) collective-permute-start(bf16[64,3200]{1,0:T(8,128)(2,1)S(1)} %collective-permute-done.1.refs_2_), channel_id=1, source_target_pairs={{0,4},{4,0},{8,12},{12,8},{1,5},{5,1},{9,13},{13,9},{2,6},{6,2},{1... | collective-permute-start | bytes 1228808 | tf_op jit(solution)/shard_map/ppermute | solution.py:29
  20.7 2.0 %collective-permute-start.7 = (bf16[64,2048]{1,0:T(8,128)(2,1)S(1)}, bf16[64,2048]{1,0:T(8,128)(2,1)S(1)}, u32[]{:S(2)}, u32[]{:S(2)}) collective-permute-start(bf16[64,2048]{1,0:T(8,128)(2,1)S(1)} %collective-permute-done.4.refs_0_), channel_id=1, source_target_pairs={{0,4},{4,0},{8,12},{12,8},{1,5},{5,1},{9,13},{13,9},{2,6},{6,2},{1... | collective-permute-start | bytes 786440 | tf_op jit(solution)/shard_map/ppermute | solution.py:29
  24.3 2.8 %collective-permute-start.8 = (bf16[128,4352]{1,0:T(8,128)(2,1)S(1)}, bf16[128,4352]{1,0:T(8,128)(2,1)S(1)}, u32[]{:S(2)}, u32[]{:S(2)}) collective-permute-start(bf16[128,4352]{1,0:T(8,128)(2,1)S(1)} %down.4), channel_id=1, source_target_pairs={{0,4},{4,0},{8,12},{12,8},{1,5},{5,1},{9,13},{13,9},{2,6},{6,2},{1... | collective-permute-start | bytes 3342344 | tf_op jit(solution)/shard_map/ppermute | solution.py:29
  25.8 3.8 %collective-permute-start.10 = (bf16[128,2816]{1,0:T(8,128)(2,1)S(1)}, bf16[128,2816]{1,0:T(8,128)(2,1)S(1)}, u32[]{:S(2)}, u32[]{:S(2)}) collective-permute-start(bf16[128,2816]{1,0:T(8,128)(2,1)S(1)} %down.7), channel_id=1, source_target_pairs={{0,4},{4,0},{8,12},{12,8},{1,5},{5,1},{9,13},{13,9},{2,6},{6,2},{1... | collective-permute-start | bytes 2162696 | tf_op jit(solution)/shard_map/ppermute | solution.py:29
  27.2 9.6 %collective-permute-start.9 = (bf16[64,4352]{1,0:T(8,128)(2,1)S(1)}, bf16[64,4352]{1,0:T(8,128)(2,1)S(1)}, u32[]{:S(2)}, u32[]{:S(2)}) collective-permute-start(bf16[64,4352]{1,0:T(8,128)(2,1)S(1)} %add_convert_fusion), channel_id=1, source_target_pairs={{0,8},{1,9},{2,10},{3,11},{4,5},{5,4},{6,7},{7,6},{8,0},{9,1},{10,... | collective-permute-start | bytes 1671176 | tf_op jit(solution)/shard_map/ppermute | solution.py:433
  29.7 11.0 %collective-permute-start.12 = (bf16[64,2816]{1,0:T(8,128)(2,1)S(1)}, bf16[64,2816]{1,0:T(8,128)(2,1)S(1)}, u32[]{:S(2)}, u32[]{:S(2)}) collective-permute-start(bf16[64,2816]{1,0:T(8,128)(2,1)S(1)} %add_convert_fusion.1), channel_id=1, source_target_pairs={{0,8},{1,9},{2,10},{3,11},{4,6},{5,7},{6,4},{7,5},{8,0},{9,1},{10,... | collective-permute-start | bytes 1081352 | tf_op jit(solution)/shard_map/ppermute | solution.py:433
  36.9 11.3 %collective-permute-start.11 = (bf16[32,4352]{1,0:T(8,128)(2,1)S(1)}, bf16[32,4352]{1,0:T(8,128)(2,1)S(1)}, u32[]{:S(2)}, u32[]{:S(2)}) collective-permute-start(bf16[32,4352]{1,0:T(8,128)(2,1)S(1)} %add_convert_fusion.2), channel_id=1, source_target_pairs={{0,2},{1,3},{2,0},{3,1},{4,12},{5,13},{6,14},{7,15},{8,10},{9,11},... | collective-permute-start | bytes 835592 | tf_op jit(solution)/shard_map/ppermute | solution.py:433
  40.8 7.9 %collective-permute-start.14 = (bf16[32,2816]{1,0:T(8,128)(2,1)S(1)}, bf16[32,2816]{1,0:T(8,128)(2,1)S(1)}, u32[]{:S(2)}, u32[]{:S(2)}) collective-permute-start(bf16[32,2816]{1,0:T(8,128)(2,1)S(1)} %add_convert_fusion.3), channel_id=1, source_target_pairs={{0,1},{1,0},{2,3},{3,2},{4,12},{5,13},{6,14},{7,15},{8,9},{9,8},{1... | collective-permute-start | bytes 540680 | tf_op jit(solution)/shard_map/ppermute | solution.py:433
  48.3 6.5 %collective-permute-start.13 = (bf16[16,4352]{1,0:T(8,128)(2,1)S(1)}, bf16[16,4352]{1,0:T(8,128)(2,1)S(1)}, u32[]{:S(2)}, u32[]{:S(2)}) collective-permute-start(bf16[16,4352]{1,0:T(8,128)(2,1)S(1)} %add_convert_fusion.4), channel_id=1, source_target_pairs={{0,1},{1,0},{2,3},{3,2},{4,6},{5,7},{6,4},{7,5},{8,9},{9,8},{10,11... | collective-permute-start | bytes 417800 | tf_op jit(solution)/shard_map/ppermute | solution.py:433
  48.7 6.0 %collective-permute-start.15 = (bf16[16,2816]{1,0:T(8,128)(2,1)S(1)}, bf16[16,2816]{1,0:T(8,128)(2,1)S(1)}, u32[]{:S(2)}, u32[]{:S(2)}) collective-permute-start(bf16[16,2816]{1,0:T(8,128)(2,1)S(1)} %add_convert_fusion.5), channel_id=1, source_target_pairs={{0,2},{1,3},{2,0},{3,1},{4,5},{5,4},{6,7},{7,6},{8,10},{9,11},{10,... | collective-permute-start | bytes 270344 | tf_op jit(solution)/shard_map/ppermute | solution.py:433
